TPU v7x, 32 devices: a whole 2x2x4 slice. The times are simulated.
32 devices in a mesh: seq: 4 (over y, x), ret: 8 (over z, core).
Axes of the slice: x: 2, y: 2, z: 4, core: 2. Of those that a mesh axis runs over, the one named last changes fastest.
Arguments:
- queries: bfloat16 [3072, 4096], P('seq', 'ret'), may hold values from -4 to 4
- grad_ctx: bfloat16 [3072, 4096], P('seq', 'ret'), may hold values from -6 to 6
- neighbours: bfloat16 [64, 128, 896], P(('seq', 'ret')), may hold values from -6 to 6
- up_weight: bfloat16 [896, 3584], replicated, may hold values from -0.1875 to 0.1875
- down_weight: bfloat16 [3584, 896], replicated, may hold values from -0.09375 to 0.09375
- key_weight: bfloat16 [896, 4096], P(None, 'ret'), may hold values from -0.1875 to 0.1875
- value_weight: bfloat16 [896, 4096], P(None, 'ret'), may hold values from -0.1875 to 0.1875
- group_ids: int32 [48, 2], P('seq'), may hold values from 0 to 3, all different within a row; in each aligned block of 12 rows (0 to 11, 12 to 23, ...) at most 8 rows name the same one
- slot_ids: int32 [48, 2], P('seq'), may hold values from 0 to 15
Outputs:
- context: bfloat16 [3072, 4096], P('seq', 'ret')
- grad_queries: bfloat16 [3072, 4096], P('seq', 'ret')
- grad_encoded: bfloat16 [64, 128, 896], P(('seq', 'ret'))
- grad_key_weight: float32 [896, 4096], P('seq', 'ret')
- grad_value_weight: float32 [896, 4096], P('seq', 'ret')
Inputs may be any that keep to these rules, and one draw needn't show every extreme that they name: `group_ids`: the two neighbours of a span lie on different indices of seq. Among the spans of one index of seq no index of seq is named more than 8 times, and in every draw some index of seq is named exactly 8 times by the spans of some index of seq.
All inputs are finite; a program needn't handle non-finite values.
Results may differ from a plain program's by a relative error of at most 0.018.
Values may be sent and summed in bfloat16 or wider, within the bound.
No kernel may reach another device: no remote copies, remote signals or barrier semaphores. Data moves between devices by JAX's collectives and lax.ppermute only.
A program may use at most 192 MiB of HBM per device.

v0:
```python
import math

import jax
import jax.numpy as jnp
from jax import lax
from jax.sharding import PartitionSpec as P

HD = 128


def encode(raw_block, up_weight, down_weight):
    amount, row_len, feat_width = raw_block.shape
    inputs = raw_block.reshape(-1, feat_width).astype(jnp.float32)
    normed = (inputs * lax.rsqrt(jnp.mean(inputs * inputs, axis=-1, keepdims=True) + 1e-06)).astype(
        jnp.bfloat16
    )
    hidden = jax.nn.gelu(jnp.dot(normed, up_weight, preferred_element_type=jnp.float32)).astype(
        jnp.bfloat16
    )
    output = inputs + jnp.dot(hidden, down_weight, preferred_element_type=jnp.float32)
    return output.astype(jnp.bfloat16).reshape(amount, row_len, feat_width)


def attend(queries, key_req, value_req, grad_out):
    score_scale = 1.0 / math.sqrt(queries.shape[-1])
    scores = (
        jnp.einsum("cqhd,ckhd->chqk", queries, key_req, preferred_element_type=jnp.float32)
        * score_scale
    )
    weights = jnp.exp(scores)
    weights = weights / jnp.sum(weights, axis=-1, keepdims=True)
    probs = weights.astype(jnp.bfloat16)
    context = jnp.einsum(
        "chqk,ckhd->cqhd", probs, value_req, preferred_element_type=jnp.float32
    ).astype(jnp.bfloat16)
    grad_probs = jnp.einsum(
        "cqhd,ckhd->chqk", grad_out, value_req, preferred_element_type=jnp.float32
    )
    mixed = (
        weights * (grad_probs - jnp.sum(weights * grad_probs, axis=-1, keepdims=True)) * score_scale
    ).astype(jnp.bfloat16)
    grad_queries = jnp.einsum(
        "chqk,ckhd->cqhd", mixed, key_req, preferred_element_type=jnp.float32
    ).astype(jnp.bfloat16)
    grad_keys = jnp.einsum(
        "chqk,cqhd->ckhd", mixed, queries, preferred_element_type=jnp.float32
    ).astype(jnp.bfloat16)
    grad_values = jnp.einsum(
        "chqk,cqhd->ckhd", probs, grad_out, preferred_element_type=jnp.float32
    ).astype(jnp.bfloat16)
    return (context, grad_queries, grad_keys, grad_values)


def full_table(encoded_own):
    return lax.all_gather(encoded_own, "ret", axis=0, tiled=True)


def home_sum(returned, served, table_len, row_len, feat_width):
    selector = (served[:, None] == jnp.arange(table_len, dtype=jnp.int32)[None, :]).astype(
        jnp.bfloat16
    )
    table_grad = jnp.einsum("ns,nx->sx", selector, returned, preferred_element_type=jnp.float32)
    table_grad = table_grad.reshape(table_len, row_len, feat_width)
    return lax.psum_scatter(table_grad, "ret", scatter_dimension=0, tiled=True).astype(jnp.bfloat16)


def body(
    queries,
    grad_ctx,
    neighbours,
    up_weight,
    down_weight,
    key_weight,
    value_weight,
    group_ids,
    slot_ids,
):
    groups = lax.axis_size("seq")
    span_count = group_ids.shape[0]
    capacity = 2 * span_count // groups + 2
    slot_total = groups * capacity
    head_width = queries.shape[1]
    block_heads = head_width // HD
    span_len = queries.shape[0] // span_count
    encoded_own = encode(neighbours, up_weight, down_weight)
    own_count, row_len, feat_width = encoded_own.shape
    table_len = own_count * lax.axis_size("ret")
    targets = group_ids.reshape(-1)
    slot_list = slot_ids.reshape(-1)
    requests = targets.shape[0]
    one_hot = (targets[:, None] == jnp.arange(groups, dtype=jnp.int32)[None, :]).astype(jnp.int32)
    before = jnp.cumsum(one_hot, axis=0) - one_hot
    position = targets * capacity + jnp.sum(before * one_hot, axis=1)
    wanted = jnp.zeros((slot_total,), jnp.int32).at[position].set(slot_list)
    served = lax.all_to_all(
        wanted.reshape(groups, capacity), "seq", split_axis=0, concat_axis=0, tiled=True
    ).reshape(-1)
    enc_table = full_table(encoded_own)
    source_rows = jnp.take(enc_table, served, axis=0)
    arrived = lax.all_to_all(
        source_rows.reshape(groups, capacity, row_len, feat_width),
        "seq",
        split_axis=0,
        concat_axis=0,
        tiled=True,
    )
    picked = jnp.take(arrived.reshape(slot_total, row_len, feat_width), position, axis=0).reshape(
        -1, feat_width
    )
    key_flat = jnp.dot(picked, key_weight, preferred_element_type=jnp.float32).astype(jnp.bfloat16)
    value_flat = jnp.dot(picked, value_weight, preferred_element_type=jnp.float32).astype(
        jnp.bfloat16
    )
    shape_q = (span_count, span_len, block_heads, HD)
    shape_kv = (span_count, 2 * row_len, block_heads, HD)
    context, grad_query, grad_keys, grad_values = attend(
        queries.reshape(shape_q),
        key_flat.reshape(shape_kv),
        value_flat.reshape(shape_kv),
        grad_ctx.reshape(shape_q),
    )
    grad_keys = grad_keys.reshape(-1, head_width)
    grad_values = grad_values.reshape(-1, head_width)
    grad_key_w = jnp.einsum("rd,rh->dh", picked, grad_keys, preferred_element_type=jnp.float32)
    grad_value_w = jnp.einsum("rd,rh->dh", picked, grad_values, preferred_element_type=jnp.float32)
    grad_part = (
        jnp.dot(grad_keys, key_weight.T, preferred_element_type=jnp.float32)
        + jnp.dot(grad_values, value_weight.T, preferred_element_type=jnp.float32)
    ).astype(jnp.bfloat16)
    placed = (
        jnp.zeros((slot_total, row_len * feat_width), jnp.bfloat16)
        .at[position]
        .set(grad_part.reshape(requests, -1))
    )
    returned = lax.all_to_all(
        placed.reshape(groups, capacity, row_len * feat_width),
        "seq",
        split_axis=0,
        concat_axis=0,
        tiled=True,
    )
    returned = returned.reshape(slot_total, -1)
    grad_encoded = home_sum(returned, served, table_len, row_len, feat_width)
    grad_key_out, grad_value_out = (
        lax.psum_scatter(grad_key_w, "seq", scatter_dimension=0, tiled=True),
        lax.psum_scatter(grad_value_w, "seq", scatter_dimension=0, tiled=True),
    )
    return (
        context.reshape(-1, head_width),
        grad_query.reshape(-1, head_width),
        grad_encoded,
        grad_key_out,
        grad_value_out,
    )


def solution(mesh):
    return jax.shard_map(
        body,
        mesh=mesh,
        in_specs=(
            P("seq", "ret"),
            P("seq", "ret"),
            P(("seq", "ret"), None, None),
            P(),
            P(),
            P(None, "ret"),
            P(None, "ret"),
            P("seq", None),
            P("seq", None),
        ),
        out_specs=(
            P("seq", "ret"),
            P("seq", "ret"),
            P(("seq", "ret"), None, None),
            P("seq", "ret"),
            P("seq", "ret"),
        ),
        check_vma=False,
    )
```

profile of v0, /device:TPU:0, one launch (start us, length us, event | category | flops | bytes accessed | tf_op | source)
XLA Modules:
  0.0 617.7 jit_solution(9666936601344220623)
XLA Ops:
  7.2 1.3 multiply_reduce_fusion
  8.5 1.2 fusion.59
  9.7 9.5 %fusion.56 = bf16[256,896]{1,0:T(8,128)(2,1)} fusion(bf16[3584,896]{1,0:T(8,128)(2,1)} %param.13, bf16[256,896]{1,0:T(8,128)(2,1)S(1)} %fusion.59, bf16[896,3584]{1,0:T(8,128)(2,1)} %param.12, bf16[256,896]{1,0:T(8,128)(2,1)} %bitcast.139), kind=kOutput, calls=%fused_computation.63 | convolution fusion | flops 3297280000 | bytes 14221312 | tf_op jit(solution)/shard_map/dot_general | solution.py:20
  20.1 0.7 scatter_custom_fusion
  20.9 9.6 %all_to_all.19 = s32[4,1,8]{2,1,0:T(1,128)S(1)} all-to-all(s32[4,1,8]{2,1,0:T(1,128)S(1)} %bitcast.143), channel_id=1, replica_groups=mesh['seq'=4,'ret'=8] {'seq'}, dimensions={0} | all-to-all | bytes 256 | tf_op jit(solution)/shard_map/all_to_all | solution.py:95
  30.5 0.5 broadcast.211
  31.0 0.7 reduce.6
  31.7 32.9 %all-gather.2.cloned.1.call-done = bf16[16,128,896]{2,1,0:T(8,128)(2,1)} async-done(((bf16[2,128,896]{2,1,0:T(8,128)(2,1)}), bf16[16,128,896]{2,1,0:T(8,128)(2,1)}) %all-gather.2.cloned.1.call-update) | async-done | bytes 3670032 | tf_op jit(solution)/shard_map/all_gather | solution.py:55
  64.7 6.4 %gather_fusion = bf16[32,128,896]{2,1,0:T(8,128)(2,1)} fusion(bf16[16,128,896]{2,1,0:T(8,128)(2,1)} %all-gather.2.cloned.1.call-done, s32[1024]{0:T(1024)S(1)} %pad_clamp_fusion.1), kind=kCustom, calls=%fused_computation | custom fusion | bytes 14680192 | tf_op jit(solution)/shard_map/jit(_take)/gather | solution.py:99
  71.1 6.9 %broadcast_select_fusion = bf16[4,8,128,896]{3,2,1,0:T(8,128)(2,1)} fusion(bf16[4,8,128,896]{3,2,1,0:T(8,128)(2,1)} %bitcast.130, pred[4,8]{1,0:T(4,128)(4,1)S(1)} %compare_and_fusion), kind=kLoop, calls=%fused_computation.9 | loop fusion | flops 3670016 | bytes 14680096 | tf_op jit(solution)/shard_map/jit(_take)/select_n | solution.py:99
  78.0 6.1 all-to-all-start.1
  84.6 81.3 %all-to-all-done.1 = bf16[4,8,128,896]{3,2,1,0:T(8,128)(2,1)} async-done(((bf16[4,8,128,896]{3,2,1,0:T(8,128)(2,1)}), bf16[4,8,128,896]{3,2,1,0:T(8,128)(2,1)}, u32[]{:S(2)}, u32[]{:S(2)}) %all-to-all-start.1) | async-done | bytes 7340064 | tf_op jit(solution)/shard_map/all_to_all | solution.py:100
  165.9 7.0 %gather_fusion.1 = bf16[24,128,896]{2,1,0:T(8,128)(2,1)} fusion(bf16[32,128,896]{2,1,0:T(8,128)(2,1)} %bitcast.10, s32[1024]{0:T(1024)S(1)} %pad_clamp_fusion), kind=kCustom, calls=%fused_computation.1 | custom fusion | bytes 11010144 | tf_op jit(solution)/shard_map/jit(_take)/gather | solution.py:107
  172.8 3.7 bitcast_select_fusion
  176.5 4.8 convolution_convert_fusion
  181.4 4.8 convolution_convert_fusion.1
  186.1 5.5 reshape.231
  191.7 5.5 reshape.232
  197.2 4.9 fusion.26
  202.1 1.3 bitcast_reduce_fusion
  203.5 1.6 copy-done.14
  205.1 3.2 convert_bitcast_fusion
  208.3 24.3 %convert_bitcast_fusion.1 = bf16[12,256,4,128]{3,1,2,0:T(8,128)(2,1)} fusion(f32[12,4,256,64]{2,3,1,0:T(8,128)} %fusion.26, bf16[12,64,4,128]{3,2,1,0:T(4,128)(2,1)S(1)} %reshape.233, f32[12,4,256,64]{2,3,1,0:T(8,128)} %copy-done.14, f32[12,4,64]{2,1,0:T(4,128)S(1)} %get-tuple-element.15), kind=kOutput, calls=%fused_computation.38 | convolution fusion | flops 209980672 | bytes 10235904 | tf_op jit(solution)/shard_map/chqk,cqhd->ckhd/dot_general | solution.py:45
  232.6 4.5 copy.58
  237.1 2.4 copy.56
  239.6 3.5 fusion.17
  243.1 5.4 add_convert_fusion
  248.5 7.2 %reshape.272 = bf16[24,114688]{1,0:T(8,128)(2,1)} reshape(bf16[3072,896]{1,0:T(8,128)(2,1)} %add_convert_fusion) | data formatting | bytes 11010048 | tf_op jit(solution)/shard_map/reshape | solution.py:133
  255.7 3.5 broadcast_in_dim.54
  259.2 106.3 %scatter_fusion = bf16[32,114688]{1,0:T(8,128)(2,1)} fusion(bf16[32,114688]{1,0:T(8,128)(2,1)} %broadcast_in_dim.54, s32[24]{0:T(128)S(1)} %fusion.70, bf16[24,114688]{1,0:T(8,128)(2,1)} %reshape.272), kind=kCustom, calls=%fused_computation.3 | custom fusion | bytes 16515168 | tf_op jit(solution)/shard_map/scatter | solution.py:133
  365.6 5.4 all-to-all-start.2
  371.2 80.8 %all-to-all-done.2 = bf16[4,8,114688]{2,1,0:T(8,128)(2,1)} async-done(((bf16[4,8,114688]{2,1,0:T(8,128)(2,1)}), bf16[4,8,114688]{2,1,0:T(8,128)(2,1)}, u32[]{:S(2)}, u32[]{:S(2)}) %all-to-all-start.2) | async-done | bytes 7340064 | tf_op jit(solution)/shard_map/all_to_all | solution.py:135
  452.0 4.2 fusion.1
  456.2 5.2 copy.60
  461.5 3.3 broadcast_select_fusion.1
  464.9 2.5 copy-done.2
  467.3 4.3 fusion.12
  471.7 0.3 reduce-scatter.6.cloned.1.call-start
  471.9 7.9 %fusion.15 = f32[896,512]{1,0:T(8,128)} fusion(bf16[3072,896]{1,0:T(8,128)(2,1)} %bitcast.132, bf16[384,8,4,128]{3,2,1,0:T(4,128)(2,1)} %bitcast.134), kind=kOutput, calls=%fused_computation.26 | convolution fusion | flops 2818572288 | bytes 10485760 | tf_op jit(solution)/shard_map/rd,rh->dh/dot_general | solution.py:124
  479.8 3.9 fusion.47
  483.8 0.6 copy.50
  484.4 22.8 %fusion.50 = bf16[12,64,4,128]{3,1,2,0:T(8,128)(2,1)S(1)} fusion(bf16[12,256,4,128]{3,2,1,0:T(4,128)(2,1)} %reshape.232, f32[12,4,256,64]{2,3,1,0:T(8,128)} %fusion.26, f32[12,4,256,64]{2,3,1,0:T(8,128)} %copy-done.14, f32[12,4,64]{2,1,0:T(4,128)S(1)} %get-tuple-element.15), kind=kOutput, calls=%fused_computation.61 | convolution fusion | flops 208801024 | bytes 10235904 | tf_op jit(solution)/shard_map/chqk,ckhd->cqhd/dot_general | solution.py:42
  507.2 0.6 copy.54
  507.8 1.5 copy_bitcast_fusion
  509.3 30.1 %reduce-scatter.4.cloned.1.call-done = f32[2,128,896]{2,1,0:T(8,128)} async-done(((f32[16,128,896]{2,1,0:T(8,128)}), f32[2,128,896]{2,1,0:T(8,128)}) %reduce-scatter.4.cloned.1.call-update) | async-done | bytes 917520 | tf_op jit(solution)/shard_map/reduce_scatter | solution.py:64
  539.4 2.0 convert_element_type.84
  541.4 33.0 %reduce-scatter.8.cloned.1.call-done = f32[224,512]{1,0:T(8,128)} async-done(((f32[896,512]{1,0:T(8,128)}), f32[224,512]{1,0:T(8,128)}) %reduce-scatter.8.cloned.1.call-update) | async-done | bytes 458768 | tf_op jit(solution)/shard_map/reduce_scatter | solution.py:146
  574.4 36.5 %reduce-scatter.6.cloned.1.call-done = f32[224,512]{1,0:T(8,128)} async-done(((f32[896,512]{1,0:T(8,128)}), f32[224,512]{1,0:T(8,128)}) %reduce-scatter.6.cloned.1.call-update) | async-done | bytes 458768 | tf_op jit(solution)/shard_map/reduce_scatter | solution.py:145
  (58 shorter events, 1.8 us)
Async XLA Ops:
  7.2 169.3 %copy-start = (bf16[896,512]{1,0:T(8,128)(2,1)S(1)}, bf16[896,512]{1,0:T(8,128)(2,1)}, u32[]{:S(2)}) copy-start(bf16[896,512]{1,0:T(8,128)(2,1)} %param.14) | copy-start | bytes 2752516
  7.2 57.5 %all-gather.2.cloned.1.call-start = ((), (), s32[]{:S(2)}) async-start(), calls=%async_computation.6 | async-start | bytes 4128768 | tf_op jit(solution)/shard_map/all_gather | solution.py:55
  9.7 9.6 %copy-start.10 = (s32[12,2]{0,1:T(2,128)S(1)}, s32[12,2]{0,1:T(2,128)}, u32[]{:S(2)}) copy-start(s32[12,2]{0,1:T(2,128)} %param.16) | copy-start | bytes 292
  9.7 9.8 %copy-start.11 = (s32[12,2]{0,1:T(2,128)S(1)}, s32[12,2]{0,1:T(2,128)}, u32[]{:S(2)}) copy-start(s32[12,2]{0,1:T(2,128)} %param.17) | copy-start | bytes 292
  78.0 6.1 copy-start.8
  78.0 6.3 %copy-start.9 = (bf16[768,512]{1,0:T(8,128)(2,1)S(1)}, bf16[768,512]{1,0:T(8,128)(2,1)}, u32[]{:S(2)}) copy-start(bf16[768,512]{1,0:T(8,128)(2,1)} %param.10) | copy-start | bytes 2359300
  78.0 87.9 %all-to-all-start.1 = ((bf16[4,8,128,896]{3,2,1,0:T(8,128)(2,1)}), bf16[4,8,128,896]{3,2,1,0:T(8,128)(2,1)}, u32[]{:S(2)}, u32[]{:S(2)}) async-start(bf16[4,8,128,896]{3,2,1,0:T(8,128)(2,1)} %broadcast_select_fusion), calls=%async_computation.1 | async-start | bytes 14680064 | tf_op jit(solution)/shard_map/all_to_all | solution.py:100
  176.5 4.9 copy-start.12
  197.2 4.9 copy-start.3
  203.5 1.6 copy-start.14
  232.6 4.5 copy-start.7
  237.1 6.0 copy-start.5
  239.6 3.5 copy-start.4
  239.6 3.5 copy-start.13
  365.6 86.4 %all-to-all-start.2 = ((bf16[4,8,114688]{2,1,0:T(8,128)(2,1)}), bf16[4,8,114688]{2,1,0:T(8,128)(2,1)}, u32[]{:S(2)}, u32[]{:S(2)}) async-start(bf16[4,8,114688]{2,1,0:T(8,128)(2,1)} %bitcast.129), calls=%async_computation.2 | async-start | bytes 14680064 | tf_op jit(solution)/shard_map/all_to_all | solution.py:135
  371.0 168.4 %reduce-scatter.4.cloned.1.call-start = ((), (), s32[]{:S(2)}) async-start(), calls=%async_computation.7 | async-start | bytes 8257536 | tf_op jit(solution)/shard_map/reduce_scatter | solution.py:64
  461.5 113.0 %reduce-scatter.8.cloned.1.call-start = ((), (), s32[]{:S(2)}) async-start(), calls=%async_computation.9 | async-start | bytes 2293760 | tf_op jit(solution)/shard_map/reduce_scatter | solution.py:146
  461.5 5.8 copy-start.6
  464.8 2.5 copy-start.2
  471.7 139.3 %reduce-scatter.6.cloned.1.call-start = ((), (), s32[]{:S(2)}) async-start(), calls=%async_computation.8 | async-start | bytes 2293760 | tf_op jit(solution)/shard_map/reduce_scatter | solution.py:145
  484.4 126.6 %copy-start.1 = (bf16[896,512]{1,0:T(8,128)(2,1)S(1)}, bf16[896,512]{1,0:T(8,128)(2,1)}, u32[]{:S(2)}) copy-start(bf16[896,512]{1,0:T(8,128)(2,1)} %param.14) | copy-start | bytes 2752516
Sparse Core Ops, SparseCore 0:
  19.3 45.2 all-gather.1
  461.6 77.7 reduce-scatter.3
  543.0 31.3 reduce-scatter.7
  577.9 32.9 reduce-scatter.5
where the time goes:
time: 624 us; the launch traced here: 618 us
  waiting for transfers between devices  295 us (47%)
  local copies, waits for them, and re-layouts  163 us (26%)
  matrix products  105 us (17%)
  other arithmetic  19.3 us (3%)
  between operations  14.3 us (2%)
  starting transfers between devices  11.9 us (2%)
  blocking collectives  9.59 us (2%)
    scatter x1, local copies, waits for them, and re-layouts, body(): placed = jnp.zeros((slot_total, row_len * feat_width), jnp.bfloat16).at[p...  106 us
    all_to_all x1, waiting for transfers between devices, body(): lax.all_to_all(source_rows.reshape(groups, capacity, row_len, feat_width)...  81.3 us
    all_to_all x1, waiting for transfers between devices, body(): lax.all_to_all(placed.reshape(groups, capacity, row_len * feat_width), 's...  80.8 us
    reduce_scatter x1, waiting for transfers between devices, body(): lax.psum_scatter(grad_key_w, 'seq', scatter_dimension=0, tiled=True)  36.5 us
    reduce_scatter x1, waiting for transfers between devices, body(): lax.psum_scatter(grad_value_w, 'seq', scatter_dimension=0, tiled=True)  33 us
    all_gather x1, waiting for transfers between devices, full_table(): return lax.all_gather(encoded_own, 'ret', axis=0, tiled=True)  32.9 us
    reduce_scatter x1, waiting for transfers between devices, home_sum(): lax.psum_scatter(table_grad, 'ret', scatter_dimension=0, tiled=True)  30.1 us
    dot_general x1, matrix products, attend(): jnp.einsum('chqk,cqhd->ckhd', mixed, queries, preferred_element_type=jnp....  24.3 us
  transfers between devices with their start and end apart: 6, of which 6 were waited for; matrix products, arithmetic and copies ran while one was open for 8% of the time, Pallas kernels for 0%

commit v1 on v0

v1 whole, which is shorter than its diff:
```python
import functools
import math

import jax
import jax.numpy as jnp
from jax import lax
from jax.experimental import pallas as pl
from jax.experimental.pallas import tpu as pltpu
from jax.sharding import PartitionSpec as P

HD = 128
VMEM_BYTES = 48 * 1024 * 1024
NT = (((1,), (1,)), ((), ()))
NN = (((1,), (0,)), ((), ()))


def params():
    return pltpu.CompilerParams(vmem_limit_bytes=VMEM_BYTES)


def vmem():
    return pl.BlockSpec(memory_space=pltpu.VMEM)


def smem():
    return pl.BlockSpec(memory_space=pltpu.SMEM)


def mm(a, b, dims):
    return lax.dot_general(a, b, dims, preferred_element_type=jnp.float32)


def encode(raw_block, up_weight, down_weight):
    amount, row_len, feat_width = raw_block.shape
    inputs = raw_block.reshape(-1, feat_width).astype(jnp.float32)
    normed = (inputs * lax.rsqrt(jnp.mean(inputs * inputs, axis=-1, keepdims=True) + 1e-06)).astype(
        jnp.bfloat16
    )
    hidden = jax.nn.gelu(jnp.dot(normed, up_weight, preferred_element_type=jnp.float32)).astype(
        jnp.bfloat16
    )
    output = inputs + jnp.dot(hidden, down_weight, preferred_element_type=jnp.float32)
    return output.astype(jnp.bfloat16).reshape(amount, row_len, feat_width)


def ranks_of(targets):
    count = targets.shape[-1]
    same = targets[..., :, None] == targets[..., None, :]
    earlier = jnp.arange(count)[:, None] > jnp.arange(count)[None, :]
    return jnp.sum((same & earlier).astype(jnp.int32), axis=-1)


def dispatch_kernel(span_of, q_ref, g_ref, out_ref):
    slots, _, span_len, _ = out_ref.shape

    def step(j, carry):
        row = pl.multiple_of(span_of[j] * span_len, span_len)
        out_ref[j, 0] = q_ref[pl.ds(row, span_len), :]
        out_ref[j, 1] = g_ref[pl.ds(row, span_len), :]
        return carry

    lax.fori_loop(0, slots, step, 0)


def dispatch(span_of, queries, grad_ctx, span_len):
    slots = span_of.shape[0]
    width = queries.shape[1]
    return pl.pallas_call(
        dispatch_kernel,
        out_shape=jax.ShapeDtypeStruct((slots, 2, span_len, width), jnp.bfloat16),
        in_specs=[smem(), vmem(), vmem()],
        out_specs=vmem(),
        compiler_params=params(),
        cost_estimate=pl.CostEstimate(
            flops=0, bytes_accessed=slots * span_len * width * 6, transcendentals=0
        ),
        name="dispatch",
    )(span_of, queries, grad_ctx)


def combine_kernel(position, back_ref, ctx_ref, gq_ref):
    span_len = back_ref.shape[2]
    spans = ctx_ref.shape[0] // span_len

    def step(c, carry):
        first, second = position[2 * c], position[2 * c + 1]
        rows = pl.ds(pl.multiple_of(c * span_len, span_len), span_len)
        for which, out in ((0, ctx_ref), (1, gq_ref)):
            total = back_ref[first, which].astype(jnp.float32) + back_ref[second, which].astype(
                jnp.float32
            )
            out[rows, :] = total.astype(out.dtype)
        return carry

    lax.fori_loop(0, spans, step, 0)


def combine(position, back, rows):
    width = back.shape[3]
    return pl.pallas_call(
        combine_kernel,
        out_shape=[jax.ShapeDtypeStruct((rows, width), jnp.bfloat16)] * 2,
        in_specs=[smem(), vmem()],
        out_specs=[vmem(), vmem()],
        compiler_params=params(),
        cost_estimate=pl.CostEstimate(
            flops=rows * width * 2, bytes_accessed=back.size * 2 + rows * width * 4, transcendentals=0
        ),
        name="combine",
    )(position, back)


def fill_diagonal(dst, block, heads, span_len):
    for h in range(heads):
        dst[h * span_len : (h + 1) * span_len, h * HD : (h + 1) * HD] = block[:, h * HD : (h + 1) * HD]


def slot_scores(kv_ref, nbr, q_diag, g_diag, row_len, width, scale):
    rows = pl.ds(pl.multiple_of(nbr * row_len, row_len), row_len)
    keys = kv_ref[rows, :width]
    values = kv_ref[rows, width:]
    expo = jnp.exp(mm(keys, q_diag[...], NT) * scale)
    grad_probs = mm(values, g_diag[...], NT)
    return rows, keys, values, expo, grad_probs


def stats_kernel(row_len, scale, nbrs, valid, qg_ref, kv_ref, stats_ref, *diag):
    slots, _, span_len, width = qg_ref.shape
    heads = width // HD
    for ref in diag:
        ref[...] = jnp.zeros_like(ref)

    def step(pair, carry):
        @pl.when(valid[2 * pair] + valid[2 * pair + 1] > 0)
        def _():
            for u in range(2):
                j = 2 * pair + u
                fill_diagonal(diag[2 * u], qg_ref[j, 0], heads, span_len)
                fill_diagonal(diag[2 * u + 1], qg_ref[j, 1], heads, span_len)
                _, _, _, expo, grad_probs = slot_scores(
                    kv_ref, nbrs[j], diag[2 * u], diag[2 * u + 1], row_len, width, scale
                )
                total = jnp.sum(expo, axis=0, keepdims=True)
                probs = expo / jnp.where(total > 0.0, total, 1.0)
                stats_ref[j, 0:1, :] = total
                stats_ref[j, 1:2, :] = jnp.sum(probs * grad_probs, axis=0, keepdims=True)

        return carry

    lax.fori_loop(0, slots // 2, step, 0)


def slot_stats(nbrs, valid, qg, kv, row_len, scale):
    slots, _, span_len, width = qg.shape
    lanes = span_len * (width // HD)
    return pl.pallas_call(
        functools.partial(stats_kernel, row_len, scale),
        out_shape=jax.ShapeDtypeStruct((slots, 2, lanes), jnp.float32),
        in_specs=[smem(), smem(), vmem(), vmem()],
        out_specs=vmem(),
        scratch_shapes=[pltpu.VMEM((lanes, width), jnp.bfloat16)] * 4,
        compiler_params=params(),
        cost_estimate=pl.CostEstimate(
            flops=slots * 4 * row_len * lanes * width,
            bytes_accessed=qg.size * 2 + kv.size * 2,
            transcendentals=slots * row_len * lanes,
        ),
        name="slot_stats",
    )(nbrs, valid, qg, kv)


def attend_kernel(
    row_len, scale, nbrs, valid, partner, qg_ref, kv_ref, own_ref, all_ref, back_ref, dkv_ref, acc, *diag
):
    slots, _, span_len, width = qg_ref.shape
    heads = width // HD
    for ref in diag:
        ref[...] = jnp.zeros_like(ref)
    acc[...] = jnp.zeros_like(acc)

    def step(pair, carry):
        @pl.when(valid[2 * pair] + valid[2 * pair + 1] > 0)
        def _():
            for u in range(2):
                j = 2 * pair + u
                q_diag, g_diag = diag[2 * u], diag[2 * u + 1]
                fill_diagonal(q_diag, qg_ref[j, 0], heads, span_len)
                fill_diagonal(g_diag, qg_ref[j, 1], heads, span_len)
                rows, keys, values, expo, grad_probs = slot_scores(
                    kv_ref, nbrs[j], q_diag, g_diag, row_len, width, scale
                )
                own = own_ref[j]
                other = all_ref[partner[j]]
                total = own[0:1] + other[0:1]
                total = jnp.where(total > 0.0, total, 1.0)
                shift = (own[0:1] / total) * own[1:2] + (other[0:1] / total) * other[1:2]
                live = valid[j] > 0
                weights = expo / total
                mixed = weights * (grad_probs - shift) * scale
                weights = jnp.where(live, weights, 0.0)
                mixed = jnp.where(live, mixed, 0.0)
                probs_n = weights.T.astype(jnp.bfloat16)
                mixed_n = mixed.T.astype(jnp.bfloat16)
                for h in range(heads):
                    part = slice(h * span_len, (h + 1) * span_len)
                    cols = slice(h * HD, (h + 1) * HD)
                    back_ref[j, 0, :, cols] = mm(probs_n[part], values[:, cols], NN).astype(jnp.bfloat16)
                    back_ref[j, 1, :, cols] = mm(mixed_n[part], keys[:, cols], NN).astype(jnp.bfloat16)
                acc[rows, :width] += mm(mixed.astype(jnp.bfloat16), q_diag[...], NN)
                acc[rows, width:] += mm(weights.astype(jnp.bfloat16), g_diag[...], NN)

        return carry

    lax.fori_loop(0, slots // 2, step, 0)
    dkv_ref[...] = acc[...].astype(jnp.bfloat16)


def attend(nbrs, valid, partner, qg, kv, own, everyone, row_len, scale):
    slots, _, span_len, width = qg.shape
    lanes = span_len * (width // HD)
    return pl.pallas_call(
        functools.partial(attend_kernel, row_len, scale),
        out_shape=[
            jax.ShapeDtypeStruct(qg.shape, jnp.bfloat16),
            jax.ShapeDtypeStruct(kv.shape, jnp.bfloat16),
        ],
        in_specs=[smem()] * 3 + [vmem()] * 4,
        out_specs=[vmem(), vmem()],
        scratch_shapes=[pltpu.VMEM(kv.shape, jnp.float32)]
        + [pltpu.VMEM((lanes, width), jnp.bfloat16)] * 4,
        compiler_params=params(),
        cost_estimate=pl.CostEstimate(
            flops=slots * 12 * row_len * lanes * width,
            bytes_accessed=qg.size * 4 + kv.size * 4,
            transcendentals=slots * row_len * lanes,
        ),
        name="attend",
    )(nbrs, valid, partner, qg, kv, own, everyone)


def body(
    queries,
    grad_ctx,
    neighbours,
    up_weight,
    down_weight,
    key_weight,
    value_weight,
    group_ids,
    slot_ids,
):
    groups = lax.axis_size("seq")
    me = lax.axis_index("seq")
    span_count = group_ids.shape[0]
    capacity = 2 * span_count // groups + 2
    slot_total = groups * capacity
    width = queries.shape[1]
    span_len = queries.shape[0] // span_count
    own_count, row_len, feat = neighbours.shape
    table_len = own_count * lax.axis_size("ret")
    scale = 1.0 / math.sqrt(HD)

    targets = group_ids.reshape(-1)
    position = targets * capacity + ranks_of(targets)
    request_ids = jnp.arange(2 * span_count, dtype=jnp.int32)
    taken = position[None, :] == jnp.arange(slot_total, dtype=jnp.int32)[:, None]
    span_of = jnp.sum(jnp.where(taken, request_ids[None, :] // 2, 0), axis=1)
    outgoing = dispatch(span_of, queries, grad_ctx, span_len)
    arrived = lax.all_to_all(
        outgoing.reshape(groups, capacity, 2, span_len, width),
        "seq",
        split_axis=0,
        concat_axis=0,
        tiled=True,
    ).reshape(slot_total, 2, span_len, width)

    codes = lax.all_gather(
        group_ids.reshape(-1) * table_len + slot_ids.reshape(-1), "seq", axis=0, tiled=False
    )
    all_targets, all_slots = codes // table_len, codes % table_len
    all_ranks = ranks_of(all_targets)
    sources = jnp.arange(groups, dtype=jnp.int32)[:, None]
    places = all_targets * slot_total + sources * capacity + all_ranks
    partners = jnp.flip(places.reshape(groups, span_count, 2), axis=2).reshape(groups, -1)
    holds = (all_targets == me)[:, None, :] & (
        all_ranks[:, None, :] == jnp.arange(capacity, dtype=jnp.int32)[None, :, None]
    )
    valid = jnp.sum(holds.astype(jnp.int32), axis=2).reshape(-1)
    nbrs = jnp.sum(jnp.where(holds, all_slots[:, None, :], 0), axis=2).reshape(-1)
    partner = jnp.sum(jnp.where(holds, partners[:, None, :], 0), axis=2).reshape(-1)

    encoded_own = encode(neighbours, up_weight, down_weight)
    table = lax.all_gather(encoded_own, "ret", axis=0, tiled=True).reshape(-1, feat)
    kv_weight = jnp.concatenate([key_weight, value_weight], axis=1)
    kv = jnp.dot(table, kv_weight, preferred_element_type=jnp.float32).astype(jnp.bfloat16)

    own_stats = slot_stats(nbrs, valid, arrived, kv, row_len, scale)
    all_stats = lax.all_gather(own_stats, "seq", axis=0, tiled=True)
    outgoing_back, grad_kv = attend(
        nbrs, valid, partner, arrived, kv, own_stats, all_stats, row_len, scale
    )
    back = lax.all_to_all(
        outgoing_back.reshape(groups, capacity, 2, span_len, width),
        "seq",
        split_axis=0,
        concat_axis=0,
        tiled=True,
    ).reshape(slot_total, 2, span_len, width)

    grad_table = mm(grad_kv, kv_weight, NT).astype(jnp.bfloat16)
    grad_encoded = lax.psum_scatter(
        grad_table.reshape(table_len, row_len, feat), "ret", scatter_dimension=0, tiled=True
    )
    grad_weight = mm(table, grad_kv, (((0,), (0,)), ((), ()))).astype(jnp.bfloat16)
    grad_weight = lax.psum_scatter(grad_weight, "seq", scatter_dimension=0, tiled=True)
    context, grad_query = combine(position, back, queries.shape[0])
    return (
        context,
        grad_query,
        grad_encoded,
        grad_weight[:, :width].astype(jnp.float32),
        grad_weight[:, width:].astype(jnp.float32),
    )


def solution(mesh):
    return jax.shard_map(
        body,
        mesh=mesh,
        in_specs=(
            P("seq", "ret"),
            P("seq", "ret"),
            P(("seq", "ret"), None, None),
            P(),
            P(),
            P(None, "ret"),
            P(None, "ret"),
            P("seq", None),
            P("seq", None),
        ),
        out_specs=(
            P("seq", "ret"),
            P("seq", "ret"),
            P(("seq", "ret"), None, None),
            P("seq", "ret"),
            P("seq", "ret"),
        ),
        check_vma=False,
    )
```

time: 624 us -> 260 us (0.42)
  waiting for transfers between devices: 295 us -> 31.9 us
  local copies, waits for them, and re-layouts: 163 us -> 6.87 us
  blocking collectives: 9.59 us -> 131 us
  matrix products: 105 us -> 35.5 us
  Pallas kernels: 0 us -> 29.5 us
  other arithmetic: 19.3 us -> 5.35 us
  starting transfers between devices: 11.9 us -> 5.38 us
    all_to_all x2 -> x1, waiting for transfers between devices: 162 us -> 0.01 us  [body(): lax.all_to_all(outgoing.reshape(groups, capacity, 2, span_len, width), 's...]
    scatter x2 -> x0, local copies, waits for them, and re-layouts: 107 us -> none  [the longest x1 106 us: body(): placed = jnp.zeros((slot_total, row_len * feat_width), jnp.bfloat16).at[p...]
    dot_general x13 -> x3, matrix products: 95.4 us -> 25.8 us  [the longest x2 16.7 us: mm(): return lax.dot_general(a, b, dims, preferred_element_type=jnp.float32)]
    reduce_scatter x3 -> x2, waiting for transfers between devices: 99.6 us -> 31.9 us  [the longest x1 31.9 us: body(): lax.psum_scatter(grad_table.reshape(table_len, row_len, feat), 'ret', sca...]
    all_gather x0 -> x2, blocking collectives: none -> 63.3 us  [the longest x1 50 us: body(): lax.all_gather(group_ids.reshape(-1) * table_len + slot_ids.reshape(-1),...]
    all_to_all x1, blocking collectives: 9.59 us -> 67.5 us  [body(): lax.all_to_all(outgoing_back.reshape(groups, capacity, 2, span_len, width...]
    all_gather x1, waiting for transfers between devices: 32.9 us -> 0.01 us  [body(): lax.all_gather(encoded_own, 'ret', axis=0, tiled=True).reshape(-1, feat)]
    pallas_call x0 -> x4, Pallas kernels: none -> 29.5 us  [the longest x1 17.8 us: attend(): pl.pallas_call(functools.partial(attend_kernel, row_len, scale), out_shap...]
  transfers between devices with their start and end apart: 6 -> 4, of which waited for: 6 -> 1; matrix products, arithmetic and copies ran while one was open for 8% -> 9% of each run, Pallas kernels for 0% -> 1%
where the time goes in v1:
time: 260 us; the launch traced here: 259 us
  blocking collectives  131 us (50%)
  matrix products  35.5 us (14%)
  waiting for transfers between devices  31.9 us (12%)
  Pallas kernels  29.5 us (11%)
  between operations  13.9 us (5%)
  local copies, waits for them, and re-layouts  6.87 us (3%)
  starting transfers between devices  5.38 us (2%)
  other arithmetic  5.35 us (2%)
    all_to_all x1, blocking collectives, body(): lax.all_to_all(outgoing_back.reshape(groups, capacity, 2, span_len, width...  67.5 us
    all_gather x1, blocking collectives, body(): lax.all_gather(group_ids.reshape(-1) * table_len + slot_ids.reshape(-1),...  50 us
    reduce_scatter x1, waiting for transfers between devices, body(): lax.psum_scatter(grad_table.reshape(table_len, row_len, feat), 'ret', sca...  31.9 us
    pallas_call x1, Pallas kernels, attend(): pl.pallas_call(functools.partial(attend_kernel, row_len, scale), out_shap...  17.8 us
    dot_general x2, matrix products, mm(): return lax.dot_general(a, b, dims, preferred_element_type=jnp.float32)  16.7 us
    all_gather x1, blocking collectives, body(): all_stats = lax.all_gather(own_stats, 'seq', axis=0, tiled=True)  13.4 us
    dot_general x1, matrix products, encode(): jnp.dot(hidden, down_weight, preferred_element_type=jnp.float32)  9.64 us
    dot_general x1, matrix products, body(): jnp.dot(table, kv_weight, preferred_element_type=jnp.float32)  9.11 us
  transfers between devices with their start and end apart: 4, of which 1 were waited for; matrix products, arithmetic and copies ran while one was open for 9% of the time, Pallas kernels for 1%

profile of v1, /device:TPU:0, one launch (start us, length us, event | category | flops | bytes accessed | tf_op | source)
XLA Modules:
  0.0 259.3 jit_solution(7849969311769653192)
XLA Ops:
  7.2 0.0 all-gather.3.cloned.1.call-start
  7.2 1.2 multiply_reduce_fusion
  8.4 1.2 fusion.20
  9.6 0.0 copy-start.6
  9.6 0.0 copy-start.2
  9.6 0.0 copy-start.3
  9.6 9.6 %fusion.17 = bf16[256,896]{1,0:T(8,128)(2,1)} fusion(bf16[3584,896]{1,0:T(8,128)(2,1)} %param.13, bf16[256,896]{1,0:T(8,128)(2,1)S(1)} %fusion.20, bf16[896,3584]{1,0:T(8,128)(2,1)} %param.12, bf16[256,896]{1,0:T(8,128)(2,1)} %bitcast.30), kind=kOutput, calls=%fused_computation.18 | convolution fusion | flops 3297280000 | bytes 14221312 | tf_op jit(solution)/shard_map/dot_general | solution.py:42
  19.3 0.0 all-gather.3.cloned.1.call-update
  19.3 0.0 copy-done.6
  19.3 0.1 copy.26
  19.4 0.1 reshape.161
  19.5 0.2 convert_reduce_fusion.2
  19.7 0.1 select_reduce_fusion.2.span_of
  19.8 0.0 copy-done.2
  19.8 0.0 copy-done.3
  19.8 1.0 dispatch.1
  20.8 1.9 copy-done
  22.7 5.3 %all-to-all-start = ((bf16[4,8,2,64,512]{4,3,2,1,0:T(8,128)(2,1)}), bf16[4,8,2,64,512]{4,3,2,1,0:T(8,128)(2,1)}, u32[]{:S(2)}, u32[]{:S(2)}) async-start(bf16[4,8,2,64,512]{4,3,2,1,0:T(8,128)(2,1)} %bitcast.26), calls=%async_computation | async-start | bytes 8388608 | tf_op jit(solution)/shard_map/all_to_all | solution.py:269
  28.0 0.0 reduce-scatter.5.cloned.1.call-start
  28.0 0.1 copy.27
  28.1 0.1 reshape.174
  28.2 50.0 %all-gather = s32[4,1,24]{2,1,0:T(1,128)S(1)} all-gather(s32[1,1,24]{2,1,0:T(1,128)S(1)} %reshape.174), channel_id=1, replica_groups=mesh['seq'=4,'ret'=8] {'seq'}, dimensions={0}, use_global_device_ids=true | all-gather | bytes 480 | tf_op jit(solution)/shard_map/all_gather | solution.py:277
  78.2 0.2 convert_reduce_fusion
  78.4 0.1 add_add_fusion
  78.5 0.1 copy.28
  78.6 0.1 copy.29
  78.7 0.3 select_reduce_fusion
  79.0 0.1 reshape.165.partner
  79.1 0.1 reshape.163.valid
  79.2 0.1 reshape.162.nbrs
  79.2 0.0 copy-done.4
  79.2 1.1 constant_dynamic-update-slice_fusion.1
  80.3 1.1 constant_dynamic-update-slice_fusion
  81.4 9.1 %convolution_convert_fusion.kv_ref = bf16[2048,1024]{1,0:T(8,128)(2,1)} fusion(bf16[2048,896]{1,0:T(8,128)(2,1)} %bitcast.36, bf16[896,1024]{1,0:T(8,128)(2,1)} %constant_dynamic-update-slice_fusion), kind=kOutput, calls=%fused_computation.1 | convolution fusion | flops 3760193536 | bytes 9699328 | tf_op jit(solution)/shard_map/dot_general | solution.py:295
  90.5 0.0 all-to-all-done
  90.5 8.6 %slot_stats.1.own_ref = f32[32,2,256]{2,1,0:T(2,128)S(1)} custom-call(s32[32]{0:T(128)S(1)} %reshape.162.nbrs, s32[32]{0:T(128)S(1)} %reshape.163.valid, bf16[32,2,64,512]{3,2,1,0:T(8,128)(2,1)} %bitcast.4.qg_ref, bf16[2048,1024]{1,0:T(8,128)(2,1)} %convolution_convert_fusion.kv_ref), custom_call_target="tpu_custom_call" | custom-call | flops 2147483648 | bytes 8388608 | tf_op jit(solution)/shard_map/slot_stats/pallas_call | solution.py:156
  99.1 13.4 %all_gather.12.all_ref = f32[128,2,256]{2,1,0:T(2,128)S(1)} all-gather(f32[32,2,256]{2,1,0:T(2,128)S(1)} %slot_stats.1.own_ref), channel_id=1, replica_groups=mesh['seq'=4,'ret'=8] {'seq'}, dimensions={0}, use_global_device_ids=true | all-gather | bytes 327680 | tf_op jit(solution)/shard_map/all_gather | solution.py:298
  112.5 17.8 %attend.1 = (bf16[32,2,64,512]{3,2,1,0:T(8,128)(2,1)S(1)}, bf16[2048,1024]{1,0:T(8,128)(2,1)}) custom-call(s32[32]{0:T(128)S(1)} %reshape.162.nbrs, s32[32]{0:T(128)S(1)} %reshape.163.valid, s32[32]{0:T(128)S(1)} %reshape.165.partner, bf16[32,2,64,512]{3,2,1,0:T(8,128)(2,1)} %bitcast.4.qg_ref, bf16[2048,1024]{1,0:T(8,128)(2,1)} %convolution_convert_fusion.kv_ref, ...), custom_call_target="tpu_custom_call" | custom-call | flops 6442450944 | bytes 16777216 | tf_op jit(solution)/shard_map/attend/pallas_call | solution.py:221
  130.3 2.0 copy-done.1
  132.3 7.5 %convolution_convert_fusion.2 = bf16[896,1024]{1,0:T(8,128)(2,1)} fusion(bf16[2048,896]{1,0:T(8,128)(2,1)S(1)} %bitcast.37, bf16[2048,1024]{1,0:T(8,128)(2,1)} %get-tuple-element.12), kind=kOutput, calls=%fused_computation.16 | convolution fusion | flops 3759013888 | bytes 9699328 | tf_op jit(solution)/shard_map/dot_general | solution.py:30
  139.8 0.0 reduce-scatter.5.cloned.1.call-update
  139.8 0.0 reduce-scatter.3.cloned.1.call-start
  139.9 9.2 %convolution_convert_fusion.1 = bf16[2048,896]{1,0:T(8,128)(2,1)} fusion(bf16[2048,1024]{1,0:T(8,128)(2,1)} %get-tuple-element.12, bf16[896,1024]{1,0:T(8,128)(2,1)} %constant_dynamic-update-slice_fusion), kind=kOutput, calls=%fused_computation.10 | convolution fusion | flops 3759931392 | bytes 9699328 | tf_op jit(solution)/shard_map/dot_general | solution.py:30
  149.1 0.0 reduce-scatter.3.cloned.1.call-update
  149.1 67.5 %all_to_all.10 = bf16[4,8,2,64,512]{4,3,2,1,0:T(8,128)(2,1)S(1)} all-to-all(bf16[4,8,2,64,512]{4,3,2,1,0:T(8,128)(2,1)} %bitcast.28), channel_id=1, replica_groups=mesh['seq'=4,'ret'=8] {'seq'}, dimensions={0} | all-to-all | bytes 8388608 | tf_op jit(solution)/shard_map/all_to_all | solution.py:302
  216.6 2.1 combine.1
  218.8 2.1 slice_convert_fusion
  220.9 31.9 %reduce-scatter.3.cloned.1.call-done = bf16[2,128,896]{2,1,0:T(8,128)(2,1)} async-done(((bf16[16,128,896]{2,1,0:T(8,128)(2,1)}), bf16[2,128,896]{2,1,0:T(8,128)(2,1)}) %reduce-scatter.3.cloned.1.call-update) | async-done | bytes 458768 | tf_op jit(solution)/shard_map/reduce_scatter | solution.py:311
  (19 shorter events, 0.1 us)
Async XLA Ops:
  7.2 74.2 %all-gather.3.cloned.1.call-start = ((), (), s32[]{:S(2)}) async-start(), calls=%async_computation.4 | async-start | bytes 4128768 | tf_op jit(solution)/shard_map/all_gather | solution.py:293
  9.6 9.7 %copy-start.6 = (s32[12,2]{0,1:T(2,128)S(1)}, s32[12,2]{0,1:T(2,128)}, u32[]{:S(2)}) copy-start(s32[12,2]{0,1:T(2,128)} %param.16) | copy-start | bytes 292
  9.6 10.2 %copy-start.2 = (bf16[768,512]{1,0:T(8,128)(2,1)S(1)}, bf16[768,512]{1,0:T(8,128)(2,1)}, u32[]{:S(2)}) copy-start(bf16[768,512]{1,0:T(8,128)(2,1)} %q_ref.1) | copy-start | bytes 2359300
  9.6 10.2 %copy-start.3 = (bf16[768,512]{1,0:T(8,128)(2,1)S(1)}, bf16[768,512]{1,0:T(8,128)(2,1)}, u32[]{:S(2)}) copy-start(bf16[768,512]{1,0:T(8,128)(2,1)} %g_ref.1) | copy-start | bytes 2359300
  20.8 1.9 copy-start
  22.7 5.3 %copy-start.7 = (s32[12,2]{0,1:T(2,128)S(1)}, s32[12,2]{0,1:T(2,128)}, u32[]{:S(2)}) copy-start(s32[12,2]{0,1:T(2,128)} %param.17) | copy-start | bytes 292
  22.7 56.5 %copy-start.4 = (bf16[896,512]{1,0:T(8,128)(2,1)S(1)}, bf16[896,512]{1,0:T(8,128)(2,1)}, u32[]{:S(2)}) copy-start(bf16[896,512]{1,0:T(8,128)(2,1)} %param.14) | copy-start | bytes 2752516
  22.7 57.6 %copy-start.5 = (bf16[896,512]{1,0:T(8,128)(2,1)S(1)}, bf16[896,512]{1,0:T(8,128)(2,1)}, u32[]{:S(2)}) copy-start(bf16[896,512]{1,0:T(8,128)(2,1)} %param.15) | copy-start | bytes 2752516
  22.7 67.8 %all-to-all-start = ((bf16[4,8,2,64,512]{4,3,2,1,0:T(8,128)(2,1)}), bf16[4,8,2,64,512]{4,3,2,1,0:T(8,128)(2,1)}, u32[]{:S(2)}, u32[]{:S(2)}) async-start(bf16[4,8,2,64,512]{4,3,2,1,0:T(8,128)(2,1)} %bitcast.26), calls=%async_computation | async-start | bytes 8388608 | tf_op jit(solution)/shard_map/all_to_all | solution.py:269
  28.0 190.8 %reduce-scatter.5.cloned.1.call-start = ((), (), s32[]{:S(2)}) async-start(), calls=%async_computation.6 | async-start | bytes 2293760 | tf_op jit(solution)/shard_map/reduce_scatter | solution.py:315
  112.5 19.8 %copy-start.8 = (bf16[16,128,896]{2,1,0:T(8,128)(2,1)S(1)}, bf16[16,128,896]{2,1,0:T(8,128)(2,1)}, u32[]{:S(2)}) copy-start(bf16[16,128,896]{2,1,0:T(8,128)(2,1)} %all-gather.3.cloned.1.call-done) | copy-start | bytes 11010052
  130.3 2.0 copy-start.1
  139.8 112.9 %reduce-scatter.3.cloned.1.call-start = ((), (), s32[]{:S(2)}) async-start(), calls=%async_computation.5 | async-start | bytes 4128768 | tf_op jit(solution)/shard_map/reduce_scatter | solution.py:311
Sparse Core Ops, SparseCore 0:
  19.4 45.2 all-gather.2
  139.9 64.7 reduce-scatter.4
  207.6 45.0 reduce-scatter.2

commit v2 on v0

v2 whole, which is shorter than its diff:
```python
import functools
import math

import jax
import jax.numpy as jnp
from jax import lax
from jax.experimental import pallas as pl
from jax.experimental.pallas import tpu as pltpu
from jax.sharding import PartitionSpec as P

HD = 128
NT = (((1,), (1,)), ((), ()))
NN = (((1,), (0,)), ((), ()))
TN = (((0,), (0,)), ((), ()))
BF16 = jnp.bfloat16
F32 = jnp.float32


def params(mib):
    return pltpu.CompilerParams(vmem_limit_bytes=mib * 1024 * 1024)


def vmem():
    return pl.BlockSpec(memory_space=pltpu.VMEM)


def anyspace():
    return pl.BlockSpec(memory_space=pl.ANY)


def smem():
    return pl.BlockSpec(memory_space=pltpu.SMEM)


def cost(flops, nbytes, trans=0):
    return pl.CostEstimate(flops=flops, bytes_accessed=nbytes, transcendentals=trans)


def mm(a, b, dims):
    return lax.dot_general(a, b, dims, preferred_element_type=F32)


def fetch(pairs, sems):
    copies = [pltpu.make_async_copy(src, dst, sems.at[i]) for i, (src, dst) in enumerate(pairs)]
    for copy in copies:
        copy.start()
    return copies


def encode_kernel(x_ref, up_ref, down_ref, out_ref, up, down, normed, acc, usem, dsem):
    steps, _, block = up.shape

    def copies(i):
        cols = pl.ds(pl.multiple_of(i * block, block), block)
        return (
            pltpu.make_async_copy(up_ref.at[:, cols], up.at[i], usem.at[i]),
            pltpu.make_async_copy(down_ref.at[cols, :], down.at[i], dsem.at[i]),
        )

    for i in range(steps):
        for copy in copies(i):
            copy.start()
    x = x_ref[...].astype(F32)
    normed[...] = (x * lax.rsqrt(jnp.mean(x * x, axis=-1, keepdims=True) + 1e-06)).astype(BF16)
    acc[...] = x

    def step(i, carry):
        up_in, down_in = copies(i)
        up_in.wait()
        h = mm(normed[...], up[i], NN)
        inner = math.sqrt(2.0 / math.pi) * (h + 0.044715 * (h * h * h))
        hidden = (0.5 * h * (1.0 + jnp.tanh(inner))).astype(BF16)
        down_in.wait()
        acc[...] += mm(hidden, down[i], NN)
        return carry

    lax.fori_loop(0, steps, step, 0)
    out_ref[...] = acc[...].astype(BF16)


def encode(neighbours, up_weight, down_weight):
    feat, hidden = up_weight.shape
    rows = neighbours.reshape(-1, feat)
    block = 512 if hidden % 512 == 0 else hidden
    steps = hidden // block
    return pl.pallas_call(
        encode_kernel,
        out_shape=jax.ShapeDtypeStruct(rows.shape, BF16),
        in_specs=[vmem(), anyspace(), anyspace()],
        out_specs=vmem(),
        scratch_shapes=[
            pltpu.VMEM((steps, feat, block), BF16),
            pltpu.VMEM((steps, block, feat), BF16),
            pltpu.VMEM(rows.shape, BF16),
            pltpu.VMEM(rows.shape, F32),
            pltpu.SemaphoreType.DMA((steps,)),
            pltpu.SemaphoreType.DMA((steps,)),
        ],
        compiler_params=params(56),
        cost_estimate=cost(4 * rows.shape[0] * feat * hidden, 4 * feat * hidden, rows.shape[0] * hidden),
        name="encode",
    )(rows, up_weight, down_weight).reshape(neighbours.shape)


def project_kernel(table_ref, kw_ref, vw_ref, kv_ref):
    width = kw_ref.shape[1]
    kv_ref[:, :width] = mm(table_ref[...], kw_ref[...], NN).astype(BF16)
    kv_ref[:, width:] = mm(table_ref[...], vw_ref[...], NN).astype(BF16)


def project(table, key_weight, value_weight):
    rows, feat = table.shape
    width = key_weight.shape[1]
    block = 512 if rows % 512 == 0 else rows
    return pl.pallas_call(
        project_kernel,
        grid=(rows // block,),
        out_shape=jax.ShapeDtypeStruct((rows, 2 * width), BF16),
        in_specs=[
            pl.BlockSpec((block, feat), lambda i: (i, 0)),
            pl.BlockSpec((feat, width), lambda i: (0, 0)),
            pl.BlockSpec((feat, width), lambda i: (0, 0)),
        ],
        out_specs=pl.BlockSpec((block, 2 * width), lambda i: (i, 0)),
        compiler_params=params(59),
        cost_estimate=cost(40 * rows * feat * width, rows * (feat + 2 * width) * 2),
        name="project",
    )(table, key_weight, value_weight)


def exchange(pieces, axis):
    size = len(pieces)
    return [pieces[0]] + [
        lax.ppermute(pieces[d], axis, [(s, s ^ d) for s in range(size)]) for d in range(1, size)
    ]


def signs_of(*arrays):
    return [lax.slice(a, (0,) * a.ndim, (1,) * (a.ndim - 1) + (8,)) for a in arrays]


def dispatch_kernel(waits, me, group_ids, q_ref, g_ref, *refs):
    out_refs, refs = refs[waits:-5], refs[-5:]
    position, place, taken, held, sems = refs
    groups, capacity, _, span_len, _ = held.shape
    for d in range(groups):
        taken[d] = 0

    def step(i, carry):
        span = i // 2
        offset = jnp.bitwise_xor(group_ids[span, i % 2], me[0])
        rank = taken[offset]
        taken[offset] = rank + 1
        position[i] = offset * capacity + rank
        place[i] = offset * groups * capacity + offset * capacity + rank
        rows = pl.ds(pl.multiple_of(span * span_len, span_len), span_len)
        held[offset, rank, 0] = q_ref[rows, :]
        held[offset, rank, 1] = g_ref[rows, :]
        return carry

    lax.fori_loop(0, position.shape[0], step, 0)
    for copy in fetch([(held.at[d], ref) for d, ref in enumerate(out_refs)], sems):
        copy.wait()


def dispatch(me, group_ids, queries, grad_ctx, groups, capacity, span_len, waits):
    width = queries.shape[1]
    requests = group_ids.size
    piece = (capacity, 2, span_len, width)
    outs = pl.pallas_call(
        functools.partial(dispatch_kernel, len(waits)),
        out_shape=[jax.ShapeDtypeStruct(piece, BF16)] * groups
        + [jax.ShapeDtypeStruct((requests,), jnp.int32)] * 2,
        in_specs=[smem(), smem(), vmem(), vmem()] + [anyspace()] * len(waits),
        out_specs=[anyspace()] * groups + [smem()] * 2,
        scratch_shapes=[
            pltpu.SMEM((groups,), jnp.int32),
            pltpu.VMEM((groups, *piece), BF16),
            pltpu.SemaphoreType.DMA((groups,)),
        ],
        compiler_params=params(56),
        cost_estimate=cost(0, groups * capacity * span_len * width * 6),
        name="dispatch",
    )(me, group_ids, queries, grad_ctx, *waits)
    return outs[:groups], outs[groups], outs[groups + 1]


def slots_kernel(groups, waits, capacity, table_len, me, *refs):
    codes, (counts, nbrs, partner, taken) = refs[:groups], refs[groups + waits :]
    slots = groups * capacity

    def clear(j, carry):
        nbrs[j] = 0
        partner[j] = 0
        return carry

    lax.fori_loop(0, slots, clear, 0)
    for d in range(groups):
        source = jnp.bitwise_xor(me[0], d)
        for h in range(groups):
            taken[h] = 0

        def step(span, carry, d=d, source=source):
            both = []
            for i in range(2):
                code = codes[d][0, 2 * span + i]
                target = code // table_len
                rank = taken[target]
                taken[target] = rank + 1
                there = jnp.bitwise_xor(target, source) * capacity + rank
                both.append((target, rank, code % table_len, there))
            for i in range(2):
                target, rank, nbr, _ = both[i]
                other, _, _, there = both[1 - i]

                @pl.when(target == me[0])
                def _():
                    nbrs[d * capacity + rank] = nbr
                    partner[d * capacity + rank] = jnp.bitwise_xor(other, me[0]) * slots + there

            return carry

        lax.fori_loop(0, codes[d].shape[1] // 2, step, 0)
        counts[d] = taken[me[0]]


def slot_lists(me, codes, capacity, table_len, waits):
    groups = len(codes)
    slots = groups * capacity
    return pl.pallas_call(
        functools.partial(slots_kernel, groups, len(waits), capacity, table_len),
        out_shape=[
            jax.ShapeDtypeStruct((groups,), jnp.int32),
            jax.ShapeDtypeStruct((slots,), jnp.int32),
            jax.ShapeDtypeStruct((slots,), jnp.int32),
        ],
        in_specs=[smem()] * (1 + groups) + [anyspace()] * len(waits),
        out_specs=[smem()] * 3,
        scratch_shapes=[pltpu.SMEM((groups,), jnp.int32)],
        compiler_params=params(56),
        cost_estimate=cost(0, slots * 16),
        name="slot_lists",
    )(me, *codes, *waits)


def gather_groups(refs, held):
    size = refs[0].shape[0]
    for d, ref in enumerate(refs):
        held[d * size : (d + 1) * size] = ref[...]


def combine_grad_kernel(groups, position, *refs):
    pieces, (out, held) = refs[:groups], refs[-2:]
    span_len = held.shape[1]
    gather_groups(pieces, held)

    def step(c, carry):
        rows = pl.ds(pl.multiple_of(c * span_len, span_len), span_len)
        first, second = held[position[2 * c]], held[position[2 * c + 1]]
        out[rows, :] = (first.astype(F32) + second.astype(F32)).astype(BF16)
        return carry

    lax.fori_loop(0, out.shape[0] // span_len, step, 0)


def combine_grad(position, pieces, rows, waits):
    groups = len(pieces)
    capacity, span_len, width = pieces[0].shape
    return pl.pallas_call(
        functools.partial(combine_grad_kernel, groups),
        out_shape=jax.ShapeDtypeStruct((rows, width), BF16),
        in_specs=[smem()] + [vmem()] * groups + [anyspace()] * len(waits),
        out_specs=vmem(),
        scratch_shapes=[pltpu.VMEM((groups * capacity, span_len, width), BF16)],
        compiler_params=params(16),
        cost_estimate=cost(rows * width * 250000, groups * pieces[0].size * 2 + rows * width * 2),
        name="combine_grad_queries",
    )(position, *pieces, *waits)


def combine_context_kernel(groups, position, place, *refs):
    pieces, stats = refs[:groups], refs[groups : 2 * groups]
    out, held, held_stats, shares = refs[2 * groups :]
    span_len, width = held.shape[1:]
    spans = out.shape[0] // span_len
    gather_groups(pieces, held)
    gather_groups(stats, held_stats)
    shares[...] = jnp.zeros_like(shares)
    for c in range(spans):
        first = held_stats[place[2 * c]][0:1]
        second = held_stats[place[2 * c + 1]][0:1]
        total = first + second
        shares[2 * c : 2 * c + 1, :] = first / total
        shares[2 * c + 1 : 2 * c + 2, :] = second / total
    columns = shares[...].T
    for c in range(spans):
        pair = [held[position[2 * c + i]] for i in range(2)]
        for h in range(width // HD):
            cols = slice(h * HD, (h + 1) * HD)
            part = columns[h * span_len : (h + 1) * span_len]
            total = sum(
                pair[i][:, cols].astype(F32) * part[:, 2 * c + i : 2 * c + i + 1] for i in range(2)
            )
            out[c * span_len : (c + 1) * span_len, cols] = total.astype(BF16)


def combine_context(position, place, pieces, stats, rows):
    groups = len(pieces)
    capacity, span_len, width = pieces[0].shape
    slots, two, lanes = stats[0].shape
    padded = -(-2 * (rows // span_len) // 128) * 128
    return pl.pallas_call(
        functools.partial(combine_context_kernel, groups),
        out_shape=jax.ShapeDtypeStruct((rows, width), BF16),
        in_specs=[smem()] * 2 + [vmem()] * (2 * groups),
        out_specs=vmem(),
        scratch_shapes=[
            pltpu.VMEM((groups * capacity, span_len, width), BF16),
            pltpu.VMEM((groups * slots, two, lanes), F32),
            pltpu.VMEM((padded, lanes), F32),
        ],
        compiler_params=params(24),
        cost_estimate=cost(rows * width * 4, groups * pieces[0].size * 2 + rows * width * 2),
        name="combine_context",
    )(position, place, *pieces, *stats)


def fill_diagonal(dst, block, heads, span_len):
    for h in range(heads):
        side = (h % 2) * HD
        dst[h * span_len : (h + 1) * span_len, side : side + HD] = block[:, h * HD : (h + 1) * HD]


def store_pair(dst, k, p, both, span_len):
    for s in range(2):
        cols = slice((2 * p + s) * HD, (2 * p + s + 1) * HD)
        rows = slice(s * span_len, (s + 1) * span_len)
        dst[k, :, cols] = both[rows, s * HD : (s + 1) * HD].astype(BF16)


def rows_of(nbr, row_len):
    return pl.ds(pl.multiple_of(nbr * row_len, row_len), row_len)


def columns_of(p, width, span_len):
    first = 2 * p * HD
    return (
        slice(first, first + 2 * HD),
        slice(width + first, width + first + 2 * HD),
        slice(2 * p * span_len, 2 * (p + 1) * span_len),
    )


def arrival(held, d, sems):
    return pltpu.make_async_copy(held.at[d], held.at[d], sems.at[d])


def local_kernel(groups, row_len, scale, counts, nbrs, *refs):
    qg_refs, (kv_ref, stats_ref), refs = refs[:groups], refs[groups : groups + 2], refs[groups + 2 :]
    ctx_refs, refs = refs[:groups], refs[groups:]
    kv, qg, ctx, ksem, isem, osem = refs[:6]
    diag = refs[6:]
    capacity, _, span_len, width = qg_refs[0].shape
    heads = width // HD
    kv_in = fetch([(kv_ref, kv)], ksem)
    fetch([(ref, qg.at[d]) for d, ref in enumerate(qg_refs)], isem)
    ctx_out = [pltpu.make_async_copy(ctx.at[d], ref, osem.at[d]) for d, ref in enumerate(ctx_refs)]
    for ref in diag:
        ref[...] = jnp.zeros_like(ref)
    kv_in[0].wait()

    def one_group(d, carry):
        arrival(qg, d, isem).wait()

        def step(i, carry):
            for u in range(2):
                k = jnp.minimum(2 * i + u, counts[d] - 1)
                j = d * capacity + k
                q_diag, g_diag = diag[2 * u], diag[2 * u + 1]
                fill_diagonal(q_diag, qg[d, k, 0], heads, span_len)
                fill_diagonal(g_diag, qg[d, k, 1], heads, span_len)
                rows = rows_of(nbrs[j], row_len)
                for p in range(heads // 2):
                    cols, vcols, lanes = columns_of(p, width, span_len)
                    values = kv[rows, vcols]
                    expo = jnp.exp(mm(kv[rows, cols], q_diag[lanes, :], NT) * scale)
                    grad_probs = mm(values, g_diag[lanes, :], NT)
                    total = jnp.sum(expo, axis=0, keepdims=True)
                    probs = expo / jnp.where(total > 0.0, total, 1.0)
                    stats_ref[j, 0:1, lanes] = total
                    stats_ref[j, 1:2, lanes] = jnp.sum(probs * grad_probs, axis=0, keepdims=True)
                    store_pair(ctx.at[d], k, p, mm(probs.astype(BF16).T, values, NN), span_len)
            return carry

        lax.fori_loop(0, (counts[d] + 1) // 2, step, 0)
        for e in range(groups):

            @pl.when(d == e)
            def _():
                ctx_out[e].start()

        return carry

    lax.fori_loop(0, groups, one_group, 0)
    for copy in ctx_out:
        copy.wait()


def attend_local(counts, nbrs, qg, kv, row_len, scale):
    groups = len(qg)
    capacity, _, span_len, width = qg[0].shape
    slots = groups * capacity
    lanes = span_len * (width // HD)
    outs = pl.pallas_call(
        functools.partial(local_kernel, groups, row_len, scale),
        out_shape=[jax.ShapeDtypeStruct((slots, 2, lanes), F32)]
        + [jax.ShapeDtypeStruct((capacity, span_len, width), BF16)] * groups,
        in_specs=[smem()] * 2 + [anyspace()] * (groups + 1),
        out_specs=[vmem()] + [anyspace()] * groups,
        scratch_shapes=[
            pltpu.VMEM(kv.shape, BF16),
            pltpu.VMEM((groups, *qg[0].shape), BF16),
            pltpu.VMEM((groups, capacity, span_len, width), BF16),
            pltpu.SemaphoreType.DMA((1,)),
            pltpu.SemaphoreType.DMA((groups,)),
            pltpu.SemaphoreType.DMA((groups,)),
        ]
        + [pltpu.VMEM((lanes, 2 * HD), BF16)] * 4,
        compiler_params=params(56),
        cost_estimate=cost(
            slots * 48 * row_len * lanes * HD,
            kv.size * 2 + slots * span_len * width * 6,
            slots * row_len * lanes,
        ),
        name="attend_local",
    )(counts, nbrs, *qg, kv)
    return outs[0], outs[1:]


def grads_kernel(groups, row_len, scale, counts, nbrs, partner, *refs):
    qg_refs, stat_refs, refs = refs[:groups], refs[groups : 2 * groups], refs[2 * groups :]
    (kv_ref, kw_ref, vw_ref), refs = refs[:3], refs[3:]
    gq_refs, (dkv_ref, part_ref), refs = refs[:groups], refs[groups : groups + 2], refs[groups + 2 :]
    kv, qg, stats, kw, vw, gq, acc, dkv, part, ksem, qsem, ssem, osem, psem = refs[:14]
    diag = refs[14:]
    capacity, _, span_len, width = qg_refs[0].shape
    slots = groups * capacity
    heads = width // HD
    stats_in = fetch(
        [(ref, stats.at[pl.ds(d * slots, slots)]) for d, ref in enumerate(stat_refs)], ssem
    )
    kv_in, kw_in, vw_in = fetch([(kv_ref, kv), (kw_ref, kw), (vw_ref, vw)], ksem)
    fetch([(ref, qg.at[d]) for d, ref in enumerate(qg_refs)], qsem)
    gq_out = [pltpu.make_async_copy(gq.at[d], ref, osem.at[d]) for d, ref in enumerate(gq_refs)]
    for ref in diag:
        ref[...] = jnp.zeros_like(ref)
    block = 256 if kv.shape[0] % 256 == 0 else kv.shape[0]
    blocks = kv.shape[0] // block

    def rows_at(i):
        return pl.ds(pl.multiple_of(i * block, block), block)

    def clear(i, carry):
        acc[rows_at(i), :] = jnp.zeros((block, 2 * width), F32)
        return carry

    lax.fori_loop(0, blocks, clear, 0)
    for copy in [*stats_in, kv_in]:
        copy.wait()

    def one_group(d, carry):
        arrival(qg, d, qsem).wait()

        def step(i, carry):
            for u in range(2):
                place = 2 * i + u
                live = place < counts[d]
                k = jnp.minimum(place, counts[d] - 1)
                j = d * capacity + k
                q_diag, g_diag = diag[2 * u], diag[2 * u + 1]
                fill_diagonal(q_diag, qg[d, k, 0], heads, span_len)
                fill_diagonal(g_diag, qg[d, k, 1], heads, span_len)
                rows = rows_of(nbrs[j], row_len)
                own, other = stats[j], stats[partner[j]]
                total = own[0:1] + other[0:1]
                total = jnp.where(total > 0.0, total, 1.0)
                shift = (own[0:1] / total) * own[1:2] + (other[0:1] / total) * other[1:2]
                for p in range(heads // 2):
                    cols, vcols, lanes = columns_of(p, width, span_len)
                    keys = kv[rows, cols]
                    expo = jnp.exp(mm(keys, q_diag[lanes, :], NT) * scale)
                    grad_probs = mm(kv[rows, vcols], g_diag[lanes, :], NT)
                    weights = expo / total[:, lanes]
                    mixed = weights * (grad_probs - shift[:, lanes]) * scale
                    store_pair(gq.at[d], k, p, mm(mixed.astype(BF16).T, keys, NN), span_len)
                    weights = jnp.where(live, weights, 0.0).astype(BF16)
                    mixed = jnp.where(live, mixed, 0.0).astype(BF16)
                    acc[rows, cols] += mm(mixed, q_diag[lanes, :], NN)
                    acc[rows, vcols] += mm(weights, g_diag[lanes, :], NN)
            return carry

        lax.fori_loop(0, (counts[d] + 1) // 2, step, 0)
        for e in range(groups):

            @pl.when(d == e)
            def _():
                gq_out[e].start()

        return carry

    lax.fori_loop(0, groups, one_group, 0)
    kw_in.wait()
    vw_in.wait()

    def results(i):
        b = rows_at(i)
        return (
            pltpu.make_async_copy(part.at[b], part_ref.at[b], psem.at[i, 0]),
            pltpu.make_async_copy(dkv.at[b], dkv_ref.at[b], psem.at[i, 1]),
        )

    def finish(i, carry):
        b = rows_at(i)
        dkv[b, :] = acc[b, :].astype(BF16)
        part[b, :] = (mm(dkv[b, :width], kw[...], NT) + mm(dkv[b, width:], vw[...], NT)).astype(BF16)
        for copy in results(i):
            copy.start()
        return carry

    def drain(i, carry):
        for copy in results(i):
            copy.wait()
        return carry

    lax.fori_loop(0, blocks, finish, 0)
    lax.fori_loop(0, blocks, drain, 0)
    for copy in gq_out:
        copy.wait()


def row_blocks(total, size):
    size = size if total % size == 0 else total
    return [pl.ds(i * size, size) for i in range(total // size)]


def attend_grads(counts, nbrs, partner, qg, stats, kv, key_weight, value_weight, row_len, scale):
    groups = len(qg)
    capacity, _, span_len, width = qg[0].shape
    slots = groups * capacity
    lanes = span_len * (width // HD)
    rows = kv.shape[0]
    feat = key_weight.shape[0]
    outs = pl.pallas_call(
        functools.partial(grads_kernel, groups, row_len, scale),
        out_shape=[jax.ShapeDtypeStruct((capacity, span_len, width), BF16)] * groups
        + [
            jax.ShapeDtypeStruct((rows, 2 * width), BF16),
            jax.ShapeDtypeStruct((rows, feat), BF16),
        ],
        in_specs=[smem()] * 3 + [anyspace()] * (2 * groups + 3),
        out_specs=[anyspace()] * (groups + 2),
        scratch_shapes=[
            pltpu.VMEM(kv.shape, BF16),
            pltpu.VMEM((groups, *qg[0].shape), BF16),
            pltpu.VMEM((groups * slots, 2, lanes), F32),
            pltpu.VMEM((feat, width), BF16),
            pltpu.VMEM((feat, width), BF16),
            pltpu.VMEM((groups, capacity, span_len, width), BF16),
            pltpu.VMEM((rows, 2 * width), F32),
            pltpu.VMEM((rows, 2 * width), BF16),
            pltpu.VMEM((rows, feat), BF16),
            pltpu.SemaphoreType.DMA((3,)),
            pltpu.SemaphoreType.DMA((groups,)),
            pltpu.SemaphoreType.DMA((groups,)),
            pltpu.SemaphoreType.DMA((groups,)),
            pltpu.SemaphoreType.DMA((max(1, rows // 256), 2)),
        ]
        + [pltpu.VMEM((lanes, 2 * HD), BF16)] * 4,
        compiler_params=params(56),
        cost_estimate=cost(
            4 * rows * feat * width + slots * 72 * row_len * lanes * HD,
            rows * feat * 2 + rows * width * 8 + slots * span_len * width * 6,
            slots * row_len * lanes,
        ),
        name="attend_grads",
    )(counts, nbrs, partner, *qg, *stats, kv, key_weight, value_weight)
    return outs[:groups], outs[groups], outs[groups + 1]


def weight_kernel(groups, waits, me, table, dkv, *refs):
    piece_refs, total = refs[waits : waits + groups], refs[-1]
    share = total.shape[1]
    for cols in row_blocks(total.shape[2], 256):
        product = mm(table[...], dkv[:, cols], TN).astype(BF16)
        for e in range(groups):
            total[e, :, cols] = product[e * share : (e + 1) * share]
    for d, piece in enumerate(piece_refs):
        piece[...] = total[jnp.bitwise_xor(me[0], d)]


def grad_weights(me, table, grad_kv, groups, waits):
    feat, columns = table.shape[1], grad_kv.shape[1]
    return pl.pallas_call(
        functools.partial(weight_kernel, groups, len(waits)),
        out_shape=[jax.ShapeDtypeStruct((feat // groups, columns), BF16)] * groups,
        in_specs=[smem(), vmem(), vmem()] + [anyspace()] * len(waits),
        out_specs=[vmem()] * groups,
        scratch_shapes=[pltpu.VMEM((groups, feat // groups, columns), BF16)],
        compiler_params=params(56),
        cost_estimate=cost(table.size * columns * 2, table.size * 2 + grad_kv.size * 2),
        name="grad_weights",
    )(me, table, grad_kv, *waits)


def body(
    queries,
    grad_ctx,
    neighbours,
    up_weight,
    down_weight,
    key_weight,
    value_weight,
    group_ids,
    slot_ids,
):
    groups = lax.axis_size("seq")
    if groups & (groups - 1):
        raise ValueError("seq size")
    me = lax.axis_index("seq").reshape(1)
    span_count = group_ids.shape[0]
    capacity = 2 * span_count // groups + 2
    width = queries.shape[1]
    span_len = queries.shape[0] // span_count
    own_count, row_len, feat = neighbours.shape
    table_len = own_count * lax.axis_size("ret")
    scale = 1.0 / math.sqrt(HD)

    encoded_own = encode(neighbours, up_weight, down_weight)
    table = lax.all_gather(encoded_own, "ret", axis=0, tiled=True).reshape(-1, feat)
    outgoing, position, place = dispatch(
        me, group_ids, queries, grad_ctx, groups, capacity, span_len, signs_of(encoded_own)
    )
    arrived = exchange(outgoing, "seq")
    kv = project(table, key_weight, value_weight)

    codes = (group_ids * table_len + slot_ids).reshape(1, -1)
    codes = exchange([codes] * groups, "seq")
    counts, nbrs, partner = slot_lists(me, codes, capacity, table_len, signs_of(kv))
    own_stats, local_ctx = attend_local(counts, nbrs, arrived, kv, row_len, scale)
    stats = exchange([own_stats] * groups, "seq")
    ctx_back = exchange(local_ctx, "seq")
    local_gq, grad_kv, grad_table = attend_grads(
        counts, nbrs, partner, arrived, stats, kv, key_weight, value_weight, row_len, scale
    )
    grad_encoded = lax.psum_scatter(
        grad_table.reshape(table_len, row_len, feat), "ret", scatter_dimension=0, tiled=True
    )
    gq_back = exchange(local_gq, "seq")
    pieces = exchange(
        grad_weights(me, table, grad_kv, groups, signs_of(*ctx_back[1:])), "seq"
    )
    grad_weight = sum(piece.astype(F32) for piece in pieces)
    context = combine_context(position, place, ctx_back, stats, queries.shape[0])
    grad_query = combine_grad(position, gq_back, queries.shape[0], [])
    return (context, grad_query, grad_encoded, grad_weight[:, :width], grad_weight[:, width:])


def solution(mesh):
    return jax.shard_map(
        body,
        mesh=mesh,
        in_specs=(
            P("seq", "ret"),
            P("seq", "ret"),
            P(("seq", "ret"), None, None),
            P(),
            P(),
            P(None, "ret"),
            P(None, "ret"),
            P("seq", None),
            P("seq", None),
        ),
        out_specs=(
            P("seq", "ret"),
            P("seq", "ret"),
            P(("seq", "ret"), None, None),
            P("seq", "ret"),
            P("seq", "ret"),
        ),
        check_vma=False,
    )
```

time: 624 us -> 194 us (0.31)
  waiting for transfers between devices: 295 us -> 60.8 us
  local copies, waits for them, and re-layouts: 163 us -> 8.33 us
  matrix products: 105 us -> 0 us
  Pallas kernels: 0 us -> 79.7 us
  other arithmetic: 19.3 us -> 0.29 us
  starting transfers between devices: 11.9 us -> 30.3 us
  blocking collectives: 9.59 us -> 0 us
    all_to_all x2 -> x0, waiting for transfers between devices: 162 us -> none  [the longest x1 81.3 us: body(): lax.all_to_all(source_rows.reshape(groups, capacity, row_len, feat_width)...]
    scatter x2 -> x0, local copies, waits for them, and re-layouts: 107 us -> none  [the longest x1 106 us: body(): placed = jnp.zeros((slot_total, row_len * feat_width), jnp.bfloat16).at[p...]
    dot_general x14 -> x0, matrix products: 105 us -> none  [the longest x1 24.3 us: attend(): jnp.einsum('chqk,cqhd->ckhd', mixed, queries, preferred_element_type=jnp....]
    reduce_scatter x3 -> x1, waiting for transfers between devices: 99.6 us -> 4.13 us  [body(): lax.psum_scatter(grad_table.reshape(table_len, row_len, feat), 'ret', sca...]
    pallas_call x0 -> x9, Pallas kernels: none -> 79.7 us  [the longest x1 26.4 us: attend_grads(): pl.pallas_call(functools.partial(grads_kernel, groups, row_len, scale), o...]
    ppermute x0 -> x18, starting transfers between devices: none -> 30.2 us  [exchange(): lax.ppermute(pieces[d], axis, [(s, s ^ d) for s in range(size)])]
    ppermute x0 -> x18, waiting for transfers between devices: none -> 26 us  [exchange(): lax.ppermute(pieces[d], axis, [(s, s ^ d) for s in range(size)])]
    reshape x10 -> x1, local copies, waits for them, and re-layouts: 20.4 us -> 0.08 us  [body(): codes = (group_ids * table_len + slot_ids).reshape(1, -1)]
  transfers between devices with their start and end apart: 6 -> 20, of which waited for: 6 -> 8; matrix products, arithmetic and copies ran while one was open for 8% -> 3% of each run, Pallas kernels for 0% -> 28%
where the time goes in v2:
time: 194 us
  Pallas kernels  79.7 us (41%)
  waiting for transfers between devices  60.8 us (31%)
  starting transfers between devices  30.3 us (16%)
  between operations  14.3 us (7%)
  local copies, waits for them, and re-layouts  8.33 us (4%)
    all_gather x1, waiting for transfers between devices, body(): lax.all_gather(encoded_own, 'ret', axis=0, tiled=True).reshape(-1, feat)  30.6 us
    ppermute x18, starting transfers between devices, exchange(): lax.ppermute(pieces[d], axis, [(s, s ^ d) for s in range(size)])  30.2 us
    pallas_call x1, Pallas kernels, attend_grads(): pl.pallas_call(functools.partial(grads_kernel, groups, row_len, scale), o...  26.4 us
    ppermute x18, waiting for transfers between devices, exchange(): lax.ppermute(pieces[d], axis, [(s, s ^ d) for s in range(size)])  26 us
    pallas_call x1, Pallas kernels, attend_local(): pl.pallas_call(functools.partial(local_kernel, groups, row_len, scale), o...  14.7 us
    pallas_call x1, Pallas kernels, encode(): pl.pallas_call(encode_kernel, out_shape=jax.ShapeDtypeStruct(rows.shape,...  10 us
    pallas_call x1, Pallas kernels, grad_weights(): pl.pallas_call(functools.partial(weight_kernel, groups, len(waits)), out_...  8.66 us
    pallas_call x1, Pallas kernels, project(): pl.pallas_call(project_kernel, grid=(rows // block,), out_shape=jax.Shape...  8.12 us
  transfers between devices with their start and end apart: 20, of which 8 were waited for; matrix products, arithmetic and copies ran while one was open for 3% of the time, Pallas kernels for 28%

profile of v2, /device:TPU:0, one launch (start us, length us, event | category | flops | bytes accessed | tf_op | source)
XLA Modules:
  0.0 193.7 jit_solution(15528677283020414750)
XLA Ops:
  7.2 0.0 all-gather.2.cloned.1.call-start
  7.2 10.0 %encode.1 = bf16[256,896]{1,0:T(8,128)(2,1)} custom-call(bf16[256,896]{1,0:T(8,128)(2,1)} %bitcast.8, bf16[896,3584]{1,0:T(8,128)(2,1)} %up_ref.1, bf16[3584,896]{1,0:T(8,128)(2,1)} %down_ref.1), custom_call_target="tpu_custom_call" | custom-call | flops 3288334336 | bytes 12845056 | tf_op jit(solution)/shard_map/encode/pallas_call | solution.py:86
  17.3 0.0 reduce-scatter.2.cloned.1.call-start
  17.4 0.1 copy.19
  17.4 0.1 reshape.31.refs_0_
  17.5 4.0 %collective-permute-start.2 = (s32[1,24]{1,0:T(1,128)S(1)}, s32[1,24]{1,0:T(1,128)S(1)}, u32[]{:S(2)}, u32[]{:S(2)}) collective-permute-start(s32[1,24]{1,0:T(1,128)S(1)} %reshape.31.refs_0_), channel_id=1, source_target_pairs={{0,24},{8,16},{16,8},{24,0},{1,25},{9,17},{17,9},{25,1},{2,26},{10... | collective-permute-start | bytes 296 | tf_op jit(solution)/shard_map/ppermute | solution.py:134
  21.5 0.5 collective-permute-start.1
  22.0 0.7 copy.18.group_ids
  22.7 1.2 slice.28.refs_0_
  23.9 4.7 %dispatch.1 = (bf16[8,2,64,512]{3,2,1,0:T(8,128)(2,1)}, bf16[8,2,64,512]{3,2,1,0:T(8,128)(2,1)}, bf16[8,2,64,512]{3,2,1,0:T(8,128)(2,1)}, bf16[8,2,64,512]{3,2,1,0:T(8,128)(2,1)}, s32[24]{0:T(128)}, /*index=5*/s32[24]{0:T(128)}) custom-call(s32[1]{0:T(128)} %bitcast.me, s32[12,2]{1,0:T(8,128)} %copy.18.group_ids, bf16[768,512]{1,0:T(8,128)(2,1)} %q_ref.1, ...), custom_call_target="tpu_custom_call" | custom-call | bytes 6291456 | tf_op jit(solution)/shard_map/dispatch/pallas_call | solution.py:170
  28.6 0.1 collective-permute-start.3
  28.7 2.0 %collective-permute-start.4 = (bf16[8,2,64,512]{3,2,1,0:T(8,128)(2,1)}, bf16[8,2,64,512]{3,2,1,0:T(8,128)(2,1)S(1)}, u32[]{:S(2)}, u32[]{:S(2)}) collective-permute-start(bf16[8,2,64,512]{3,2,1,0:T(8,128)(2,1)} %get-tuple-element.35), channel_id=1, source_target_pairs={{0,16},{8,24},{16,0},{24,8},{1,17},{9,25},{17,1},{25,9},{2,18},{10... | collective-permute-start | bytes 3145736 | tf_op jit(solution)/shard_map/ppermute | solution.py:134
  30.7 1.4 collective-permute-start.5
  32.1 30.6 %all-gather.2.cloned.1.call-done = bf16[16,128,896]{2,1,0:T(8,128)(2,1)} async-done(((bf16[2,128,896]{2,1,0:T(8,128)(2,1)}), bf16[16,128,896]{2,1,0:T(8,128)(2,1)}) %all-gather.2.cloned.1.call-update) | async-done | bytes 3670032 | tf_op jit(solution)/shard_map/all_gather | solution.py:639
  62.7 8.1 %project.1.refs_4_.refs_8_ = bf16[2048,1024]{1,0:T(8,128)(2,1)} custom-call(bf16[2048,896]{1,0:T(8,128)(2,1)} %bitcast.9, bf16[896,512]{1,0:T(8,128)(2,1)} %refs_9_.1, bf16[896,512]{1,0:T(8,128)(2,1)} %refs_10_.1), custom_call_target="tpu_custom_call" | custom-call | flops 37580963840 | bytes 7864320 | tf_op jit(solution)/shard_map/project/pallas_call | solution.py:115
  70.9 1.2 slice.29.refs_4_
  72.1 1.5 collective-permute-start
  73.6 2.1 %collective-permute-done.refs_1_ = s32[1,24]{1,0:T(1,128)S(1)} collective-permute-done((s32[1,24]{1,0:T(1,128)S(1)}, s32[1,24]{1,0:T(1,128)S(1)}, u32[]{:S(2)}, u32[]{:S(2)}) %collective-permute-start) | collective-permute-done | bytes 128 | tf_op jit(solution)/shard_map/ppermute | solution.py:134
  75.7 0.5 copy-done.17
  76.2 2.7 %slot_lists.1 = (s32[4]{0:T(128)}, s32[32]{0:T(128)}, s32[32]{0:T(128)}) custom-call(s32[1]{0:T(128)} %bitcast.me, s32[1,24]{1,0:T(1,128)} %copy-done.13, s32[1,24]{1,0:T(1,128)} %copy-done.17, s32[1,24]{1,0:T(1,128)} %copy-done.16, s32[1,24]{1,0:T(1,128)} %copy-done.15, bf16[1,8]{1,0:T(2,128)(2,1)} %slice.29.refs_4_), custom_call_target="tpu_custom_call" | custom-call | bytes 512 | tf_op jit(solution)/shard_map/slot_lists/pallas_call | solution.py:230
  79.0 0.9 copy-done.18
  79.9 0.3 copy-done.19
  80.3 14.7 %attend_local.1 = (f32[32,2,256]{2,1,0:T(2,128)}, bf16[8,64,512]{2,1,0:T(8,128)(2,1)}, bf16[8,64,512]{2,1,0:T(8,128)(2,1)}, bf16[8,64,512]{2,1,0:T(8,128)(2,1)}, bf16[8,64,512]{2,1,0:T(8,128)(2,1)}) custom-call(s32[4]{0:T(128)} %get-tuple-element.31.counts, s32[32]{0:T(128)} %get-tuple-element.32.nbrs, bf16[8,2,64,512]{3,2,1,0:T(8,128)(2,1)} %get-tuple-element.33.refs_0_, ...), custom_call_target="tpu_custom_call" | custom-call | flops 6442450944 | bytes 10485760 | tf_op jit(solution)/shard_map/attend_local/pallas_call | solution.py:414
  95.0 0.1 collective-permute-start.11
  95.1 6.0 %collective-permute-start.10 = (f32[32,2,256]{2,1,0:T(2,128)}, f32[32,2,256]{2,1,0:T(2,128)S(1)}, u32[]{:S(2)}, u32[]{:S(2)}) collective-permute-start(f32[32,2,256]{2,1,0:T(2,128)} %get-tuple-element.41.refs_4_), channel_id=1, source_target_pairs={{0,16},{8,24},{16,0},{24,8},{1,17},{9,25},{17,1},{25,9},{2,18},{10... | collective-permute-start | bytes 196616 | tf_op jit(solution)/shard_map/ppermute | solution.py:134
  101.1 2.0 %collective-permute-start.6 = (bf16[8,64,512]{2,1,0:T(8,128)(2,1)}, bf16[8,64,512]{2,1,0:T(8,128)(2,1)S(1)}, u32[]{:S(2)}, u32[]{:S(2)}) collective-permute-start(bf16[8,64,512]{2,1,0:T(8,128)(2,1)} %get-tuple-element.38), channel_id=1, source_target_pairs={{0,8},{8,0},{16,24},{24,16},{1,9},{9,1},{17,25},{25,17},{2,10},{10... | collective-permute-start | bytes 1572872 | tf_op jit(solution)/shard_map/ppermute | solution.py:134
  103.1 0.0 collective-permute-start.7
  103.2 1.5 collective-permute-start.8
  104.7 1.7 collective-permute-done.9.refs_5_
  106.4 0.6 copy-done.6
  107.0 26.4 %attend_grads.1 = (bf16[8,64,512]{2,1,0:T(8,128)(2,1)}, bf16[8,64,512]{2,1,0:T(8,128)(2,1)}, bf16[8,64,512]{2,1,0:T(8,128)(2,1)}, bf16[8,64,512]{2,1,0:T(8,128)(...) custom-call(s32[4]{0:T(128)} %get-tuple-element.31.counts, s32[32]{0:T(128)} %get-tuple-element.32.nbrs, ...), custom_call_target="tpu_custom_call" | custom-call | flops 13421772800 | bytes 18350080 | tf_op jit(solution)/shard_map/attend_grads/pallas_call | solution.py:553
  133.4 5.9 %collective-permute-start.12 = (bf16[8,64,512]{2,1,0:T(8,128)(2,1)}, bf16[8,64,512]{2,1,0:T(8,128)(2,1)S(1)}, u32[]{:S(2)}, u32[]{:S(2)}) collective-permute-start(bf16[8,64,512]{2,1,0:T(8,128)(2,1)} %get-tuple-element.44), channel_id=1, source_target_pairs={{0,8},{8,0},{16,24},{24,16},{1,9},{9,1},{17,25},{25,17},{2,10},{10... | collective-permute-start | bytes 1572872 | tf_op jit(solution)/shard_map/ppermute | solution.py:134
  139.3 1.5 collective-permute-start.14
  140.8 0.5 slice.30.refs_0_
  141.4 0.6 slice.31.refs_1_
  141.9 0.5 slice.32.refs_2_
  142.5 8.7 %grad_weights.1 = (bf16[224,1024]{1,0:T(8,128)(2,1)}, bf16[224,1024]{1,0:T(8,128)(2,1)}, bf16[224,1024]{1,0:T(8,128)(2,1)}, bf16[224,1024]{1,0:T(8,128)(2,1)}) custom-call(s32[1]{0:T(128)} %bitcast.me, bf16[2048,896]{1,0:T(8,128)(2,1)} %bitcast.10, bf16[2048,1024]{1,0:T(8,128)(2,1)} %get-tuple-element.48.dkv, bf16[1,1,8]{2,1,0:T(2,128)(2,1)} %slice.30.refs_0_, ...), custom_call_target="tpu_custom_call" | custom-call | flops 3758096384 | bytes 7864320 | tf_op jit(solution)/shard_map/grad_weights/pallas_call | solution.py:603
  151.2 1.9 %collective-permute-start.15 = (bf16[224,1024]{1,0:T(8,128)(2,1)}, bf16[224,1024]{1,0:T(8,128)(2,1)S(1)}, u32[]{:S(2)}, u32[]{:S(2)}) collective-permute-start(bf16[224,1024]{1,0:T(8,128)(2,1)} %get-tuple-element.50), channel_id=1, source_target_pairs={{0,8},{8,0},{16,24},{24,16},{1,9},{9,1},{17,25},{25,17},{2,10},{10... | collective-permute-start | bytes 1376264 | tf_op jit(solution)/shard_map/ppermute | solution.py:134
  153.2 2.6 %combine_context.1 = bf16[768,512]{1,0:T(8,128)(2,1)} custom-call(s32[24]{0:T(128)S(1)} %copy-done.8, s32[24]{0:T(128)S(1)} %copy-done.9, bf16[8,64,512]{2,1,0:T(8,128)(2,1)S(1)} %copy-done, bf16[8,64,512]{2,1,0:T(8,128)(2,1)S(1)} %collective-permute-done.6.refs_1_, bf16[8,64,512]{2,1,0:T(8,128)(2,1)S(1)} %collective-permute-done.7.refs_2_, ...), custom_call_target="tpu_custom_call" | custom-call | flops 1572864 | bytes 2883584 | tf_op jit(solution)/shard_map/combine_context/pallas_call | solution.py:312
  155.8 1.5 collective-permute-start.17
  157.3 3.2 %collective-permute-done.13.refs_2_ = bf16[8,64,512]{2,1,0:T(8,128)(2,1)S(1)} collective-permute-done((bf16[8,64,512]{2,1,0:T(8,128)(2,1)}, bf16[8,64,512]{2,1,0:T(8,128)(2,1)S(1)}, u32[]{:S(2)}, u32[]{:S(2)}) %collective-permute-start.13) | collective-permute-done | bytes 524320 | tf_op jit(solution)/shard_map/ppermute | solution.py:134
  160.5 4.5 %collective-permute-done.14.refs_3_ = bf16[8,64,512]{2,1,0:T(8,128)(2,1)S(1)} collective-permute-done((bf16[8,64,512]{2,1,0:T(8,128)(2,1)}, bf16[8,64,512]{2,1,0:T(8,128)(2,1)S(1)}, u32[]{:S(2)}, u32[]{:S(2)}) %collective-permute-start.14) | collective-permute-done | bytes 524320 | tf_op jit(solution)/shard_map/ppermute | solution.py:134
  165.0 1.8 combine_grad_queries.1
  166.8 6.6 %collective-permute-done.15 = bf16[224,1024]{1,0:T(8,128)(2,1)S(1)} collective-permute-done((bf16[224,1024]{1,0:T(8,128)(2,1)}, bf16[224,1024]{1,0:T(8,128)(2,1)S(1)}, u32[]{:S(2)}, u32[]{:S(2)}) %collective-permute-start.15) | collective-permute-done | bytes 458784 | tf_op jit(solution)/shard_map/ppermute | solution.py:134
  173.4 8.0 %collective-permute-done.16 = bf16[224,1024]{1,0:T(8,128)(2,1)S(1)} collective-permute-done((bf16[224,1024]{1,0:T(8,128)(2,1)}, bf16[224,1024]{1,0:T(8,128)(2,1)S(1)}, u32[]{:S(2)}, u32[]{:S(2)}) %collective-permute-start.16) | collective-permute-done | bytes 458784 | tf_op jit(solution)/shard_map/ppermute | solution.py:134
  181.4 0.3 convert_add_fusion
  181.7 1.0 fusion
  182.7 4.1 %reduce-scatter.2.cloned.1.call-done = bf16[2,128,896]{2,1,0:T(8,128)(2,1)} async-done(((bf16[16,128,896]{2,1,0:T(8,128)(2,1)}), bf16[2,128,896]{2,1,0:T(8,128)(2,1)}) %reduce-scatter.2.cloned.1.call-update) | async-done | bytes 458768 | tf_op jit(solution)/shard_map/reduce_scatter | solution.py:655
  (54 shorter events, 0.2 us)
Async XLA Ops:
  7.2 55.6 %all-gather.2.cloned.1.call-start = ((), (), s32[]{:S(2)}) async-start(), calls=%async_computation.1 | async-start | bytes 4128768 | tf_op jit(solution)/shard_map/all_gather | solution.py:639
  7.2 10.1 %copy-start.12 = (s32[12,2]{0,1:T(2,128)S(1)}, s32[12,2]{0,1:T(2,128)}, u32[]{:S(2)}) copy-start(s32[12,2]{0,1:T(2,128)} %param.16) | copy-start | bytes 292
  7.2 10.1 %copy-start.14 = (s32[12,2]{0,1:T(2,128)S(1)}, s32[12,2]{0,1:T(2,128)}, u32[]{:S(2)}) copy-start(s32[12,2]{0,1:T(2,128)} %param.17) | copy-start | bytes 292
  17.3 169.6 %reduce-scatter.2.cloned.1.call-start = ((), (), s32[]{:S(2)}) async-start(), calls=%async_computation.2 | async-start | bytes 4128768 | tf_op jit(solution)/shard_map/reduce_scatter | solution.py:655
  17.5 54.5 %copy-start.13 = (s32[1,24]{1,0:T(1,128)}, s32[1,24]{1,0:T(1,128)S(1)}, u32[]{:S(2)}) copy-start(s32[1,24]{1,0:T(1,128)S(1)} %reshape.31.refs_0_) | copy-start | bytes 292
  17.5 54.5 %collective-permute-start.2 = (s32[1,24]{1,0:T(1,128)S(1)}, s32[1,24]{1,0:T(1,128)S(1)}, u32[]{:S(2)}, u32[]{:S(2)}) collective-permute-start(s32[1,24]{1,0:T(1,128)S(1)} %reshape.31.refs_0_), channel_id=1, source_target_pairs={{0,24},{8,16},{16,8},{24,0},{1,25},{9,17},{17,9},{25,1},{2,26},{10... | collective-permute-start | bytes 296 | tf_op jit(solution)/shard_map/ppermute | solution.py:134
  21.5 52.1 %collective-permute-start.1 = (s32[1,24]{1,0:T(1,128)S(1)}, s32[1,24]{1,0:T(1,128)S(1)}, u32[]{:S(2)}, u32[]{:S(2)}) collective-permute-start(s32[1,24]{1,0:T(1,128)S(1)} %reshape.31.refs_0_), channel_id=1, source_target_pairs={{0,16},{8,24},{16,0},{24,8},{1,17},{9,25},{17,1},{25,9},{2,18},{10... | collective-permute-start | bytes 296 | tf_op jit(solution)/shard_map/ppermute | solution.py:134
  28.6 50.4 %collective-permute-start.3 = (bf16[8,2,64,512]{3,2,1,0:T(8,128)(2,1)}, bf16[8,2,64,512]{3,2,1,0:T(8,128)(2,1)S(1)}, u32[]{:S(2)}, u32[]{:S(2)}) collective-permute-start(bf16[8,2,64,512]{3,2,1,0:T(8,128)(2,1)} %get-tuple-element.34), channel_id=1, source_target_pairs={{0,8},{8,0},{16,24},{24,16},{1,9},{9,1},{17,25},{25,17},{2,10},{10... | collective-permute-start | bytes 3145736 | tf_op jit(solution)/shard_map/ppermute | solution.py:134
  28.7 50.3 %collective-permute-start.4 = (bf16[8,2,64,512]{3,2,1,0:T(8,128)(2,1)}, bf16[8,2,64,512]{3,2,1,0:T(8,128)(2,1)S(1)}, u32[]{:S(2)}, u32[]{:S(2)}) collective-permute-start(bf16[8,2,64,512]{3,2,1,0:T(8,128)(2,1)} %get-tuple-element.35), channel_id=1, source_target_pairs={{0,16},{8,24},{16,0},{24,8},{1,17},{9,25},{17,1},{25,9},{2,18},{10... | collective-permute-start | bytes 3145736 | tf_op jit(solution)/shard_map/ppermute | solution.py:134
  30.7 48.3 %collective-permute-start.5 = (bf16[8,2,64,512]{3,2,1,0:T(8,128)(2,1)}, bf16[8,2,64,512]{3,2,1,0:T(8,128)(2,1)}, u32[]{:S(2)}, u32[]{:S(2)}) collective-permute-start(bf16[8,2,64,512]{3,2,1,0:T(8,128)(2,1)} %get-tuple-element.36), channel_id=1, source_target_pairs={{0,24},{8,16},{16,8},{24,0},{1,25},{9,17},{17,9},{25,1},{2,26},{10... | collective-permute-start | bytes 3145736 | tf_op jit(solution)/shard_map/ppermute | solution.py:134
  72.0 3.6 %copy-start.15 = (s32[1,24]{1,0:T(1,128)}, s32[1,24]{1,0:T(1,128)S(1)}, u32[]{:S(2)}) copy-start(s32[1,24]{1,0:T(1,128)S(1)} %collective-permute-done.2.refs_3_) | copy-start | bytes 292
  72.1 3.6 %collective-permute-start = (s32[1,24]{1,0:T(1,128)S(1)}, s32[1,24]{1,0:T(1,128)S(1)}, u32[]{:S(2)}, u32[]{:S(2)}) collective-permute-start(s32[1,24]{1,0:T(1,128)S(1)} %reshape.31.refs_0_), channel_id=1, source_target_pairs={{0,8},{8,0},{16,24},{24,16},{1,9},{9,1},{17,25},{25,17},{2,10},{10... | collective-permute-start | bytes 296 | tf_op jit(solution)/shard_map/ppermute | solution.py:134
  73.6 2.1 %copy-start.16 = (s32[1,24]{1,0:T(1,128)}, s32[1,24]{1,0:T(1,128)S(1)}, u32[]{:S(2)}) copy-start(s32[1,24]{1,0:T(1,128)S(1)} %collective-permute-done.1.refs_2_) | copy-start | bytes 292
  75.7 0.5 copy-start.17
  78.9 1.0 copy-start.18
  79.0 1.3 copy-start.19
  95.0 8.2 %collective-permute-start.11 = (f32[32,2,256]{2,1,0:T(2,128)}, f32[32,2,256]{2,1,0:T(2,128)S(1)}, u32[]{:S(2)}, u32[]{:S(2)}) collective-permute-start(f32[32,2,256]{2,1,0:T(2,128)} %get-tuple-element.41.refs_4_), channel_id=1, source_target_pairs={{0,24},{8,16},{16,8},{24,0},{1,25},{9,17},{17,9},{25,1},{2,26},{10... | collective-permute-start | bytes 196616 | tf_op jit(solution)/shard_map/ppermute | solution.py:134
  95.1 9.6 %collective-permute-start.10 = (f32[32,2,256]{2,1,0:T(2,128)}, f32[32,2,256]{2,1,0:T(2,128)S(1)}, u32[]{:S(2)}, u32[]{:S(2)}) collective-permute-start(f32[32,2,256]{2,1,0:T(2,128)} %get-tuple-element.41.refs_4_), channel_id=1, source_target_pairs={{0,16},{8,24},{16,0},{24,8},{1,17},{9,25},{17,1},{25,9},{2,18},{10... | collective-permute-start | bytes 196616 | tf_op jit(solution)/shard_map/ppermute | solution.py:134
  101.1 5.2 %collective-permute-start.9 = (f32[32,2,256]{2,1,0:T(2,128)}, f32[32,2,256]{2,1,0:T(2,128)S(1)}, u32[]{:S(2)}, u32[]{:S(2)}) collective-permute-start(f32[32,2,256]{2,1,0:T(2,128)} %get-tuple-element.41.refs_4_), channel_id=1, source_target_pairs={{0,8},{8,0},{16,24},{24,16},{1,9},{9,1},{17,25},{25,17},{2,10},{10... | collective-permute-start | bytes 196616 | tf_op jit(solution)/shard_map/ppermute | solution.py:134
  101.1 38.2 %collective-permute-start.6 = (bf16[8,64,512]{2,1,0:T(8,128)(2,1)}, bf16[8,64,512]{2,1,0:T(8,128)(2,1)S(1)}, u32[]{:S(2)}, u32[]{:S(2)}) collective-permute-start(bf16[8,64,512]{2,1,0:T(8,128)(2,1)} %get-tuple-element.38), channel_id=1, source_target_pairs={{0,8},{8,0},{16,24},{24,16},{1,9},{9,1},{17,25},{25,17},{2,10},{10... | collective-permute-start | bytes 1572872 | tf_op jit(solution)/shard_map/ppermute | solution.py:134
  103.1 38.2 %collective-permute-start.7 = (bf16[8,64,512]{2,1,0:T(8,128)(2,1)}, bf16[8,64,512]{2,1,0:T(8,128)(2,1)S(1)}, u32[]{:S(2)}, u32[]{:S(2)}) collective-permute-start(bf16[8,64,512]{2,1,0:T(8,128)(2,1)} %get-tuple-element.39), channel_id=1, source_target_pairs={{0,16},{8,24},{16,0},{24,8},{1,17},{9,25},{17,1},{25,9},{2,18},{10... | collective-permute-start | bytes 1572872 | tf_op jit(solution)/shard_map/ppermute | solution.py:134
  103.2 3.2 %copy-start.2 = (f32[32,2,256]{2,1,0:T(2,128)}, f32[32,2,256]{2,1,0:T(2,128)S(1)}, u32[]{:S(2)}) copy-start(f32[32,2,256]{2,1,0:T(2,128)S(1)} %collective-permute-done.11.refs_7_) | copy-start | bytes 196612
  103.2 38.8 %collective-permute-start.8 = (bf16[8,64,512]{2,1,0:T(8,128)(2,1)}, bf16[8,64,512]{2,1,0:T(8,128)(2,1)S(1)}, u32[]{:S(2)}, u32[]{:S(2)}) collective-permute-start(bf16[8,64,512]{2,1,0:T(8,128)(2,1)} %get-tuple-element.40), channel_id=1, source_target_pairs={{0,24},{8,16},{16,8},{24,0},{1,25},{9,17},{17,9},{25,1},{2,26},{10... | collective-permute-start | bytes 1572872 | tf_op jit(solution)/shard_map/ppermute | solution.py:134
  104.7 1.7 copy-start.4
  106.4 0.6 copy-start.6
  133.4 22.4 %collective-permute-start.12 = (bf16[8,64,512]{2,1,0:T(8,128)(2,1)}, bf16[8,64,512]{2,1,0:T(8,128)(2,1)S(1)}, u32[]{:S(2)}, u32[]{:S(2)}) collective-permute-start(bf16[8,64,512]{2,1,0:T(8,128)(2,1)} %get-tuple-element.44), channel_id=1, source_target_pairs={{0,8},{8,0},{16,24},{24,16},{1,9},{9,1},{17,25},{25,17},{2,10},{10... | collective-permute-start | bytes 1572872 | tf_op jit(solution)/shard_map/ppermute | solution.py:134
  139.3 21.2 %collective-permute-start.13 = (bf16[8,64,512]{2,1,0:T(8,128)(2,1)}, bf16[8,64,512]{2,1,0:T(8,128)(2,1)S(1)}, u32[]{:S(2)}, u32[]{:S(2)}) collective-permute-start(bf16[8,64,512]{2,1,0:T(8,128)(2,1)} %get-tuple-element.45), channel_id=1, source_target_pairs={{0,16},{8,24},{16,0},{24,8},{1,17},{9,25},{17,1},{25,9},{2,18},{10... | collective-permute-start | bytes 1572872 | tf_op jit(solution)/shard_map/ppermute | solution.py:134
  139.3 25.7 %collective-permute-start.14 = (bf16[8,64,512]{2,1,0:T(8,128)(2,1)}, bf16[8,64,512]{2,1,0:T(8,128)(2,1)S(1)}, u32[]{:S(2)}, u32[]{:S(2)}) collective-permute-start(bf16[8,64,512]{2,1,0:T(8,128)(2,1)} %get-tuple-element.46), channel_id=1, source_target_pairs={{0,24},{8,16},{16,8},{24,0},{1,25},{9,17},{17,9},{25,1},{2,26},{10... | collective-permute-start | bytes 1572872 | tf_op jit(solution)/shard_map/ppermute | solution.py:134
  142.5 10.7 %copy-start = (bf16[8,64,512]{2,1,0:T(8,128)(2,1)S(1)}, bf16[8,64,512]{2,1,0:T(8,128)(2,1)}, u32[]{:S(2)}) copy-start(bf16[8,64,512]{2,1,0:T(8,128)(2,1)} %get-tuple-element.37.refs_0_) | copy-start | bytes 1572868
  142.5 10.7 %copy-start.1 = (f32[32,2,256]{2,1,0:T(2,128)S(1)}, f32[32,2,256]{2,1,0:T(2,128)}, u32[]{:S(2)}) copy-start(f32[32,2,256]{2,1,0:T(2,128)} %get-tuple-element.41.refs_4_) | copy-start | bytes 196612
  142.5 10.7 %copy-start.3 = (f32[32,2,256]{2,1,0:T(2,128)S(1)}, f32[32,2,256]{2,1,0:T(2,128)}, u32[]{:S(2)}) copy-start(f32[32,2,256]{2,1,0:T(2,128)} %copy-done.2) | copy-start | bytes 196612
  142.5 10.7 %copy-start.5 = (f32[32,2,256]{2,1,0:T(2,128)S(1)}, f32[32,2,256]{2,1,0:T(2,128)}, u32[]{:S(2)}) copy-start(f32[32,2,256]{2,1,0:T(2,128)} %copy-done.4) | copy-start | bytes 196612
  142.5 10.7 %copy-start.7 = (f32[32,2,256]{2,1,0:T(2,128)S(1)}, f32[32,2,256]{2,1,0:T(2,128)}, u32[]{:S(2)}) copy-start(f32[32,2,256]{2,1,0:T(2,128)} %copy-done.6) | copy-start | bytes 196612
  142.5 10.7 %copy-start.8 = (s32[24]{0:T(128)S(1)}, s32[24]{0:T(128)}, u32[]{:S(2)}) copy-start(s32[24]{0:T(128)} %get-tuple-element.29.position) | copy-start | bytes 292
  142.5 10.7 %copy-start.9 = (s32[24]{0:T(128)S(1)}, s32[24]{0:T(128)}, u32[]{:S(2)}) copy-start(s32[24]{0:T(128)} %get-tuple-element.30.place) | copy-start | bytes 292
  142.5 22.5 %copy-start.10 = (bf16[8,64,512]{2,1,0:T(8,128)(2,1)S(1)}, bf16[8,64,512]{2,1,0:T(8,128)(2,1)}, u32[]{:S(2)}) copy-start(bf16[8,64,512]{2,1,0:T(8,128)(2,1)} %get-tuple-element.43.refs_0_) | copy-start | bytes 1572868
  151.2 22.3 %collective-permute-start.15 = (bf16[224,1024]{1,0:T(8,128)(2,1)}, bf16[224,1024]{1,0:T(8,128)(2,1)S(1)}, u32[]{:S(2)}, u32[]{:S(2)}) collective-permute-start(bf16[224,1024]{1,0:T(8,128)(2,1)} %get-tuple-element.50), channel_id=1, source_target_pairs={{0,8},{8,0},{16,24},{24,16},{1,9},{9,1},{17,25},{25,17},{2,10},{10... | collective-permute-start | bytes 1376264 | tf_op jit(solution)/shard_map/ppermute | solution.py:134
  153.1 28.3 %collective-permute-start.16 = (bf16[224,1024]{1,0:T(8,128)(2,1)}, bf16[224,1024]{1,0:T(8,128)(2,1)S(1)}, u32[]{:S(2)}, u32[]{:S(2)}) collective-permute-start(bf16[224,1024]{1,0:T(8,128)(2,1)} %get-tuple-element.51), channel_id=1, source_target_pairs={{0,16},{8,24},{16,0},{24,8},{1,17},{9,25},{17,1},{25,9},{2,18},{10... | collective-permute-start | bytes 1376264 | tf_op jit(solution)/shard_map/ppermute | solution.py:134
  155.8 25.6 %collective-permute-start.17 = (bf16[224,1024]{1,0:T(8,128)(2,1)}, bf16[224,1024]{1,0:T(8,128)(2,1)S(1)}, u32[]{:S(2)}, u32[]{:S(2)}) collective-permute-start(bf16[224,1024]{1,0:T(8,128)(2,1)} %get-tuple-element.52), channel_id=1, source_target_pairs={{0,24},{8,16},{16,8},{24,0},{1,25},{9,17},{17,9},{25,1},{2,26},{10... | collective-permute-start | bytes 1376264 | tf_op jit(solution)/shard_map/ppermute | solution.py:134
  165.0 16.4 %copy-start.11 = (bf16[224,1024]{1,0:T(8,128)(2,1)S(1)}, bf16[224,1024]{1,0:T(8,128)(2,1)}, u32[]{:S(2)}) copy-start(bf16[224,1024]{1,0:T(8,128)(2,1)} %get-tuple-element.49) | copy-start | bytes 1376260
Sparse Core Ops, SparseCore 0:
  17.4 45.2 all-gather.1
  141.0 45.8 reduce-scatter.1

commit v3 on v2

--- a/solution.py
+++ b/solution.py
@@ -9,6 +9,9 @@
 from jax.sharding import PartitionSpec as P
 
 HD = 128
+UNROLL = 4
+TAIL_FLOPS = 32000000000
+WEIGHT_FLOPS = 70000000000
 NT = (((1,), (1,)), ((), ()))
 NN = (((1,), (0,)), ((), ()))
 TN = (((0,), (0,)), ((), ()))
@@ -123,7 +126,7 @@
         ],
         out_specs=pl.BlockSpec((block, 2 * width), lambda i: (i, 0)),
         compiler_params=params(59),
-        cost_estimate=cost(40 * rows * feat * width, rows * (feat + 2 * width) * 2),
+        cost_estimate=cost(8 * rows * feat * width, rows * (feat + 2 * width) * 2),
         name="project",
     )(table, key_weight, value_weight)
 
@@ -148,7 +151,7 @@
 
     def step(i, carry):
         span = i // 2
-        offset = jnp.bitwise_xor(group_ids[span, i % 2], me[0])
+        offset = jnp.bitwise_xor(group_ids[i % 2, span], me[0])
         rank = taken[offset]
         taken[offset] = rank + 1
         position[i] = offset * capacity + rank
@@ -185,16 +188,9 @@
     return outs[:groups], outs[groups], outs[groups + 1]
 
 
-def slots_kernel(groups, waits, capacity, table_len, me, *refs):
+def slots_kernel(groups, waits, capacity, slot_bits, me, *refs):
     codes, (counts, nbrs, partner, taken) = refs[:groups], refs[groups + waits :]
     slots = groups * capacity
-
-    def clear(j, carry):
-        nbrs[j] = 0
-        partner[j] = 0
-        return carry
-
-    lax.fori_loop(0, slots, clear, 0)
     for d in range(groups):
         source = jnp.bitwise_xor(me[0], d)
         for h in range(groups):
@@ -204,11 +200,11 @@
             both = []
             for i in range(2):
                 code = codes[d][0, 2 * span + i]
-                target = code // table_len
+                target = jnp.right_shift(code, slot_bits)
                 rank = taken[target]
                 taken[target] = rank + 1
                 there = jnp.bitwise_xor(target, source) * capacity + rank
-                both.append((target, rank, code % table_len, there))
+                both.append((target, rank, jnp.bitwise_and(code, (1 << slot_bits) - 1), there))
             for i in range(2):
                 target, rank, nbr, _ = both[i]
                 other, _, _, there = both[1 - i]
@@ -224,11 +220,11 @@
         counts[d] = taken[me[0]]
 
 
-def slot_lists(me, codes, capacity, table_len, waits):
+def slot_lists(me, codes, capacity, slot_bits, waits):
     groups = len(codes)
     slots = groups * capacity
     return pl.pallas_call(
-        functools.partial(slots_kernel, groups, len(waits), capacity, table_len),
+        functools.partial(slots_kernel, groups, len(waits), capacity, slot_bits),
         out_shape=[
             jax.ShapeDtypeStruct((groups,), jnp.int32),
             jax.ShapeDtypeStruct((slots,), jnp.int32),
@@ -273,7 +269,7 @@
         out_specs=vmem(),
         scratch_shapes=[pltpu.VMEM((groups * capacity, span_len, width), BF16)],
         compiler_params=params(16),
-        cost_estimate=cost(rows * width * 250000, groups * pieces[0].size * 2 + rows * width * 2),
+        cost_estimate=cost(TAIL_FLOPS, groups * pieces[0].size * 2 + rows * width * 2),
         name="combine_grad_queries",
     )(position, *pieces, *waits)
 
@@ -373,8 +369,8 @@
         arrival(qg, d, isem).wait()
 
         def step(i, carry):
-            for u in range(2):
-                k = jnp.minimum(2 * i + u, counts[d] - 1)
+            for u in range(UNROLL):
+                k = jnp.minimum(UNROLL * i + u, counts[d] - 1)
                 j = d * capacity + k
                 q_diag, g_diag = diag[2 * u], diag[2 * u + 1]
                 fill_diagonal(q_diag, qg[d, k, 0], heads, span_len)
@@ -392,7 +388,7 @@
                     store_pair(ctx.at[d], k, p, mm(probs.astype(BF16).T, values, NN), span_len)
             return carry
 
-        lax.fori_loop(0, (counts[d] + 1) // 2, step, 0)
+        lax.fori_loop(0, (counts[d] + UNROLL - 1) // UNROLL, step, 0)
         for e in range(groups):
 
             @pl.when(d == e)
@@ -425,7 +421,7 @@
             pltpu.SemaphoreType.DMA((groups,)),
             pltpu.SemaphoreType.DMA((groups,)),
         ]
-        + [pltpu.VMEM((lanes, 2 * HD), BF16)] * 4,
+        + [pltpu.VMEM((lanes, 2 * HD), BF16)] * (2 * UNROLL),
         compiler_params=params(56),
         cost_estimate=cost(
             slots * 48 * row_len * lanes * HD,
@@ -472,8 +468,8 @@
         arrival(qg, d, qsem).wait()
 
         def step(i, carry):
-            for u in range(2):
-                place = 2 * i + u
+            for u in range(UNROLL):
+                place = UNROLL * i + u
                 live = place < counts[d]
                 k = jnp.minimum(place, counts[d] - 1)
                 j = d * capacity + k
@@ -499,7 +495,7 @@
                     acc[rows, vcols] += mm(weights, g_diag[lanes, :], NN)
             return carry
 
-        lax.fori_loop(0, (counts[d] + 1) // 2, step, 0)
+        lax.fori_loop(0, (counts[d] + UNROLL - 1) // UNROLL, step, 0)
         for e in range(groups):
 
             @pl.when(d == e)
@@ -575,7 +571,7 @@
             pltpu.SemaphoreType.DMA((groups,)),
             pltpu.SemaphoreType.DMA((max(1, rows // 256), 2)),
         ]
-        + [pltpu.VMEM((lanes, 2 * HD), BF16)] * 4,
+        + [pltpu.VMEM((lanes, 2 * HD), BF16)] * (2 * UNROLL),
         compiler_params=params(56),
         cost_estimate=cost(
             4 * rows * feat * width + slots * 72 * row_len * lanes * HD,
@@ -607,7 +603,7 @@
         out_specs=[vmem()] * groups,
         scratch_shapes=[pltpu.VMEM((groups, feat // groups, columns), BF16)],
         compiler_params=params(56),
-        cost_estimate=cost(table.size * columns * 2, table.size * 2 + grad_kv.size * 2),
+        cost_estimate=cost(WEIGHT_FLOPS, table.size * 2 + grad_kv.size * 2),
         name="grad_weights",
     )(me, table, grad_kv, *waits)
 
@@ -638,14 +634,15 @@
     encoded_own = encode(neighbours, up_weight, down_weight)
     table = lax.all_gather(encoded_own, "ret", axis=0, tiled=True).reshape(-1, feat)
     outgoing, position, place = dispatch(
-        me, group_ids, queries, grad_ctx, groups, capacity, span_len, signs_of(encoded_own)
+        me, group_ids.T, queries, grad_ctx, groups, capacity, span_len, [encoded_own]
     )
     arrived = exchange(outgoing, "seq")
     kv = project(table, key_weight, value_weight)
 
-    codes = (group_ids * table_len + slot_ids).reshape(1, -1)
+    slot_bits = (table_len - 1).bit_length()
+    codes = (group_ids * (1 << slot_bits) + slot_ids).reshape(1, -1)
     codes = exchange([codes] * groups, "seq")
-    counts, nbrs, partner = slot_lists(me, codes, capacity, table_len, signs_of(kv))
+    counts, nbrs, partner = slot_lists(me, codes, capacity, slot_bits, [kv])
     own_stats, local_ctx = attend_local(counts, nbrs, arrived, kv, row_len, scale)
     stats = exchange([own_stats] * groups, "seq")
     ctx_back = exchange(local_ctx, "seq")

time: 194 us -> 187 us (0.964)
  Pallas kernels: 79.7 us -> 69.8 us
  starting transfers between devices: 30.3 us -> 37.7 us
  local copies, waits for them, and re-layouts: 8.33 us -> 5.27 us
    ppermute x18, starting transfers between devices: 30.2 us -> 37.7 us  [exchange(): lax.ppermute(pieces[d], axis, [(s, s ^ d) for s in range(size)])]
    pallas_call x1, Pallas kernels: 26.4 us -> 20.9 us  [attend_grads(): pl.pallas_call(functools.partial(grads_kernel, groups, row_len, scale), o...]
    pallas_call x1, Pallas kernels: 14.7 us -> 10.9 us  [attend_local(): pl.pallas_call(functools.partial(local_kernel, groups, row_len, scale), o...]
    slice x5 -> x3, local copies, waits for them, and re-layouts: 4 us -> 1.62 us  [signs_of(): lax.slice(a, (0,) * a.ndim, (1,) * (a.ndim - 1) + (8,))]
    reduce_scatter x1, waiting for transfers between devices: 4.13 us -> 1.95 us  [body(): lax.psum_scatter(grad_table.reshape(table_len, row_len, feat), 'ret', sca...]
    all_gather x1, waiting for transfers between devices: 30.6 us -> 32.6 us  [body(): lax.all_gather(encoded_own, 'ret', axis=0, tiled=True).reshape(-1, feat)]
  transfers between devices with their start and end apart: 20 -> 20, of which waited for: 8 -> 10; matrix products, arithmetic and copies ran while one was open for 3% -> 2% of each run, Pallas kernels for 28% -> 26%
where the time goes in v3:
time: 187 us
  Pallas kernels  69.8 us (37%)
  waiting for transfers between devices  59.4 us (32%)
  starting transfers between devices  37.7 us (20%)
  between operations  14.3 us (8%)
  local copies, waits for them, and re-layouts  5.27 us (3%)
    ppermute x18, starting transfers between devices, exchange(): lax.ppermute(pieces[d], axis, [(s, s ^ d) for s in range(size)])  37.7 us
    all_gather x1, waiting for transfers between devices, body(): lax.all_gather(encoded_own, 'ret', axis=0, tiled=True).reshape(-1, feat)  32.6 us
    ppermute x18, waiting for transfers between devices, exchange(): lax.ppermute(pieces[d], axis, [(s, s ^ d) for s in range(size)])  24.9 us
    pallas_call x1, Pallas kernels, attend_grads(): pl.pallas_call(functools.partial(grads_kernel, groups, row_len, scale), o...  20.9 us
    pallas_call x1, Pallas kernels, attend_local(): pl.pallas_call(functools.partial(local_kernel, groups, row_len, scale), o...  10.9 us
    pallas_call x1, Pallas kernels, encode(): pl.pallas_call(encode_kernel, out_shape=jax.ShapeDtypeStruct(rows.shape,...  10 us
    pallas_call x1, Pallas kernels, grad_weights(): pl.pallas_call(functools.partial(weight_kernel, groups, len(waits)), out_...  9.01 us
    pallas_call x1, Pallas kernels, project(): pl.pallas_call(project_kernel, grid=(rows // block,), out_shape=jax.Shape...  8.13 us
  transfers between devices with their start and end apart: 20, of which 10 were waited for; matrix products, arithmetic and copies ran while one was open for 2% of the time, Pallas kernels for 26%

profile of v3, /device:TPU:0, one launch (start us, length us, event | category | flops | bytes accessed | tf_op | source)
XLA Modules:
  0.0 186.8 jit_solution(13220392519225284385)
XLA Ops:
  7.2 0.0 all-gather.2.cloned.1.call-start
  7.2 10.0 %encode.1 = bf16[256,896]{1,0:T(8,128)(2,1)} custom-call(bf16[256,896]{1,0:T(8,128)(2,1)} %bitcast.9, bf16[896,3584]{1,0:T(8,128)(2,1)} %up_ref.1, bf16[3584,896]{1,0:T(8,128)(2,1)} %down_ref.1), custom_call_target="tpu_custom_call" | custom-call | flops 3288334336 | bytes 12845056 | tf_op jit(solution)/shard_map/encode/pallas_call | solution.py:89
  17.3 0.0 reduce-scatter.2.cloned.1.call-start
  17.3 4.6 %dispatch.1 = (bf16[8,2,64,512]{3,2,1,0:T(8,128)(2,1)}, bf16[8,2,64,512]{3,2,1,0:T(8,128)(2,1)}, bf16[8,2,64,512]{3,2,1,0:T(8,128)(2,1)}, bf16[8,2,64,512]{3,2,1,0:T(8,128)(2,1)}, s32[24]{0:T(128)}, /*index=5*/s32[24]{0:T(128)}) custom-call(s32[1]{0:T(128)} %bitcast.me, s32[2,12]{1,0:T(2,128)} %bitcast.10, bf16[768,512]{1,0:T(8,128)(2,1)} %q_ref.1, ...), custom_call_target="tpu_custom_call" | custom-call | bytes 6291456 | tf_op jit(solution)/shard_map/dispatch/pallas_call | solution.py:173
  21.9 3.0 %collective-permute-start.3 = (bf16[8,2,64,512]{3,2,1,0:T(8,128)(2,1)}, bf16[8,2,64,512]{3,2,1,0:T(8,128)(2,1)S(1)}, u32[]{:S(2)}, u32[]{:S(2)}) collective-permute-start(bf16[8,2,64,512]{3,2,1,0:T(8,128)(2,1)} %get-tuple-element.34), channel_id=1, source_target_pairs={{0,8},{8,0},{16,24},{24,16},{1,9},{9,1},{17,25},{25,17},{2,10},{10... | collective-permute-start | bytes 3145736 | tf_op jit(solution)/shard_map/ppermute | solution.py:137
  24.9 1.5 collective-permute-start.4
  26.5 0.1 copy.16
  26.6 0.1 reshape.31.refs_0_
  26.7 3.0 %collective-permute-start.2 = (s32[1,24]{1,0:T(1,128)S(1)}, s32[1,24]{1,0:T(1,128)S(1)}, u32[]{:S(2)}, u32[]{:S(2)}) collective-permute-start(s32[1,24]{1,0:T(1,128)S(1)} %reshape.31.refs_0_), channel_id=1, source_target_pairs={{0,24},{8,16},{16,8},{24,0},{1,25},{9,17},{17,9},{25,1},{2,26},{10... | collective-permute-start | bytes 296 | tf_op jit(solution)/shard_map/ppermute | solution.py:137
  29.7 0.5 collective-permute-start.1
  30.2 32.6 %all-gather.2.cloned.1.call-done = bf16[16,128,896]{2,1,0:T(8,128)(2,1)} async-done(((bf16[2,128,896]{2,1,0:T(8,128)(2,1)}), bf16[16,128,896]{2,1,0:T(8,128)(2,1)}) %all-gather.2.cloned.1.call-update) | async-done | bytes 3670032 | tf_op jit(solution)/shard_map/all_gather | solution.py:635
  62.7 8.1 %project.1.refs_4_.refs_8_ = bf16[2048,1024]{1,0:T(8,128)(2,1)} custom-call(bf16[2048,896]{1,0:T(8,128)(2,1)} %bitcast.11, bf16[896,512]{1,0:T(8,128)(2,1)} %refs_9_.1, bf16[896,512]{1,0:T(8,128)(2,1)} %refs_10_.1), custom_call_target="tpu_custom_call" | custom-call | flops 7516192768 | bytes 7864320 | tf_op jit(solution)/shard_map/project/pallas_call | solution.py:118
  70.9 1.3 collective-permute-done.2.refs_3_
  72.2 1.4 collective-permute-start
  73.6 2.1 %collective-permute-done.refs_1_ = s32[1,24]{1,0:T(1,128)S(1)} collective-permute-done((s32[1,24]{1,0:T(1,128)S(1)}, s32[1,24]{1,0:T(1,128)S(1)}, u32[]{:S(2)}, u32[]{:S(2)}) %collective-permute-start) | collective-permute-done | bytes 128 | tf_op jit(solution)/shard_map/ppermute | solution.py:137
  75.7 0.5 copy-done.17
  76.3 1.9 %slot_lists.1 = (s32[4]{0:T(128)}, s32[32]{0:T(128)}, s32[32]{0:T(128)}) custom-call(s32[1]{0:T(128)} %bitcast.me, s32[1,24]{1,0:T(1,128)} %copy-done.13, s32[1,24]{1,0:T(1,128)} %copy-done.17, s32[1,24]{1,0:T(1,128)} %copy-done.16, s32[1,24]{1,0:T(1,128)} %copy-done.15, bf16[2048,1024]{1,0:T(8,128)(2,1)} %project.1.refs_4_.refs_8_), custom_call_target="tpu_custom_call" | custom-call | bytes 512 | tf_op jit(solution)/shard_map/slot_lists/pallas_call | solution.py:226
  78.3 0.9 copy-done.18
  79.2 0.3 copy-done.19
  79.5 10.9 %attend_local.1 = (f32[32,2,256]{2,1,0:T(2,128)}, bf16[8,64,512]{2,1,0:T(8,128)(2,1)}, bf16[8,64,512]{2,1,0:T(8,128)(2,1)}, bf16[8,64,512]{2,1,0:T(8,128)(2,1)}, bf16[8,64,512]{2,1,0:T(8,128)(2,1)}) custom-call(s32[4]{0:T(128)} %get-tuple-element.31.counts, s32[32]{0:T(128)} %get-tuple-element.32.nbrs, bf16[8,2,64,512]{3,2,1,0:T(8,128)(2,1)} %get-tuple-element.33.refs_0_, ...), custom_call_target="tpu_custom_call" | custom-call | flops 6442450944 | bytes 10485760 | tf_op jit(solution)/shard_map/attend_local/pallas_call | solution.py:410
  90.4 7.0 %collective-permute-start.11 = (f32[32,2,256]{2,1,0:T(2,128)}, f32[32,2,256]{2,1,0:T(2,128)S(1)}, u32[]{:S(2)}, u32[]{:S(2)}) collective-permute-start(f32[32,2,256]{2,1,0:T(2,128)} %get-tuple-element.41.refs_4_), channel_id=1, source_target_pairs={{0,24},{8,16},{16,8},{24,0},{1,25},{9,17},{17,9},{25,1},{2,26},{10... | collective-permute-start | bytes 196616 | tf_op jit(solution)/shard_map/ppermute | solution.py:137
  97.4 1.4 collective-permute-start.10
  98.8 2.0 %collective-permute-start.6 = (bf16[8,64,512]{2,1,0:T(8,128)(2,1)}, bf16[8,64,512]{2,1,0:T(8,128)(2,1)S(1)}, u32[]{:S(2)}, u32[]{:S(2)}) collective-permute-start(bf16[8,64,512]{2,1,0:T(8,128)(2,1)} %get-tuple-element.38), channel_id=1, source_target_pairs={{0,8},{8,0},{16,24},{24,16},{1,9},{9,1},{17,25},{25,17},{2,10},{10... | collective-permute-start | bytes 1572872 | tf_op jit(solution)/shard_map/ppermute | solution.py:137
  100.8 0.6 collective-permute-start.7
  101.5 1.9 %collective-permute-start.8 = (bf16[8,64,512]{2,1,0:T(8,128)(2,1)}, bf16[8,64,512]{2,1,0:T(8,128)(2,1)S(1)}, u32[]{:S(2)}, u32[]{:S(2)}) collective-permute-start(bf16[8,64,512]{2,1,0:T(8,128)(2,1)} %get-tuple-element.40), channel_id=1, source_target_pairs={{0,24},{8,16},{16,8},{24,0},{1,25},{9,17},{17,9},{25,1},{2,26},{10... | collective-permute-start | bytes 1572872 | tf_op jit(solution)/shard_map/ppermute | solution.py:137
  103.4 0.6 collective-permute-done.9.refs_5_
  104.1 0.6 copy-done.6
  104.7 20.9 %attend_grads.1 = (bf16[8,64,512]{2,1,0:T(8,128)(2,1)}, bf16[8,64,512]{2,1,0:T(8,128)(2,1)}, bf16[8,64,512]{2,1,0:T(8,128)(2,1)}, bf16[8,64,512]{2,1,0:T(8,128)(...) custom-call(s32[4]{0:T(128)} %get-tuple-element.31.counts, s32[32]{0:T(128)} %get-tuple-element.32.nbrs, ...), custom_call_target="tpu_custom_call" | custom-call | flops 13421772800 | bytes 18350080 | tf_op jit(solution)/shard_map/attend_grads/pallas_call | solution.py:549
  125.6 9.8 %collective-permute-start.12 = (bf16[8,64,512]{2,1,0:T(8,128)(2,1)}, bf16[8,64,512]{2,1,0:T(8,128)(2,1)S(1)}, u32[]{:S(2)}, u32[]{:S(2)}) collective-permute-start(bf16[8,64,512]{2,1,0:T(8,128)(2,1)} %get-tuple-element.44), channel_id=1, source_target_pairs={{0,8},{8,0},{16,24},{24,16},{1,9},{9,1},{17,25},{25,17},{2,10},{10... | collective-permute-start | bytes 1572872 | tf_op jit(solution)/shard_map/ppermute | solution.py:137
  135.4 0.9 collective-permute-start.13
  136.4 1.0 collective-permute-start.14
  137.4 0.5 slice.20.refs_0_
  137.9 0.6 slice.21.refs_1_
  138.5 0.5 slice.22.refs_2_
  139.0 9.0 %grad_weights.1 = (bf16[224,1024]{1,0:T(8,128)(2,1)}, bf16[224,1024]{1,0:T(8,128)(2,1)}, bf16[224,1024]{1,0:T(8,128)(2,1)}, bf16[224,1024]{1,0:T(8,128)(2,1)}) custom-call(s32[1]{0:T(128)} %bitcast.me, bf16[2048,896]{1,0:T(8,128)(2,1)} %bitcast.12, bf16[2048,1024]{1,0:T(8,128)(2,1)} %get-tuple-element.48.dkv, bf16[1,1,8]{2,1,0:T(2,128)(2,1)} %slice.20.refs_0_, ...), custom_call_target="tpu_custom_call" | custom-call | flops 70000001024 | bytes 7864320 | tf_op jit(solution)/shard_map/grad_weights/pallas_call | solution.py:599
  148.0 1.6 collective-permute-start.15
  149.6 0.9 collective-permute-start.16
  150.6 2.6 %combine_context.1 = bf16[768,512]{1,0:T(8,128)(2,1)} custom-call(s32[24]{0:T(128)S(1)} %copy-done.8, s32[24]{0:T(128)S(1)} %copy-done.9, bf16[8,64,512]{2,1,0:T(8,128)(2,1)S(1)} %copy-done, bf16[8,64,512]{2,1,0:T(8,128)(2,1)S(1)} %collective-permute-done.6.refs_1_, bf16[8,64,512]{2,1,0:T(8,128)(2,1)S(1)} %collective-permute-done.7.refs_2_, ...), custom_call_target="tpu_custom_call" | custom-call | flops 1572864 | bytes 2883584 | tf_op jit(solution)/shard_map/combine_context/pallas_call | solution.py:308
  153.1 1.0 collective-permute-start.17
  154.2 1.7 collective-permute-done.13.refs_2_
  155.9 5.8 %collective-permute-done.14.refs_3_ = bf16[8,64,512]{2,1,0:T(8,128)(2,1)S(1)} collective-permute-done((bf16[8,64,512]{2,1,0:T(8,128)(2,1)}, bf16[8,64,512]{2,1,0:T(8,128)(2,1)S(1)}, u32[]{:S(2)}, u32[]{:S(2)}) %collective-permute-start.14) | collective-permute-done | bytes 524320 | tf_op jit(solution)/shard_map/ppermute | solution.py:137
  161.7 1.8 combine_grad_queries.1
  163.5 6.1 %collective-permute-done.15 = bf16[224,1024]{1,0:T(8,128)(2,1)S(1)} collective-permute-done((bf16[224,1024]{1,0:T(8,128)(2,1)}, bf16[224,1024]{1,0:T(8,128)(2,1)S(1)}, u32[]{:S(2)}, u32[]{:S(2)}) %collective-permute-start.15) | collective-permute-done | bytes 458784 | tf_op jit(solution)/shard_map/ppermute | solution.py:137
  169.6 5.8 %collective-permute-done.16 = bf16[224,1024]{1,0:T(8,128)(2,1)S(1)} collective-permute-done((bf16[224,1024]{1,0:T(8,128)(2,1)}, bf16[224,1024]{1,0:T(8,128)(2,1)S(1)}, u32[]{:S(2)}, u32[]{:S(2)}) %collective-permute-start.16) | collective-permute-done | bytes 458784 | tf_op jit(solution)/shard_map/ppermute | solution.py:137
  175.4 1.3 collective-permute-done.17
  176.7 0.3 convert_add_fusion
  177.0 1.0 fusion
  178.0 2.0 %reduce-scatter.2.cloned.1.call-done = bf16[2,128,896]{2,1,0:T(8,128)(2,1)} async-done(((bf16[16,128,896]{2,1,0:T(8,128)(2,1)}), bf16[2,128,896]{2,1,0:T(8,128)(2,1)}) %reduce-scatter.2.cloned.1.call-update) | async-done | bytes 458768 | tf_op jit(solution)/shard_map/reduce_scatter | solution.py:652
  (51 shorter events, 0.2 us)
Async XLA Ops:
  7.2 55.6 %all-gather.2.cloned.1.call-start = ((), (), s32[]{:S(2)}) async-start(), calls=%async_computation.1 | async-start | bytes 4128768 | tf_op jit(solution)/shard_map/all_gather | solution.py:635
  7.2 19.3 %copy-start.12 = (s32[12,2]{0,1:T(2,128)S(1)}, s32[12,2]{0,1:T(2,128)}, u32[]{:S(2)}) copy-start(s32[12,2]{0,1:T(2,128)} %param.16) | copy-start | bytes 292
  7.2 19.3 %copy-start.14 = (s32[12,2]{0,1:T(2,128)S(1)}, s32[12,2]{0,1:T(2,128)}, u32[]{:S(2)}) copy-start(s32[12,2]{0,1:T(2,128)} %param.17) | copy-start | bytes 292
  17.3 162.7 %reduce-scatter.2.cloned.1.call-start = ((), (), s32[]{:S(2)}) async-start(), calls=%async_computation.2 | async-start | bytes 4128768 | tf_op jit(solution)/shard_map/reduce_scatter | solution.py:652
  21.9 56.3 %collective-permute-start.3 = (bf16[8,2,64,512]{3,2,1,0:T(8,128)(2,1)}, bf16[8,2,64,512]{3,2,1,0:T(8,128)(2,1)S(1)}, u32[]{:S(2)}, u32[]{:S(2)}) collective-permute-start(bf16[8,2,64,512]{3,2,1,0:T(8,128)(2,1)} %get-tuple-element.34), channel_id=1, source_target_pairs={{0,8},{8,0},{16,24},{24,16},{1,9},{9,1},{17,25},{25,17},{2,10},{10... | collective-permute-start | bytes 3145736 | tf_op jit(solution)/shard_map/ppermute | solution.py:137
  24.9 53.3 %collective-permute-start.4 = (bf16[8,2,64,512]{3,2,1,0:T(8,128)(2,1)}, bf16[8,2,64,512]{3,2,1,0:T(8,128)(2,1)S(1)}, u32[]{:S(2)}, u32[]{:S(2)}) collective-permute-start(bf16[8,2,64,512]{3,2,1,0:T(8,128)(2,1)} %get-tuple-element.35), channel_id=1, source_target_pairs={{0,16},{8,24},{16,0},{24,8},{1,17},{9,25},{17,1},{25,9},{2,18},{10... | collective-permute-start | bytes 3145736 | tf_op jit(solution)/shard_map/ppermute | solution.py:137
  26.5 51.8 %collective-permute-start.5 = (bf16[8,2,64,512]{3,2,1,0:T(8,128)(2,1)}, bf16[8,2,64,512]{3,2,1,0:T(8,128)(2,1)}, u32[]{:S(2)}, u32[]{:S(2)}) collective-permute-start(bf16[8,2,64,512]{3,2,1,0:T(8,128)(2,1)} %get-tuple-element.36), channel_id=1, source_target_pairs={{0,24},{8,16},{16,8},{24,0},{1,25},{9,17},{17,9},{25,1},{2,26},{10... | collective-permute-start | bytes 3145736 | tf_op jit(solution)/shard_map/ppermute | solution.py:137
  26.7 45.5 %copy-start.13 = (s32[1,24]{1,0:T(1,128)}, s32[1,24]{1,0:T(1,128)S(1)}, u32[]{:S(2)}) copy-start(s32[1,24]{1,0:T(1,128)S(1)} %reshape.31.refs_0_) | copy-start | bytes 292
  26.7 45.5 %collective-permute-start.2 = (s32[1,24]{1,0:T(1,128)S(1)}, s32[1,24]{1,0:T(1,128)S(1)}, u32[]{:S(2)}, u32[]{:S(2)}) collective-permute-start(s32[1,24]{1,0:T(1,128)S(1)} %reshape.31.refs_0_), channel_id=1, source_target_pairs={{0,24},{8,16},{16,8},{24,0},{1,25},{9,17},{17,9},{25,1},{2,26},{10... | collective-permute-start | bytes 296 | tf_op jit(solution)/shard_map/ppermute | solution.py:137
  29.7 43.9 %collective-permute-start.1 = (s32[1,24]{1,0:T(1,128)S(1)}, s32[1,24]{1,0:T(1,128)S(1)}, u32[]{:S(2)}, u32[]{:S(2)}) collective-permute-start(s32[1,24]{1,0:T(1,128)S(1)} %reshape.31.refs_0_), channel_id=1, source_target_pairs={{0,16},{8,24},{16,0},{24,8},{1,17},{9,25},{17,1},{25,9},{2,18},{10... | collective-permute-start | bytes 296 | tf_op jit(solution)/shard_map/ppermute | solution.py:137
  72.2 3.5 %copy-start.15 = (s32[1,24]{1,0:T(1,128)}, s32[1,24]{1,0:T(1,128)S(1)}, u32[]{:S(2)}) copy-start(s32[1,24]{1,0:T(1,128)S(1)} %collective-permute-done.2.refs_3_) | copy-start | bytes 292
  72.2 3.5 %collective-permute-start = (s32[1,24]{1,0:T(1,128)S(1)}, s32[1,24]{1,0:T(1,128)S(1)}, u32[]{:S(2)}, u32[]{:S(2)}) collective-permute-start(s32[1,24]{1,0:T(1,128)S(1)} %reshape.31.refs_0_), channel_id=1, source_target_pairs={{0,8},{8,0},{16,24},{24,16},{1,9},{9,1},{17,25},{25,17},{2,10},{10... | collective-permute-start | bytes 296 | tf_op jit(solution)/shard_map/ppermute | solution.py:137
  73.6 2.2 %copy-start.16 = (s32[1,24]{1,0:T(1,128)}, s32[1,24]{1,0:T(1,128)S(1)}, u32[]{:S(2)}) copy-start(s32[1,24]{1,0:T(1,128)S(1)} %collective-permute-done.1.refs_2_) | copy-start | bytes 292
  75.7 0.5 copy-start.17
  78.2 1.0 copy-start.18
  78.2 1.3 copy-start.19
  90.4 11.0 %collective-permute-start.11 = (f32[32,2,256]{2,1,0:T(2,128)}, f32[32,2,256]{2,1,0:T(2,128)S(1)}, u32[]{:S(2)}, u32[]{:S(2)}) collective-permute-start(f32[32,2,256]{2,1,0:T(2,128)} %get-tuple-element.41.refs_4_), channel_id=1, source_target_pairs={{0,24},{8,16},{16,8},{24,0},{1,25},{9,17},{17,9},{25,1},{2,26},{10... | collective-permute-start | bytes 196616 | tf_op jit(solution)/shard_map/ppermute | solution.py:137
  97.4 6.0 %collective-permute-start.10 = (f32[32,2,256]{2,1,0:T(2,128)}, f32[32,2,256]{2,1,0:T(2,128)S(1)}, u32[]{:S(2)}, u32[]{:S(2)}) collective-permute-start(f32[32,2,256]{2,1,0:T(2,128)} %get-tuple-element.41.refs_4_), channel_id=1, source_target_pairs={{0,16},{8,24},{16,0},{24,8},{1,17},{9,25},{17,1},{25,9},{2,18},{10... | collective-permute-start | bytes 196616 | tf_op jit(solution)/shard_map/ppermute | solution.py:137
  98.8 5.2 %collective-permute-start.9 = (f32[32,2,256]{2,1,0:T(2,128)}, f32[32,2,256]{2,1,0:T(2,128)S(1)}, u32[]{:S(2)}, u32[]{:S(2)}) collective-permute-start(f32[32,2,256]{2,1,0:T(2,128)} %get-tuple-element.41.refs_4_), channel_id=1, source_target_pairs={{0,8},{8,0},{16,24},{24,16},{1,9},{9,1},{17,25},{25,17},{2,10},{10... | collective-permute-start | bytes 196616 | tf_op jit(solution)/shard_map/ppermute | solution.py:137
  98.8 37.6 %collective-permute-start.6 = (bf16[8,64,512]{2,1,0:T(8,128)(2,1)}, bf16[8,64,512]{2,1,0:T(8,128)(2,1)S(1)}, u32[]{:S(2)}, u32[]{:S(2)}) collective-permute-start(bf16[8,64,512]{2,1,0:T(8,128)(2,1)} %get-tuple-element.38), channel_id=1, source_target_pairs={{0,8},{8,0},{16,24},{24,16},{1,9},{9,1},{17,25},{25,17},{2,10},{10... | collective-permute-start | bytes 1572872 | tf_op jit(solution)/shard_map/ppermute | solution.py:137
  100.8 37.0 %collective-permute-start.7 = (bf16[8,64,512]{2,1,0:T(8,128)(2,1)}, bf16[8,64,512]{2,1,0:T(8,128)(2,1)S(1)}, u32[]{:S(2)}, u32[]{:S(2)}) collective-permute-start(bf16[8,64,512]{2,1,0:T(8,128)(2,1)} %get-tuple-element.39), channel_id=1, source_target_pairs={{0,16},{8,24},{16,0},{24,8},{1,17},{9,25},{17,1},{25,9},{2,18},{10... | collective-permute-start | bytes 1572872 | tf_op jit(solution)/shard_map/ppermute | solution.py:137
  101.5 2.6 %copy-start.2 = (f32[32,2,256]{2,1,0:T(2,128)}, f32[32,2,256]{2,1,0:T(2,128)S(1)}, u32[]{:S(2)}) copy-start(f32[32,2,256]{2,1,0:T(2,128)S(1)} %collective-permute-done.11.refs_7_) | copy-start | bytes 196612
  101.5 37.0 %collective-permute-start.8 = (bf16[8,64,512]{2,1,0:T(8,128)(2,1)}, bf16[8,64,512]{2,1,0:T(8,128)(2,1)S(1)}, u32[]{:S(2)}, u32[]{:S(2)}) collective-permute-start(bf16[8,64,512]{2,1,0:T(8,128)(2,1)} %get-tuple-element.40), channel_id=1, source_target_pairs={{0,24},{8,16},{16,8},{24,0},{1,25},{9,17},{17,9},{25,1},{2,26},{10... | collective-permute-start | bytes 1572872 | tf_op jit(solution)/shard_map/ppermute | solution.py:137
  103.4 0.7 copy-start.4
  104.1 0.6 copy-start.6
  125.6 27.6 %collective-permute-start.12 = (bf16[8,64,512]{2,1,0:T(8,128)(2,1)}, bf16[8,64,512]{2,1,0:T(8,128)(2,1)S(1)}, u32[]{:S(2)}, u32[]{:S(2)}) collective-permute-start(bf16[8,64,512]{2,1,0:T(8,128)(2,1)} %get-tuple-element.44), channel_id=1, source_target_pairs={{0,8},{8,0},{16,24},{24,16},{1,9},{9,1},{17,25},{25,17},{2,10},{10... | collective-permute-start | bytes 1572872 | tf_op jit(solution)/shard_map/ppermute | solution.py:137
  135.4 20.5 %collective-permute-start.13 = (bf16[8,64,512]{2,1,0:T(8,128)(2,1)}, bf16[8,64,512]{2,1,0:T(8,128)(2,1)S(1)}, u32[]{:S(2)}, u32[]{:S(2)}) collective-permute-start(bf16[8,64,512]{2,1,0:T(8,128)(2,1)} %get-tuple-element.45), channel_id=1, source_target_pairs={{0,16},{8,24},{16,0},{24,8},{1,17},{9,25},{17,1},{25,9},{2,18},{10... | collective-permute-start | bytes 1572872 | tf_op jit(solution)/shard_map/ppermute | solution.py:137
  136.4 25.3 %collective-permute-start.14 = (bf16[8,64,512]{2,1,0:T(8,128)(2,1)}, bf16[8,64,512]{2,1,0:T(8,128)(2,1)S(1)}, u32[]{:S(2)}, u32[]{:S(2)}) collective-permute-start(bf16[8,64,512]{2,1,0:T(8,128)(2,1)} %get-tuple-element.46), channel_id=1, source_target_pairs={{0,24},{8,16},{16,8},{24,0},{1,25},{9,17},{17,9},{25,1},{2,26},{10... | collective-permute-start | bytes 1572872 | tf_op jit(solution)/shard_map/ppermute | solution.py:137
  139.0 11.5 %copy-start = (bf16[8,64,512]{2,1,0:T(8,128)(2,1)S(1)}, bf16[8,64,512]{2,1,0:T(8,128)(2,1)}, u32[]{:S(2)}) copy-start(bf16[8,64,512]{2,1,0:T(8,128)(2,1)} %get-tuple-element.37.refs_0_) | copy-start | bytes 1572868
  139.0 11.5 %copy-start.1 = (f32[32,2,256]{2,1,0:T(2,128)S(1)}, f32[32,2,256]{2,1,0:T(2,128)}, u32[]{:S(2)}) copy-start(f32[32,2,256]{2,1,0:T(2,128)} %get-tuple-element.41.refs_4_) | copy-start | bytes 196612
  139.0 11.5 %copy-start.3 = (f32[32,2,256]{2,1,0:T(2,128)S(1)}, f32[32,2,256]{2,1,0:T(2,128)}, u32[]{:S(2)}) copy-start(f32[32,2,256]{2,1,0:T(2,128)} %copy-done.2) | copy-start | bytes 196612
  139.0 11.5 %copy-start.5 = (f32[32,2,256]{2,1,0:T(2,128)S(1)}, f32[32,2,256]{2,1,0:T(2,128)}, u32[]{:S(2)}) copy-start(f32[32,2,256]{2,1,0:T(2,128)} %copy-done.4) | copy-start | bytes 196612
  139.0 11.5 %copy-start.7 = (f32[32,2,256]{2,1,0:T(2,128)S(1)}, f32[32,2,256]{2,1,0:T(2,128)}, u32[]{:S(2)}) copy-start(f32[32,2,256]{2,1,0:T(2,128)} %copy-done.6) | copy-start | bytes 196612
  139.0 11.5 %copy-start.8 = (s32[24]{0:T(128)S(1)}, s32[24]{0:T(128)}, u32[]{:S(2)}) copy-start(s32[24]{0:T(128)} %get-tuple-element.29.position) | copy-start | bytes 292
  139.0 11.5 %copy-start.9 = (s32[24]{0:T(128)S(1)}, s32[24]{0:T(128)}, u32[]{:S(2)}) copy-start(s32[24]{0:T(128)} %get-tuple-element.30.place) | copy-start | bytes 292
  139.0 22.7 %copy-start.10 = (bf16[8,64,512]{2,1,0:T(8,128)(2,1)S(1)}, bf16[8,64,512]{2,1,0:T(8,128)(2,1)}, u32[]{:S(2)}) copy-start(bf16[8,64,512]{2,1,0:T(8,128)(2,1)} %get-tuple-element.43.refs_0_) | copy-start | bytes 1572868
  148.0 21.5 %collective-permute-start.15 = (bf16[224,1024]{1,0:T(8,128)(2,1)}, bf16[224,1024]{1,0:T(8,128)(2,1)S(1)}, u32[]{:S(2)}, u32[]{:S(2)}) collective-permute-start(bf16[224,1024]{1,0:T(8,128)(2,1)} %get-tuple-element.50), channel_id=1, source_target_pairs={{0,8},{8,0},{16,24},{24,16},{1,9},{9,1},{17,25},{25,17},{2,10},{10... | collective-permute-start | bytes 1376264 | tf_op jit(solution)/shard_map/ppermute | solution.py:137
  149.6 25.8 %collective-permute-start.16 = (bf16[224,1024]{1,0:T(8,128)(2,1)}, bf16[224,1024]{1,0:T(8,128)(2,1)S(1)}, u32[]{:S(2)}, u32[]{:S(2)}) collective-permute-start(bf16[224,1024]{1,0:T(8,128)(2,1)} %get-tuple-element.51), channel_id=1, source_target_pairs={{0,16},{8,24},{16,0},{24,8},{1,17},{9,25},{17,1},{25,9},{2,18},{10... | collective-permute-start | bytes 1376264 | tf_op jit(solution)/shard_map/ppermute | solution.py:137
  153.1 23.6 %collective-permute-start.17 = (bf16[224,1024]{1,0:T(8,128)(2,1)}, bf16[224,1024]{1,0:T(8,128)(2,1)S(1)}, u32[]{:S(2)}, u32[]{:S(2)}) collective-permute-start(bf16[224,1024]{1,0:T(8,128)(2,1)} %get-tuple-element.52), channel_id=1, source_target_pairs={{0,24},{8,16},{16,8},{24,0},{1,25},{9,17},{17,9},{25,1},{2,26},{10... | collective-permute-start | bytes 1376264 | tf_op jit(solution)/shard_map/ppermute | solution.py:137
  161.7 15.1 %copy-start.11 = (bf16[224,1024]{1,0:T(8,128)(2,1)S(1)}, bf16[224,1024]{1,0:T(8,128)(2,1)}, u32[]{:S(2)}) copy-start(bf16[224,1024]{1,0:T(8,128)(2,1)} %get-tuple-element.49) | copy-start | bytes 1376260
Sparse Core Ops, SparseCore 0:
  17.4 45.2 all-gather.1
  125.7 54.2 reduce-scatter.1

commit v4 on v3

--- a/solution.py
+++ b/solution.py
@@ -9,6 +9,7 @@
 from jax.sharding import PartitionSpec as P
 
 HD = 128
+HEADER = 16
 UNROLL = 4
 TAIL_FLOPS = 32000000000
 WEIGHT_FLOPS = 70000000000
@@ -105,26 +106,32 @@
     )(rows, up_weight, down_weight).reshape(neighbours.shape)
 
 
-def project_kernel(table_ref, kw_ref, vw_ref, kv_ref):
-    width = kw_ref.shape[1]
-    kv_ref[:, :width] = mm(table_ref[...], kw_ref[...], NN).astype(BF16)
-    kv_ref[:, width:] = mm(table_ref[...], vw_ref[...], NN).astype(BF16)
-
-
-def project(table, key_weight, value_weight):
+def project_kernel(row_len, table_ref, kw_ref, vw_ref, kv_ref):
+    pairs = kw_ref.shape[1] // (2 * HD)
+    for first, weight in ((0, kw_ref), (pairs, vw_ref)):
+        product = mm(table_ref[...], weight[...], NN).astype(BF16)
+        for n in range(table_ref.shape[0] // row_len):
+            for p in range(pairs):
+                kv_ref[n, first + p] = product[
+                    n * row_len : (n + 1) * row_len, p * 2 * HD : (p + 1) * 2 * HD
+                ]
+
+
+def project(table, key_weight, value_weight, row_len):
     rows, feat = table.shape
     width = key_weight.shape[1]
     block = 512 if rows % 512 == 0 else rows
+    blocks = 2 * width // (2 * HD)
     return pl.pallas_call(
-        project_kernel,
+        functools.partial(project_kernel, row_len),
         grid=(rows // block,),
-        out_shape=jax.ShapeDtypeStruct((rows, 2 * width), BF16),
+        out_shape=jax.ShapeDtypeStruct((rows // row_len, blocks, row_len, 2 * HD), BF16),
         in_specs=[
             pl.BlockSpec((block, feat), lambda i: (i, 0)),
             pl.BlockSpec((feat, width), lambda i: (0, 0)),
             pl.BlockSpec((feat, width), lambda i: (0, 0)),
         ],
-        out_specs=pl.BlockSpec((block, 2 * width), lambda i: (i, 0)),
+        out_specs=pl.BlockSpec((block // row_len, blocks, row_len, 2 * HD), lambda i: (i, 0, 0, 0)),
         compiler_params=params(59),
         cost_estimate=cost(8 * rows * feat * width, rows * (feat + 2 * width) * 2),
         name="project",
@@ -142,12 +149,17 @@
     return [lax.slice(a, (0,) * a.ndim, (1,) * (a.ndim - 1) + (8,)) for a in arrays]
 
 
-def dispatch_kernel(waits, me, group_ids, q_ref, g_ref, *refs):
-    out_refs, refs = refs[waits:-5], refs[-5:]
-    position, place, taken, held, sems = refs
-    groups, capacity, _, span_len, _ = held.shape
+def dispatch_kernel(waits, me, group_ids, slot_ids, q_ref, g_ref, *refs):
+    out_refs, refs = refs[waits:-6], refs[-6:]
+    position, place, taken, held, info, sems = refs
+    groups, rows, _ = held.shape
+    requests = position.shape[0]
+    span_len = q_ref.shape[0] // (requests // 2)
+    capacity = (rows - HEADER) // (2 * span_len)
+    slots = groups * capacity
     for d in range(groups):
         taken[d] = 0
+    info[...] = jnp.zeros_like(info)
 
     def step(i, carry):
         span = i // 2
@@ -155,88 +167,61 @@
         rank = taken[offset]
         taken[offset] = rank + 1
         position[i] = offset * capacity + rank
-        place[i] = offset * groups * capacity + offset * capacity + rank
-        rows = pl.ds(pl.multiple_of(span * span_len, span_len), span_len)
-        held[offset, rank, 0] = q_ref[rows, :]
-        held[offset, rank, 1] = g_ref[rows, :]
-        return carry
-
-    lax.fori_loop(0, position.shape[0], step, 0)
+        place[i] = offset * slots + offset * capacity + rank
+        source = pl.ds(pl.multiple_of(span * span_len, span_len), span_len)
+        first = pl.multiple_of(rank * (2 * span_len), span_len)
+        held[offset, pl.ds(first, span_len), :] = q_ref[source, :]
+        held[offset, pl.ds(first + span_len, span_len), :] = g_ref[source, :]
+        return carry
+
+    lax.fori_loop(0, requests, step, 0)
+    kind = lax.broadcasted_iota(jnp.int32, info.shape[1:], 0)
+    lane = lax.broadcasted_iota(jnp.int32, info.shape[1:], 1)
+
+    def note(i, carry):
+        span, side = i // 2, i % 2
+        target, other = group_ids[side, span], group_ids[1 - side, span]
+        offset = jnp.bitwise_xor(target, me[0])
+        rank = position[i] - offset * capacity
+        there = position[2 * span + 1 - side]
+        facts = jnp.where(
+            kind == 0,
+            slot_ids[side, span],
+            jnp.where(kind == 1, jnp.bitwise_xor(target, other), jnp.where(kind == 2, there, 0)),
+        )
+        info[offset] = jnp.where((lane == rank) & (kind < 3), facts, info[offset])
+        return carry
+
+    lax.fori_loop(0, requests, note, 0)
+    for d in range(groups):
+        facts = jnp.where(kind == 3, taken[d], info[d]).astype(F32)
+        held[d, rows - HEADER :, :] = jnp.zeros((HEADER, held.shape[2]), BF16)
+        held[d, rows - HEADER :, :128] = facts.astype(BF16)
     for copy in fetch([(held.at[d], ref) for d, ref in enumerate(out_refs)], sems):
         copy.wait()
 
 
-def dispatch(me, group_ids, queries, grad_ctx, groups, capacity, span_len, waits):
+def dispatch(me, group_ids, slot_ids, queries, grad_ctx, groups, capacity, span_len, waits):
     width = queries.shape[1]
     requests = group_ids.size
-    piece = (capacity, 2, span_len, width)
+    piece = (capacity * 2 * span_len + HEADER, width)
     outs = pl.pallas_call(
         functools.partial(dispatch_kernel, len(waits)),
         out_shape=[jax.ShapeDtypeStruct(piece, BF16)] * groups
         + [jax.ShapeDtypeStruct((requests,), jnp.int32)] * 2,
-        in_specs=[smem(), smem(), vmem(), vmem()] + [anyspace()] * len(waits),
+        in_specs=[smem()] * 3 + [vmem(), vmem()] + [anyspace()] * len(waits),
         out_specs=[anyspace()] * groups + [smem()] * 2,
         scratch_shapes=[
             pltpu.SMEM((groups,), jnp.int32),
             pltpu.VMEM((groups, *piece), BF16),
+            pltpu.VMEM((groups, HEADER, 128), jnp.int32),
             pltpu.SemaphoreType.DMA((groups,)),
         ],
         compiler_params=params(56),
         cost_estimate=cost(0, groups * capacity * span_len * width * 6),
         name="dispatch",
-    )(me, group_ids, queries, grad_ctx, *waits)
+    )(me, group_ids, slot_ids, queries, grad_ctx, *waits)
     return outs[:groups], outs[groups], outs[groups + 1]
-
-
-def slots_kernel(groups, waits, capacity, slot_bits, me, *refs):
-    codes, (counts, nbrs, partner, taken) = refs[:groups], refs[groups + waits :]
-    slots = groups * capacity
-    for d in range(groups):
-        source = jnp.bitwise_xor(me[0], d)
-        for h in range(groups):
-            taken[h] = 0
-
-        def step(span, carry, d=d, source=source):
-            both = []
-            for i in range(2):
-                code = codes[d][0, 2 * span + i]
-                target = jnp.right_shift(code, slot_bits)
-                rank = taken[target]
-                taken[target] = rank + 1
-                there = jnp.bitwise_xor(target, source) * capacity + rank
-                both.append((target, rank, jnp.bitwise_and(code, (1 << slot_bits) - 1), there))
-            for i in range(2):
-                target, rank, nbr, _ = both[i]
-                other, _, _, there = both[1 - i]
-
-                @pl.when(target == me[0])
-                def _():
-                    nbrs[d * capacity + rank] = nbr
-                    partner[d * capacity + rank] = jnp.bitwise_xor(other, me[0]) * slots + there
-
-            return carry
-
-        lax.fori_loop(0, codes[d].shape[1] // 2, step, 0)
-        counts[d] = taken[me[0]]
-
-
-def slot_lists(me, codes, capacity, slot_bits, waits):
-    groups = len(codes)
-    slots = groups * capacity
-    return pl.pallas_call(
-        functools.partial(slots_kernel, groups, len(waits), capacity, slot_bits),
-        out_shape=[
-            jax.ShapeDtypeStruct((groups,), jnp.int32),
-            jax.ShapeDtypeStruct((slots,), jnp.int32),
-            jax.ShapeDtypeStruct((slots,), jnp.int32),
-        ],
-        in_specs=[smem()] * (1 + groups) + [anyspace()] * len(waits),
-        out_specs=[smem()] * 3,
-        scratch_shapes=[pltpu.SMEM((groups,), jnp.int32)],
-        compiler_params=params(56),
-        cost_estimate=cost(0, slots * 16),
-        name="slot_lists",
-    )(me, *codes, *waits)
 
 
 def gather_groups(refs, held):
@@ -327,42 +312,90 @@
         dst[h * span_len : (h + 1) * span_len, side : side + HD] = block[:, h * HD : (h + 1) * HD]
 
 
-def store_pair(dst, k, p, both, span_len):
-    for s in range(2):
-        cols = slice((2 * p + s) * HD, (2 * p + s + 1) * HD)
-        rows = slice(s * span_len, (s + 1) * span_len)
-        dst[k, :, cols] = both[rows, s * HD : (s + 1) * HD].astype(BF16)
-
-
-def rows_of(nbr, row_len):
-    return pl.ds(pl.multiple_of(nbr * row_len, row_len), row_len)
-
-
-def columns_of(p, width, span_len):
-    first = 2 * p * HD
-    return (
-        slice(first, first + 2 * HD),
-        slice(width + first, width + first + 2 * HD),
-        slice(2 * p * span_len, 2 * (p + 1) * span_len),
-    )
+def blocks_of(square, size):
+    count = square.shape[0] // size
+    return jnp.concatenate(
+        [square[i * size : (i + 1) * size, i * size : (i + 1) * size] for i in range(count)], axis=1
+    )
+
+
+def on_diagonal(parts):
+    zero = jnp.zeros_like(parts[0])
+    return jnp.concatenate(
+        [
+            jnp.concatenate([part if j == i else zero for j in range(len(parts))], axis=1)
+            for i, part in enumerate(parts)
+        ],
+        axis=0,
+    )
+
+
+def halves(wide, size):
+    return [wide[:, i * size : (i + 1) * size] for i in range(wide.shape[1] // size)]
+
+
+def store_heads(dst, k, both, span_len):
+    for h in range(both.shape[0] // span_len):
+        rows = slice(h * span_len, (h + 1) * span_len)
+        side = (h % 2) * HD
+        dst[k, :, h * HD : (h + 1) * HD] = both[rows, side : side + HD].astype(BF16)
+
+
+def stacked(kv, nbr, first, pairs):
+    return kv[nbr, first : first + pairs].reshape(pairs * kv.shape[2], kv.shape[3])
+
+
+def slot_rows(qg, d, which, span_len):
+    return qg[d, pl.ds(pl.multiple_of(which * span_len, span_len), span_len), :]
+
+
+def safe_inverse(total):
+    shrink = jnp.where(total > 2.0**100, 2.0**-64, 1.0)
+    scaled = total * shrink
+    return shrink, 1.0 / jnp.where(scaled > 0.0, scaled, 1.0)
 
 
 def arrival(held, d, sems):
     return pltpu.make_async_copy(held.at[d], held.at[d], sems.at[d])
 
 
-def local_kernel(groups, row_len, scale, counts, nbrs, *refs):
-    qg_refs, (kv_ref, stats_ref), refs = refs[:groups], refs[groups : groups + 2], refs[groups + 2 :]
-    ctx_refs, refs = refs[:groups], refs[groups:]
-    kv, qg, ctx, ksem, isem, osem = refs[:6]
-    diag = refs[6:]
-    capacity, _, span_len, width = qg_refs[0].shape
+def local_kernel(groups, row_len, span_len, *refs):
+    qg_refs, refs = refs[:groups], refs[groups:]
+    (kv_ref, stats_ref), refs = refs[:2], refs[2:]
+    ctx_refs, (counts, nbrs, partner), refs = refs[:groups], refs[groups : groups + 3], refs[groups + 3 :]
+    kv, qg, ctx, heads_up, facts, plain, ksem, isem, hsem, osem = refs[:10]
+    diag = refs[10:]
+    rows, width = qg_refs[0].shape
     heads = width // HD
+    capacity = (rows - HEADER) // (2 * span_len)
+    slots = groups * capacity
+    pairs = heads // 2
+    factor = math.log2(math.e) / math.sqrt(HD)
+    head_rows = pl.ds(rows - HEADER, HEADER)
+    heads_in = fetch(
+        [(ref.at[head_rows, pl.ds(0, 128)], heads_up.at[d]) for d, ref in enumerate(qg_refs)], hsem
+    )
     kv_in = fetch([(kv_ref, kv)], ksem)
     fetch([(ref, qg.at[d]) for d, ref in enumerate(qg_refs)], isem)
     ctx_out = [pltpu.make_async_copy(ctx.at[d], ref, osem.at[d]) for d, ref in enumerate(ctx_refs)]
+    for copy in heads_in:
+        copy.wait()
+    facts[...] = heads_up[...].astype(F32).astype(jnp.int32)
+    to_scalar = pltpu.make_async_copy(facts, plain, osem.at[groups])
+    to_scalar.start()
     for ref in diag:
         ref[...] = jnp.zeros_like(ref)
+    to_scalar.wait()
+
+    def unpack(j, carry):
+        d, k = j // capacity, j % capacity
+        nbrs[j] = plain[d, 0, k]
+        partner[j] = plain[d, 1, k] * slots + plain[d, 2, k]
+        return carry
+
+    lax.fori_loop(0, slots, unpack, 0)
+    for d in range(groups):
+        counts[d] = plain[d, 3, 0]
     kv_in[0].wait()
 
     def one_group(d, carry):
@@ -373,19 +406,19 @@
                 k = jnp.minimum(UNROLL * i + u, counts[d] - 1)
                 j = d * capacity + k
                 q_diag, g_diag = diag[2 * u], diag[2 * u + 1]
-                fill_diagonal(q_diag, qg[d, k, 0], heads, span_len)
-                fill_diagonal(g_diag, qg[d, k, 1], heads, span_len)
-                rows = rows_of(nbrs[j], row_len)
-                for p in range(heads // 2):
-                    cols, vcols, lanes = columns_of(p, width, span_len)
-                    values = kv[rows, vcols]
-                    expo = jnp.exp(mm(kv[rows, cols], q_diag[lanes, :], NT) * scale)
-                    grad_probs = mm(values, g_diag[lanes, :], NT)
-                    total = jnp.sum(expo, axis=0, keepdims=True)
-                    probs = expo / jnp.where(total > 0.0, total, 1.0)
-                    stats_ref[j, 0:1, lanes] = total
-                    stats_ref[j, 1:2, lanes] = jnp.sum(probs * grad_probs, axis=0, keepdims=True)
-                    store_pair(ctx.at[d], k, p, mm(probs.astype(BF16).T, values, NN), span_len)
+                fill_diagonal(q_diag, slot_rows(qg, d, 2 * k, span_len), heads, span_len)
+                fill_diagonal(g_diag, slot_rows(qg, d, 2 * k + 1, span_len), heads, span_len)
+                values = stacked(kv, nbrs[j], pairs, pairs)
+                scores = mm(stacked(kv, nbrs[j], 0, pairs), q_diag[...], NT)
+                expo = jnp.exp2(blocks_of(scores, row_len) * factor)
+                grad_probs = blocks_of(mm(values, g_diag[...], NT), row_len)
+                total = jnp.sum(expo, axis=0, keepdims=True)
+                shrink, inverse = safe_inverse(total)
+                probs = (expo * shrink) * inverse
+                stats_ref[j, 0:1, :] = total
+                stats_ref[j, 1:2, :] = jnp.sum(probs * grad_probs, axis=0, keepdims=True)
+                turned = on_diagonal([x.T for x in halves(probs.astype(BF16), row_len)])
+                store_heads(ctx.at[d], k, mm(turned, values, NN), span_len)
             return carry
 
         lax.fori_loop(0, (counts[d] + UNROLL - 1) // UNROLL, step, 0)
@@ -402,24 +435,30 @@
         copy.wait()
 
 
-def attend_local(counts, nbrs, qg, kv, row_len, scale):
+def attend_local(qg, kv, row_len, span_len):
     groups = len(qg)
-    capacity, _, span_len, width = qg[0].shape
+    rows, width = qg[0].shape
+    capacity = (rows - HEADER) // (2 * span_len)
     slots = groups * capacity
     lanes = span_len * (width // HD)
     outs = pl.pallas_call(
-        functools.partial(local_kernel, groups, row_len, scale),
+        functools.partial(local_kernel, groups, row_len, span_len),
         out_shape=[jax.ShapeDtypeStruct((slots, 2, lanes), F32)]
-        + [jax.ShapeDtypeStruct((capacity, span_len, width), BF16)] * groups,
-        in_specs=[smem()] * 2 + [anyspace()] * (groups + 1),
-        out_specs=[vmem()] + [anyspace()] * groups,
+        + [jax.ShapeDtypeStruct((capacity, span_len, width), BF16)] * groups
+        + [jax.ShapeDtypeStruct((n,), jnp.int32) for n in (groups, slots, slots)],
+        in_specs=[anyspace()] * (groups + 1),
+        out_specs=[vmem()] + [anyspace()] * groups + [smem()] * 3,
         scratch_shapes=[
             pltpu.VMEM(kv.shape, BF16),
-            pltpu.VMEM((groups, *qg[0].shape), BF16),
+            pltpu.VMEM((groups, rows, width), BF16),
             pltpu.VMEM((groups, capacity, span_len, width), BF16),
+            pltpu.VMEM((groups, HEADER, 128), BF16),
+            pltpu.VMEM((groups, HEADER, 128), jnp.int32),
+            pltpu.SMEM((groups, HEADER, 128), jnp.int32),
             pltpu.SemaphoreType.DMA((1,)),
             pltpu.SemaphoreType.DMA((groups,)),
             pltpu.SemaphoreType.DMA((groups,)),
+            pltpu.SemaphoreType.DMA((groups + 1,)),
         ]
         + [pltpu.VMEM((lanes, 2 * HD), BF16)] * (2 * UNROLL),
         compiler_params=params(56),
@@ -429,38 +468,46 @@
             slots * row_len * lanes,
         ),
         name="attend_local",
-    )(counts, nbrs, *qg, kv)
-    return outs[0], outs[1:]
-
-
-def grads_kernel(groups, row_len, scale, counts, nbrs, partner, *refs):
+    )(*qg, kv)
+    return outs[0], outs[1 : groups + 1], outs[groups + 1 :]
+
+
+def grads_kernel(groups, row_len, span_len, counts, nbrs, partner, *refs):
     qg_refs, stat_refs, refs = refs[:groups], refs[groups : 2 * groups], refs[2 * groups :]
     (kv_ref, kw_ref, vw_ref), refs = refs[:3], refs[3:]
     gq_refs, (dkv_ref, part_ref), refs = refs[:groups], refs[groups : groups + 2], refs[groups + 2 :]
     kv, qg, stats, kw, vw, gq, acc, dkv, part, ksem, qsem, ssem, osem, psem = refs[:14]
     diag = refs[14:]
-    capacity, _, span_len, width = qg_refs[0].shape
+    width = qg_refs[0].shape[1]
+    capacity = gq_refs[0].shape[0]
     slots = groups * capacity
     heads = width // HD
+    scale = 1.0 / math.sqrt(HD)
+    pairs = heads // 2
+    factor = math.log2(math.e) * scale
     stats_in = fetch(
         [(ref, stats.at[pl.ds(d * slots, slots)]) for d, ref in enumerate(stat_refs)], ssem
     )
     kv_in, kw_in, vw_in = fetch([(kv_ref, kv), (kw_ref, kw), (vw_ref, vw)], ksem)
     fetch([(ref, qg.at[d]) for d, ref in enumerate(qg_refs)], qsem)
-    gq_out = [pltpu.make_async_copy(gq.at[d], ref, osem.at[d]) for d, ref in enumerate(gq_refs)]
+    gq_out = [
+        pltpu.make_async_copy(gq.at[d, pl.ds(0, capacity)], ref, osem.at[d])
+        for d, ref in enumerate(gq_refs)
+    ]
     for ref in diag:
         ref[...] = jnp.zeros_like(ref)
-    block = 256 if kv.shape[0] % 256 == 0 else kv.shape[0]
-    blocks = kv.shape[0] // block
+    some = 2 if acc.shape[0] % 2 == 0 else 1
+    block = some * row_len
+    blocks = acc.shape[0] // some
 
     def rows_at(i):
         return pl.ds(pl.multiple_of(i * block, block), block)
 
-    def clear(i, carry):
-        acc[rows_at(i), :] = jnp.zeros((block, 2 * width), F32)
-        return carry
-
-    lax.fori_loop(0, blocks, clear, 0)
+    def clear(n, carry):
+        acc[n] = jnp.zeros(acc.shape[1:], F32)
+        return carry
+
+    lax.fori_loop(0, acc.shape[0], clear, 0)
     for copy in [*stats_in, kv_in]:
         copy.wait()
 
@@ -474,25 +521,27 @@
                 k = jnp.minimum(place, counts[d] - 1)
                 j = d * capacity + k
                 q_diag, g_diag = diag[2 * u], diag[2 * u + 1]
-                fill_diagonal(q_diag, qg[d, k, 0], heads, span_len)
-                fill_diagonal(g_diag, qg[d, k, 1], heads, span_len)
-                rows = rows_of(nbrs[j], row_len)
+                fill_diagonal(q_diag, slot_rows(qg, d, 2 * k, span_len), heads, span_len)
+                fill_diagonal(g_diag, slot_rows(qg, d, 2 * k + 1, span_len), heads, span_len)
+                nbr = nbrs[j]
+                kept = jnp.where(live, k, capacity)
                 own, other = stats[j], stats[partner[j]]
                 total = own[0:1] + other[0:1]
-                total = jnp.where(total > 0.0, total, 1.0)
-                shift = (own[0:1] / total) * own[1:2] + (other[0:1] / total) * other[1:2]
-                for p in range(heads // 2):
-                    cols, vcols, lanes = columns_of(p, width, span_len)
-                    keys = kv[rows, cols]
-                    expo = jnp.exp(mm(keys, q_diag[lanes, :], NT) * scale)
-                    grad_probs = mm(kv[rows, vcols], g_diag[lanes, :], NT)
-                    weights = expo / total[:, lanes]
-                    mixed = weights * (grad_probs - shift[:, lanes]) * scale
-                    store_pair(gq.at[d], k, p, mm(mixed.astype(BF16).T, keys, NN), span_len)
-                    weights = jnp.where(live, weights, 0.0).astype(BF16)
-                    mixed = jnp.where(live, mixed, 0.0).astype(BF16)
-                    acc[rows, cols] += mm(mixed, q_diag[lanes, :], NN)
-                    acc[rows, vcols] += mm(weights, g_diag[lanes, :], NN)
+                shrink, inverse = safe_inverse(total)
+                shift = ((own[0:1] * shrink) * inverse) * own[1:2]
+                shift += ((other[0:1] * shrink) * inverse) * other[1:2]
+                inverse = jnp.where(live, inverse, 0.0)
+                keys = stacked(kv, nbr, 0, pairs)
+                expo = jnp.exp2(blocks_of(mm(keys, q_diag[...], NT), row_len) * factor) * shrink
+                grad_probs = blocks_of(mm(stacked(kv, nbr, pairs, pairs), g_diag[...], NT), row_len)
+                weights = expo * inverse
+                mixed = halves((weights * (grad_probs - shift) * scale).astype(BF16), row_len)
+                weights = halves(weights.astype(BF16), row_len)
+                turned = on_diagonal([x.T for x in mixed])
+                store_heads(gq.at[d], kept, mm(turned, keys, NN), span_len)
+                shape = (pairs, row_len, 2 * HD)
+                acc[nbr, :pairs] += mm(on_diagonal(mixed), q_diag[...], NN).reshape(shape)
+                acc[nbr, pairs:] += mm(on_diagonal(weights), g_diag[...], NN).reshape(shape)
             return carry
 
         lax.fori_loop(0, (counts[d] + UNROLL - 1) // UNROLL, step, 0)
@@ -517,7 +566,9 @@
 
     def finish(i, carry):
         b = rows_at(i)
-        dkv[b, :] = acc[b, :].astype(BF16)
+        for p in range(2 * pairs):
+            part_of = acc[pl.ds(i * some, some), p].reshape(block, 2 * HD)
+            dkv[b, p * 2 * HD : (p + 1) * 2 * HD] = part_of.astype(BF16)
         part[b, :] = (mm(dkv[b, :width], kw[...], NT) + mm(dkv[b, width:], vw[...], NT)).astype(BF16)
         for copy in results(i):
             copy.start()
@@ -539,15 +590,16 @@
     return [pl.ds(i * size, size) for i in range(total // size)]
 
 
-def attend_grads(counts, nbrs, partner, qg, stats, kv, key_weight, value_weight, row_len, scale):
+def attend_grads(lists, qg, stats, kv, key_weight, value_weight, row_len, span_len):
     groups = len(qg)
-    capacity, _, span_len, width = qg[0].shape
+    width = qg[0].shape[1]
+    capacity = (qg[0].shape[0] - HEADER) // (2 * span_len)
     slots = groups * capacity
     lanes = span_len * (width // HD)
-    rows = kv.shape[0]
+    rows = kv.shape[0] * row_len
     feat = key_weight.shape[0]
     outs = pl.pallas_call(
-        functools.partial(grads_kernel, groups, row_len, scale),
+        functools.partial(grads_kernel, groups, row_len, span_len),
         out_shape=[jax.ShapeDtypeStruct((capacity, span_len, width), BF16)] * groups
         + [
             jax.ShapeDtypeStruct((rows, 2 * width), BF16),
@@ -561,15 +613,15 @@
             pltpu.VMEM((groups * slots, 2, lanes), F32),
             pltpu.VMEM((feat, width), BF16),
             pltpu.VMEM((feat, width), BF16),
-            pltpu.VMEM((groups, capacity, span_len, width), BF16),
-            pltpu.VMEM((rows, 2 * width), F32),
+            pltpu.VMEM((groups, capacity + 1, span_len, width), BF16),
+            pltpu.VMEM(kv.shape, F32),
             pltpu.VMEM((rows, 2 * width), BF16),
             pltpu.VMEM((rows, feat), BF16),
             pltpu.SemaphoreType.DMA((3,)),
             pltpu.SemaphoreType.DMA((groups,)),
             pltpu.SemaphoreType.DMA((groups,)),
             pltpu.SemaphoreType.DMA((groups,)),
-            pltpu.SemaphoreType.DMA((max(1, rows // 256), 2)),
+            pltpu.SemaphoreType.DMA((kv.shape[0], 2)),
         ]
         + [pltpu.VMEM((lanes, 2 * HD), BF16)] * (2 * UNROLL),
         compiler_params=params(56),
@@ -579,7 +631,7 @@
             slots * row_len * lanes,
         ),
         name="attend_grads",
-    )(counts, nbrs, partner, *qg, *stats, kv, key_weight, value_weight)
+    )(*lists, *qg, *stats, kv, key_weight, value_weight)
     return outs[:groups], outs[groups], outs[groups + 1]
 
 
@@ -629,25 +681,19 @@
     span_len = queries.shape[0] // span_count
     own_count, row_len, feat = neighbours.shape
     table_len = own_count * lax.axis_size("ret")
-    scale = 1.0 / math.sqrt(HD)
 
     encoded_own = encode(neighbours, up_weight, down_weight)
     table = lax.all_gather(encoded_own, "ret", axis=0, tiled=True).reshape(-1, feat)
     outgoing, position, place = dispatch(
-        me, group_ids.T, queries, grad_ctx, groups, capacity, span_len, [encoded_own]
+        me, group_ids.T, slot_ids.T, queries, grad_ctx, groups, capacity, span_len, [encoded_own]
     )
     arrived = exchange(outgoing, "seq")
-    kv = project(table, key_weight, value_weight)
-
-    slot_bits = (table_len - 1).bit_length()
-    codes = (group_ids * (1 << slot_bits) + slot_ids).reshape(1, -1)
-    codes = exchange([codes] * groups, "seq")
-    counts, nbrs, partner = slot_lists(me, codes, capacity, slot_bits, [kv])
-    own_stats, local_ctx = attend_local(counts, nbrs, arrived, kv, row_len, scale)
+    kv = project(table, key_weight, value_weight, row_len)
+    own_stats, local_ctx, lists = attend_local(arrived, kv, row_len, span_len)
     stats = exchange([own_stats] * groups, "seq")
     ctx_back = exchange(local_ctx, "seq")
     local_gq, grad_kv, grad_table = attend_grads(
-        counts, nbrs, partner, arrived, stats, kv, key_weight, value_weight, row_len, scale
+        lists, arrived, stats, kv, key_weight, value_weight, row_len, span_len
     )
     grad_encoded = lax.psum_scatter(
         grad_table.reshape(table_len, row_len, feat), "ret", scatter_dimension=0, tiled=True

time: 187 us -> 172 us (0.920)
  starting transfers between devices: 37.7 us -> 29.1 us
  Pallas kernels: 69.8 us -> 63.2 us
    ppermute x18 -> x15, starting transfers between devices: 37.7 us -> 29 us  [exchange(): lax.ppermute(pieces[d], axis, [(s, s ^ d) for s in range(size)])]
    pallas_call x4 -> x3, Pallas kernels: 41.8 us -> 34.8 us  [the longest x1 17.9 us: attend_grads(): pl.pallas_call(functools.partial(grads_kernel, groups, row_len, span_len)...]
    all_gather x1, waiting for transfers between devices: 32.6 us -> 35.8 us  [body(): lax.all_gather(encoded_own, 'ret', axis=0, tiled=True).reshape(-1, feat)]
    ppermute x18 -> x15, waiting for transfers between devices: 24.9 us -> 22.7 us  [exchange(): lax.ppermute(pieces[d], axis, [(s, s ^ d) for s in range(size)])]
  transfers between devices with their start and end apart: 20 -> 17, of which waited for: 10 -> 8; matrix products, arithmetic and copies ran while one was open for 2% -> 2% of each run, Pallas kernels for 26% -> 26%
where the time goes in v4:
time: 172 us
  Pallas kernels  63.2 us (37%)
  waiting for transfers between devices  60.5 us (35%)
  starting transfers between devices  29.1 us (17%)
  between operations  14.2 us (8%)
  local copies, waits for them, and re-layouts  5.22 us (3%)
    all_gather x1, waiting for transfers between devices, body(): lax.all_gather(encoded_own, 'ret', axis=0, tiled=True).reshape(-1, feat)  35.8 us
    ppermute x15, starting transfers between devices, exchange(): lax.ppermute(pieces[d], axis, [(s, s ^ d) for s in range(size)])  29 us
    ppermute x15, waiting for transfers between devices, exchange(): lax.ppermute(pieces[d], axis, [(s, s ^ d) for s in range(size)])  22.7 us
    pallas_call x1, Pallas kernels, attend_grads(): pl.pallas_call(functools.partial(grads_kernel, groups, row_len, span_len)...  17.9 us
    pallas_call x1, Pallas kernels, encode(): pl.pallas_call(encode_kernel, out_shape=jax.ShapeDtypeStruct(rows.shape,...  10 us
    pallas_call x1, Pallas kernels, grad_weights(): pl.pallas_call(functools.partial(weight_kernel, groups, len(waits)), out_...  8.98 us
    pallas_call x1, Pallas kernels, attend_local(): pl.pallas_call(functools.partial(local_kernel, groups, row_len, span_len)...  8.76 us
    pallas_call x1, Pallas kernels, project(): pl.pallas_call(functools.partial(project_kernel, row_len), grid=(rows //...  8.15 us
  transfers between devices with their start and end apart: 17, of which 8 were waited for; matrix products, arithmetic and copies ran while one was open for 2% of the time, Pallas kernels for 26%

profile of v4, /device:TPU:0, one launch (start us, length us, event | category | flops | bytes accessed | tf_op | source)
XLA Modules:
  0.0 172.5 jit_solution(15253763765309190409)
XLA Ops:
  7.2 0.0 all-gather.2.cloned.1.call-start
  7.2 10.0 %encode.1 = bf16[256,896]{1,0:T(8,128)(2,1)} custom-call(bf16[256,896]{1,0:T(8,128)(2,1)} %bitcast.10, bf16[896,3584]{1,0:T(8,128)(2,1)} %up_ref.1, bf16[3584,896]{1,0:T(8,128)(2,1)} %down_ref.1), custom_call_target="tpu_custom_call" | custom-call | flops 3288334336 | bytes 12845056 | tf_op jit(solution)/shard_map/encode/pallas_call | solution.py:90
  17.2 0.0 all-gather.2.cloned.1.call-update
  17.2 0.0 reduce-scatter.2.cloned.1.call-start
  17.3 5.0 %dispatch.1 = (bf16[1040,512]{1,0:T(8,128)(2,1)}, bf16[1040,512]{1,0:T(8,128)(2,1)}, bf16[1040,512]{1,0:T(8,128)(2,1)}, bf16[1040,512]{1,0:T(8,128)(2,1)}, s32[24]{0:T(128)}, /*index=5*/s32[24]{0:T(128)}) custom-call(s32[1]{0:T(128)} %bitcast.me, s32[2,12]{1,0:T(2,128)} %bitcast.11, s32[2,12]{1,0:T(2,128)} %bitcast.12, bf16[768,512]{1,0:T(8,128)(2,1)} %q_ref.1, ...), custom_call_target="tpu_custom_call" | custom-call | bytes 6291456 | tf_op jit(solution)/shard_map/dispatch/pallas_call | solution.py:208
  22.3 3.0 %collective-permute-start = (bf16[1040,512]{1,0:T(8,128)(2,1)}, bf16[1040,512]{1,0:T(8,128)(2,1)S(1)}, u32[]{:S(2)}, u32[]{:S(2)}) collective-permute-start(bf16[1040,512]{1,0:T(8,128)(2,1)} %get-tuple-element.32), channel_id=1, source_target_pairs={{0,8},{8,0},{16,24},{24,16},{1,9},{9,1},{17,25},{25,17},{2,10},{10... | collective-permute-start | bytes 3194888 | tf_op jit(solution)/shard_map/ppermute | solution.py:144
  25.3 1.5 collective-permute-start.1
  26.9 0.0 collective-permute-start.2
  26.9 35.8 %all-gather.2.cloned.1.call-done = bf16[16,128,896]{2,1,0:T(8,128)(2,1)} async-done(((bf16[2,128,896]{2,1,0:T(8,128)(2,1)}), bf16[16,128,896]{2,1,0:T(8,128)(2,1)}) %all-gather.2.cloned.1.call-update) | async-done | bytes 3670032 | tf_op jit(solution)/shard_map/all_gather | solution.py:686
  62.7 8.1 %project.1.refs_4_.refs_8_ = bf16[16,4,128,256]{3,2,1,0:T(8,128)(2,1)} custom-call(bf16[2048,896]{1,0:T(8,128)(2,1)} %bitcast.13, bf16[896,512]{1,0:T(8,128)(2,1)} %refs_9_.1, bf16[896,512]{1,0:T(8,128)(2,1)} %refs_10_.1), custom_call_target="tpu_custom_call" | custom-call | flops 7516192768 | bytes 7864320 | tf_op jit(solution)/shard_map/project/pallas_call | solution.py:125
  70.8 0.0 collective-permute-done.refs_1_
  70.8 2.5 %collective-permute-done.1.refs_2_ = bf16[1040,512]{1,0:T(8,128)(2,1)S(1)} collective-permute-done((bf16[1040,512]{1,0:T(8,128)(2,1)}, bf16[1040,512]{1,0:T(8,128)(2,1)S(1)}, u32[]{:S(2)}, u32[]{:S(2)}) %collective-permute-start.1) | collective-permute-done | bytes 1064992 | tf_op jit(solution)/shard_map/ppermute | solution.py:144
  73.4 0.0 collective-permute-done.2.refs_3_
  73.4 1.0 copy-done.13
  74.3 8.8 %attend_local.1 = (f32[32,2,256]{2,1,0:T(2,128)}, bf16[8,64,512]{2,1,0:T(8,128)(2,1)}, bf16[8,64,512]{2,1,0:T(8,128)(2,1)}, bf16[8,64,512]{2,1,0:T(8,128)(2,1)},...) custom-call(bf16[1040,512]{1,0:T(8,128)(2,1)} %get-tuple-element.31.refs_0_, ...), custom_call_target="tpu_custom_call" | custom-call | flops 6442450944 | bytes 10485760 | tf_op jit(solution)/shard_map/attend_local/pallas_call | solution.py:444
  83.1 5.4 %collective-permute-start.8 = (f32[32,2,256]{2,1,0:T(2,128)}, f32[32,2,256]{2,1,0:T(2,128)S(1)}, u32[]{:S(2)}, u32[]{:S(2)}) collective-permute-start(f32[32,2,256]{2,1,0:T(2,128)} %get-tuple-element.39.refs_4_), channel_id=1, source_target_pairs={{0,24},{8,16},{16,8},{24,0},{1,25},{9,17},{17,9},{25,1},{2,26},{10... | collective-permute-start | bytes 196616 | tf_op jit(solution)/shard_map/ppermute | solution.py:144
  88.5 0.3 collective-permute-start.7
  88.8 1.2 collective-permute-start.6
  90.0 0.9 collective-permute-start.3
  90.9 1.7 collective-permute-start.4
  92.6 0.0 collective-permute-done.8.refs_7_
  92.6 2.0 %collective-permute-start.5 = (bf16[8,64,512]{2,1,0:T(8,128)(2,1)}, bf16[8,64,512]{2,1,0:T(8,128)(2,1)S(1)}, u32[]{:S(2)}, u32[]{:S(2)}) collective-permute-start(bf16[8,64,512]{2,1,0:T(8,128)(2,1)} %get-tuple-element.38), channel_id=1, source_target_pairs={{0,24},{8,16},{16,8},{24,0},{1,25},{9,17},{17,9},{25,1},{2,26},{10... | collective-permute-start | bytes 1572872 | tf_op jit(solution)/shard_map/ppermute | solution.py:144
  94.6 0.0 collective-permute-done.6.refs_5_
  94.6 0.6 copy-done.4
  95.2 0.0 copy-done.6
  95.2 17.9 %attend_grads.1 = (bf16[8,64,512]{2,1,0:T(8,128)(2,1)}, bf16[8,64,512]{2,1,0:T(8,128)(2,1)}, bf16[8,64,512]{2,1,0:T(8,128)(2,1)}, bf16[8,64,512]{2,1,0:T(8,128)(...) custom-call(s32[4]{0:T(128)} %get-tuple-element.40.counts, s32[32]{0:T(128)} %get-tuple-element.41.nbrs, ...), custom_call_target="tpu_custom_call" | custom-call | flops 13421772800 | bytes 18350080 | tf_op jit(solution)/shard_map/attend_grads/pallas_call | solution.py:601
  113.2 0.0 reduce-scatter.2.cloned.1.call-update
  113.2 1.0 copy-done.16
  114.2 7.9 %collective-permute-start.9 = (bf16[8,64,512]{2,1,0:T(8,128)(2,1)S(1)}, bf16[8,64,512]{2,1,0:T(8,128)(2,1)S(1)}, u32[]{:S(2)}, u32[]{:S(2)}) collective-permute-start(bf16[8,64,512]{2,1,0:T(8,128)(2,1)S(1)} %copy-done.16), channel_id=1, source_target_pairs={{0,8},{8,0},{16,24},{24,16},{1,9},{9,1},{17,25},{25,17},{2,10},{10... | collective-permute-start | bytes 1572872 | tf_op jit(solution)/shard_map/ppermute | solution.py:144
  122.1 1.1 collective-permute-start.10
  123.2 0.5 collective-permute-start.11
  123.7 0.5 slice.20.refs_0_
  124.2 0.6 slice.21.refs_1_
  124.8 0.5 slice.22.refs_2_
  125.3 9.0 %grad_weights.1 = (bf16[224,1024]{1,0:T(8,128)(2,1)}, bf16[224,1024]{1,0:T(8,128)(2,1)}, bf16[224,1024]{1,0:T(8,128)(2,1)}, bf16[224,1024]{1,0:T(8,128)(2,1)}) custom-call(s32[1]{0:T(128)} %bitcast.me, bf16[2048,896]{1,0:T(8,128)(2,1)} %bitcast.14, bf16[2048,1024]{1,0:T(8,128)(2,1)} %get-tuple-element.48.dkv, bf16[1,1,8]{2,1,0:T(2,128)(2,1)} %slice.20.refs_0_, ...), custom_call_target="tpu_custom_call" | custom-call | flops 70000001024 | bytes 7864320 | tf_op jit(solution)/shard_map/grad_weights/pallas_call | solution.py:651
  134.3 1.9 %collective-permute-start.12 = (bf16[224,1024]{1,0:T(8,128)(2,1)}, bf16[224,1024]{1,0:T(8,128)(2,1)S(1)}, u32[]{:S(2)}, u32[]{:S(2)}) collective-permute-start(bf16[224,1024]{1,0:T(8,128)(2,1)} %get-tuple-element.50), channel_id=1, source_target_pairs={{0,8},{8,0},{16,24},{24,16},{1,9},{9,1},{17,25},{25,17},{2,10},{10... | collective-permute-start | bytes 1376264 | tf_op jit(solution)/shard_map/ppermute | solution.py:144
  136.2 1.1 collective-permute-start.13
  137.3 2.6 %combine_context.1 = bf16[768,512]{1,0:T(8,128)(2,1)} custom-call(s32[24]{0:T(128)S(1)} %copy-done.8, s32[24]{0:T(128)S(1)} %copy-done.9, bf16[8,64,512]{2,1,0:T(8,128)(2,1)S(1)} %copy-done, bf16[8,64,512]{2,1,0:T(8,128)(2,1)S(1)} %collective-permute-done.3.refs_1_, bf16[8,64,512]{2,1,0:T(8,128)(2,1)S(1)} %collective-permute-done.4.refs_2_, ...), custom_call_target="tpu_custom_call" | custom-call | flops 1572864 | bytes 2883584 | tf_op jit(solution)/shard_map/combine_context/pallas_call | solution.py:293
  139.9 0.5 collective-permute-start.14
  140.4 1.2 collective-permute-done.10.refs_2_
  141.7 5.6 %collective-permute-done.11.refs_3_ = bf16[8,64,512]{2,1,0:T(8,128)(2,1)S(1)} collective-permute-done((bf16[8,64,512]{2,1,0:T(8,128)(2,1)S(1)}, bf16[8,64,512]{2,1,0:T(8,128)(2,1)S(1)}, u32[]{:S(2)}, u32[]{:S(2)}) %collective-permute-start.11) | collective-permute-done | bytes 524320 | tf_op jit(solution)/shard_map/ppermute | solution.py:144
  147.3 1.8 %combine_grad_queries.1 = bf16[768,512]{1,0:T(8,128)(2,1)} custom-call(s32[24]{0:T(128)S(1)} %copy-done.8, bf16[8,64,512]{2,1,0:T(8,128)(2,1)S(1)} %copy-done.10, bf16[8,64,512]{2,1,0:T(8,128)(2,1)S(1)} %collective-permute-done.9.refs_1_, bf16[8,64,512]{2,1,0:T(8,128)(2,1)S(1)} %collective-permute-done.10.refs_2_, ...), custom_call_target="tpu_custom_call" | custom-call | flops 32000000000 | bytes 2883584 | tf_op jit(solution)/shard_map/combine_grad_queries/pallas_call | solution.py:250
  149.1 6.9 %collective-permute-done.12 = bf16[224,1024]{1,0:T(8,128)(2,1)S(1)} collective-permute-done((bf16[224,1024]{1,0:T(8,128)(2,1)}, bf16[224,1024]{1,0:T(8,128)(2,1)S(1)}, u32[]{:S(2)}, u32[]{:S(2)}) %collective-permute-start.12) | collective-permute-done | bytes 458784 | tf_op jit(solution)/shard_map/ppermute | solution.py:144
  156.0 5.3 %collective-permute-done.13 = bf16[224,1024]{1,0:T(8,128)(2,1)S(1)} collective-permute-done((bf16[224,1024]{1,0:T(8,128)(2,1)}, bf16[224,1024]{1,0:T(8,128)(2,1)S(1)}, u32[]{:S(2)}, u32[]{:S(2)}) %collective-permute-start.13) | collective-permute-done | bytes 458784 | tf_op jit(solution)/shard_map/ppermute | solution.py:144
  161.3 1.1 collective-permute-done.14
  162.4 0.3 convert_add_fusion
  162.7 1.0 fusion
  163.7 1.9 %reduce-scatter.2.cloned.1.call-done = bf16[2,128,896]{2,1,0:T(8,128)(2,1)} async-done(((bf16[16,128,896]{2,1,0:T(8,128)(2,1)}), bf16[2,128,896]{2,1,0:T(8,128)(2,1)}) %reduce-scatter.2.cloned.1.call-update) | async-done | bytes 458768 | tf_op jit(solution)/shard_map/reduce_scatter | solution.py:698
  (37 shorter events, 0.1 us)
Async XLA Ops:
  7.2 55.5 %all-gather.2.cloned.1.call-start = ((), (), s32[]{:S(2)}) async-start(), calls=%async_computation.1 | async-start | bytes 4128768 | tf_op jit(solution)/shard_map/all_gather | solution.py:686
  17.2 148.4 %reduce-scatter.2.cloned.1.call-start = ((), (), s32[]{:S(2)}) async-start(), calls=%async_computation.2 | async-start | bytes 4128768 | tf_op jit(solution)/shard_map/reduce_scatter | solution.py:698
  22.3 48.5 %collective-permute-start = (bf16[1040,512]{1,0:T(8,128)(2,1)}, bf16[1040,512]{1,0:T(8,128)(2,1)S(1)}, u32[]{:S(2)}, u32[]{:S(2)}) collective-permute-start(bf16[1040,512]{1,0:T(8,128)(2,1)} %get-tuple-element.32), channel_id=1, source_target_pairs={{0,8},{8,0},{16,24},{24,16},{1,9},{9,1},{17,25},{25,17},{2,10},{10... | collective-permute-start | bytes 3194888 | tf_op jit(solution)/shard_map/ppermute | solution.py:144
  25.3 48.0 %collective-permute-start.1 = (bf16[1040,512]{1,0:T(8,128)(2,1)}, bf16[1040,512]{1,0:T(8,128)(2,1)S(1)}, u32[]{:S(2)}, u32[]{:S(2)}) collective-permute-start(bf16[1040,512]{1,0:T(8,128)(2,1)} %get-tuple-element.33), channel_id=1, source_target_pairs={{0,16},{8,24},{16,0},{24,8},{1,17},{9,25},{17,1},{25,9},{2,18},{10... | collective-permute-start | bytes 3194888 | tf_op jit(solution)/shard_map/ppermute | solution.py:144
  26.9 46.5 %collective-permute-start.2 = (bf16[1040,512]{1,0:T(8,128)(2,1)}, bf16[1040,512]{1,0:T(8,128)(2,1)}, u32[]{:S(2)}, u32[]{:S(2)}) collective-permute-start(bf16[1040,512]{1,0:T(8,128)(2,1)} %get-tuple-element.34), channel_id=1, source_target_pairs={{0,24},{8,16},{16,8},{24,0},{1,25},{9,17},{17,9},{25,1},{2,26},{10... | collective-permute-start | bytes 3194888 | tf_op jit(solution)/shard_map/ppermute | solution.py:144
  70.8 2.5 %copy-start.12 = (bf16[1040,512]{1,0:T(8,128)(2,1)}, bf16[1040,512]{1,0:T(8,128)(2,1)S(1)}, u32[]{:S(2)}) copy-start(bf16[1040,512]{1,0:T(8,128)(2,1)S(1)} %collective-permute-done.refs_1_) | copy-start | bytes 3194884
  73.4 1.0 copy-start.13
  83.1 9.4 %collective-permute-start.8 = (f32[32,2,256]{2,1,0:T(2,128)}, f32[32,2,256]{2,1,0:T(2,128)S(1)}, u32[]{:S(2)}, u32[]{:S(2)}) collective-permute-start(f32[32,2,256]{2,1,0:T(2,128)} %get-tuple-element.39.refs_4_), channel_id=1, source_target_pairs={{0,24},{8,16},{16,8},{24,0},{1,25},{9,17},{17,9},{25,1},{2,26},{10... | collective-permute-start | bytes 196616 | tf_op jit(solution)/shard_map/ppermute | solution.py:144
  88.5 6.1 %collective-permute-start.7 = (f32[32,2,256]{2,1,0:T(2,128)}, f32[32,2,256]{2,1,0:T(2,128)S(1)}, u32[]{:S(2)}, u32[]{:S(2)}) collective-permute-start(f32[32,2,256]{2,1,0:T(2,128)} %get-tuple-element.39.refs_4_), channel_id=1, source_target_pairs={{0,16},{8,24},{16,0},{24,8},{1,17},{9,25},{17,1},{25,9},{2,18},{10... | collective-permute-start | bytes 196616 | tf_op jit(solution)/shard_map/ppermute | solution.py:144
  88.8 5.8 %collective-permute-start.6 = (f32[32,2,256]{2,1,0:T(2,128)}, f32[32,2,256]{2,1,0:T(2,128)S(1)}, u32[]{:S(2)}, u32[]{:S(2)}) collective-permute-start(f32[32,2,256]{2,1,0:T(2,128)} %get-tuple-element.39.refs_4_), channel_id=1, source_target_pairs={{0,8},{8,0},{16,24},{24,16},{1,9},{9,1},{17,25},{25,17},{2,10},{10... | collective-permute-start | bytes 196616 | tf_op jit(solution)/shard_map/ppermute | solution.py:144
  90.0 33.2 %collective-permute-start.3 = (bf16[8,64,512]{2,1,0:T(8,128)(2,1)}, bf16[8,64,512]{2,1,0:T(8,128)(2,1)S(1)}, u32[]{:S(2)}, u32[]{:S(2)}) collective-permute-start(bf16[8,64,512]{2,1,0:T(8,128)(2,1)} %get-tuple-element.36), channel_id=1, source_target_pairs={{0,8},{8,0},{16,24},{24,16},{1,9},{9,1},{17,25},{25,17},{2,10},{10... | collective-permute-start | bytes 1572872 | tf_op jit(solution)/shard_map/ppermute | solution.py:144
  90.9 33.4 %collective-permute-start.4 = (bf16[8,64,512]{2,1,0:T(8,128)(2,1)}, bf16[8,64,512]{2,1,0:T(8,128)(2,1)S(1)}, u32[]{:S(2)}, u32[]{:S(2)}) collective-permute-start(bf16[8,64,512]{2,1,0:T(8,128)(2,1)} %get-tuple-element.37), channel_id=1, source_target_pairs={{0,16},{8,24},{16,0},{24,8},{1,17},{9,25},{17,1},{25,9},{2,18},{10... | collective-permute-start | bytes 1572872 | tf_op jit(solution)/shard_map/ppermute | solution.py:144
  92.6 2.1 %copy-start.2 = (f32[32,2,256]{2,1,0:T(2,128)}, f32[32,2,256]{2,1,0:T(2,128)S(1)}, u32[]{:S(2)}) copy-start(f32[32,2,256]{2,1,0:T(2,128)S(1)} %collective-permute-done.8.refs_7_) | copy-start | bytes 196612
  92.6 32.2 %collective-permute-start.5 = (bf16[8,64,512]{2,1,0:T(8,128)(2,1)}, bf16[8,64,512]{2,1,0:T(8,128)(2,1)S(1)}, u32[]{:S(2)}, u32[]{:S(2)}) collective-permute-start(bf16[8,64,512]{2,1,0:T(8,128)(2,1)} %get-tuple-element.38), channel_id=1, source_target_pairs={{0,24},{8,16},{16,8},{24,0},{1,25},{9,17},{17,9},{25,1},{2,26},{10... | collective-permute-start | bytes 1572872 | tf_op jit(solution)/shard_map/ppermute | solution.py:144
  94.6 0.6 copy-start.4
  94.6 0.6 copy-start.6
  113.1 1.0 copy-start.16
  113.1 8.9 %copy-start.15 = (bf16[8,64,512]{2,1,0:T(8,128)(2,1)S(1)}, bf16[8,64,512]{2,1,0:T(8,128)(2,1)}, u32[]{:S(2)}) copy-start(bf16[8,64,512]{2,1,0:T(8,128)(2,1)} %get-tuple-element.45) | copy-start | bytes 1572868
  113.1 10.0 %copy-start.14 = (bf16[8,64,512]{2,1,0:T(8,128)(2,1)S(1)}, bf16[8,64,512]{2,1,0:T(8,128)(2,1)}, u32[]{:S(2)}) copy-start(bf16[8,64,512]{2,1,0:T(8,128)(2,1)} %get-tuple-element.46) | copy-start | bytes 1572868
  114.2 25.7 %collective-permute-start.9 = (bf16[8,64,512]{2,1,0:T(8,128)(2,1)S(1)}, bf16[8,64,512]{2,1,0:T(8,128)(2,1)S(1)}, u32[]{:S(2)}, u32[]{:S(2)}) collective-permute-start(bf16[8,64,512]{2,1,0:T(8,128)(2,1)S(1)} %copy-done.16), channel_id=1, source_target_pairs={{0,8},{8,0},{16,24},{24,16},{1,9},{9,1},{17,25},{25,17},{2,10},{10... | collective-permute-start | bytes 1572872 | tf_op jit(solution)/shard_map/ppermute | solution.py:144
  122.1 19.6 %collective-permute-start.10 = (bf16[8,64,512]{2,1,0:T(8,128)(2,1)S(1)}, bf16[8,64,512]{2,1,0:T(8,128)(2,1)S(1)}, u32[]{:S(2)}, u32[]{:S(2)}) collective-permute-start(bf16[8,64,512]{2,1,0:T(8,128)(2,1)S(1)} %copy-done.15), channel_id=1, source_target_pairs={{0,16},{8,24},{16,0},{24,8},{1,17},{9,25},{17,1},{25,9},{2,18},{10... | collective-permute-start | bytes 1572872 | tf_op jit(solution)/shard_map/ppermute | solution.py:144
  123.2 24.1 %collective-permute-start.11 = (bf16[8,64,512]{2,1,0:T(8,128)(2,1)S(1)}, bf16[8,64,512]{2,1,0:T(8,128)(2,1)S(1)}, u32[]{:S(2)}, u32[]{:S(2)}) collective-permute-start(bf16[8,64,512]{2,1,0:T(8,128)(2,1)S(1)} %copy-done.14), channel_id=1, source_target_pairs={{0,24},{8,16},{16,8},{24,0},{1,25},{9,17},{17,9},{25,1},{2,26},{10... | collective-permute-start | bytes 1572872 | tf_op jit(solution)/shard_map/ppermute | solution.py:144
  125.3 12.0 %copy-start = (bf16[8,64,512]{2,1,0:T(8,128)(2,1)S(1)}, bf16[8,64,512]{2,1,0:T(8,128)(2,1)}, u32[]{:S(2)}) copy-start(bf16[8,64,512]{2,1,0:T(8,128)(2,1)} %get-tuple-element.35.refs_0_) | copy-start | bytes 1572868
  125.3 12.0 %copy-start.1 = (f32[32,2,256]{2,1,0:T(2,128)S(1)}, f32[32,2,256]{2,1,0:T(2,128)}, u32[]{:S(2)}) copy-start(f32[32,2,256]{2,1,0:T(2,128)} %get-tuple-element.39.refs_4_) | copy-start | bytes 196612
  125.3 12.0 %copy-start.3 = (f32[32,2,256]{2,1,0:T(2,128)S(1)}, f32[32,2,256]{2,1,0:T(2,128)}, u32[]{:S(2)}) copy-start(f32[32,2,256]{2,1,0:T(2,128)} %copy-done.2) | copy-start | bytes 196612
  125.3 12.0 %copy-start.5 = (f32[32,2,256]{2,1,0:T(2,128)S(1)}, f32[32,2,256]{2,1,0:T(2,128)}, u32[]{:S(2)}) copy-start(f32[32,2,256]{2,1,0:T(2,128)} %copy-done.4) | copy-start | bytes 196612
  125.3 12.0 %copy-start.7 = (f32[32,2,256]{2,1,0:T(2,128)S(1)}, f32[32,2,256]{2,1,0:T(2,128)}, u32[]{:S(2)}) copy-start(f32[32,2,256]{2,1,0:T(2,128)} %copy-done.6) | copy-start | bytes 196612
  125.3 12.0 %copy-start.8 = (s32[24]{0:T(128)S(1)}, s32[24]{0:T(128)}, u32[]{:S(2)}) copy-start(s32[24]{0:T(128)} %get-tuple-element.29.position) | copy-start | bytes 292
  125.3 12.0 %copy-start.9 = (s32[24]{0:T(128)S(1)}, s32[24]{0:T(128)}, u32[]{:S(2)}) copy-start(s32[24]{0:T(128)} %get-tuple-element.30.place) | copy-start | bytes 292
  134.3 21.7 %collective-permute-start.12 = (bf16[224,1024]{1,0:T(8,128)(2,1)}, bf16[224,1024]{1,0:T(8,128)(2,1)S(1)}, u32[]{:S(2)}, u32[]{:S(2)}) collective-permute-start(bf16[224,1024]{1,0:T(8,128)(2,1)} %get-tuple-element.50), channel_id=1, source_target_pairs={{0,8},{8,0},{16,24},{24,16},{1,9},{9,1},{17,25},{25,17},{2,10},{10... | collective-permute-start | bytes 1376264 | tf_op jit(solution)/shard_map/ppermute | solution.py:144
  136.2 25.2 %collective-permute-start.13 = (bf16[224,1024]{1,0:T(8,128)(2,1)}, bf16[224,1024]{1,0:T(8,128)(2,1)S(1)}, u32[]{:S(2)}, u32[]{:S(2)}) collective-permute-start(bf16[224,1024]{1,0:T(8,128)(2,1)} %get-tuple-element.51), channel_id=1, source_target_pairs={{0,16},{8,24},{16,0},{24,8},{1,17},{9,25},{17,1},{25,9},{2,18},{10... | collective-permute-start | bytes 1376264 | tf_op jit(solution)/shard_map/ppermute | solution.py:144
  137.3 2.6 %copy-start.17 = (bf16[224,1024]{1,0:T(8,128)(2,1)S(1)}, bf16[224,1024]{1,0:T(8,128)(2,1)}, u32[]{:S(2)}) copy-start(bf16[224,1024]{1,0:T(8,128)(2,1)} %get-tuple-element.52) | copy-start | bytes 1376260
  137.3 9.9 %copy-start.10 = (bf16[8,64,512]{2,1,0:T(8,128)(2,1)S(1)}, bf16[8,64,512]{2,1,0:T(8,128)(2,1)}, u32[]{:S(2)}) copy-start(bf16[8,64,512]{2,1,0:T(8,128)(2,1)} %get-tuple-element.43.refs_0_) | copy-start | bytes 1572868
  139.9 22.5 %collective-permute-start.14 = (bf16[224,1024]{1,0:T(8,128)(2,1)S(1)}, bf16[224,1024]{1,0:T(8,128)(2,1)S(1)}, u32[]{:S(2)}, u32[]{:S(2)}) collective-permute-start(bf16[224,1024]{1,0:T(8,128)(2,1)S(1)} %copy-done.17), channel_id=1, source_target_pairs={{0,24},{8,16},{16,8},{24,0},{1,25},{9,17},{17,9},{25,1},{2,26},{10... | collective-permute-start | bytes 1376264 | tf_op jit(solution)/shard_map/ppermute | solution.py:144
  147.3 15.2 %copy-start.11 = (bf16[224,1024]{1,0:T(8,128)(2,1)S(1)}, bf16[224,1024]{1,0:T(8,128)(2,1)}, u32[]{:S(2)}) copy-start(bf16[224,1024]{1,0:T(8,128)(2,1)} %get-tuple-element.49) | copy-start | bytes 1376260
Sparse Core Ops, SparseCore 0:
  17.4 45.2 all-gather.1
  113.3 52.2 reduce-scatter.1

commit v5 on v4

--- a/solution.py
+++ b/solution.py
@@ -10,7 +10,7 @@
 
 HD = 128
 HEADER = 16
-UNROLL = 4
+UNROLL = 8
 TAIL_FLOPS = 32000000000
 WEIGHT_FLOPS = 70000000000
 NT = (((1,), (1,)), ((), ()))
@@ -85,7 +85,7 @@
 def encode(neighbours, up_weight, down_weight):
     feat, hidden = up_weight.shape
     rows = neighbours.reshape(-1, feat)
-    block = 512 if hidden % 512 == 0 else hidden
+    block = 896 if hidden % 896 == 0 else hidden
     steps = hidden // block
     return pl.pallas_call(
         encode_kernel,
@@ -100,7 +100,7 @@
             pltpu.SemaphoreType.DMA((steps,)),
             pltpu.SemaphoreType.DMA((steps,)),
         ],
-        compiler_params=params(56),
+        compiler_params=params(62),
         cost_estimate=cost(4 * rows.shape[0] * feat * hidden, 4 * feat * hidden, rows.shape[0] * hidden),
         name="encode",
     )(rows, up_weight, down_weight).reshape(neighbours.shape)
@@ -150,9 +150,9 @@
 
 
 def dispatch_kernel(waits, me, group_ids, slot_ids, q_ref, g_ref, *refs):
-    out_refs, refs = refs[waits:-6], refs[-6:]
-    position, place, taken, held, info, sems = refs
-    groups, rows, _ = held.shape
+    out_refs, refs = refs[waits:-7], refs[-7:]
+    position, place, taken, info, header, sems, hsem = refs
+    groups, rows = len(out_refs), out_refs[0].shape[0]
     requests = position.shape[0]
     span_len = q_ref.shape[0] // (requests // 2)
     capacity = (rows - HEADER) // (2 * span_len)
@@ -169,9 +169,15 @@
         position[i] = offset * capacity + rank
         place[i] = offset * slots + offset * capacity + rank
         source = pl.ds(pl.multiple_of(span * span_len, span_len), span_len)
-        first = pl.multiple_of(rank * (2 * span_len), span_len)
-        held[offset, pl.ds(first, span_len), :] = q_ref[source, :]
-        held[offset, pl.ds(first + span_len, span_len), :] = g_ref[source, :]
+        for e, out_ref in enumerate(out_refs):
+
+            @pl.when(offset == e)
+            def _():
+                for half, ref in enumerate((q_ref, g_ref)):
+                    first = pl.multiple_of((2 * rank + half) * span_len, span_len)
+                    target = out_ref.at[pl.ds(first, span_len)]
+                    pltpu.make_async_copy(ref.at[source], target, sems.at[i, half]).start()
+
         return carry
 
     lax.fori_loop(0, requests, step, 0)
@@ -195,9 +201,19 @@
     lax.fori_loop(0, requests, note, 0)
     for d in range(groups):
         facts = jnp.where(kind == 3, taken[d], info[d]).astype(F32)
-        held[d, rows - HEADER :, :] = jnp.zeros((HEADER, held.shape[2]), BF16)
-        held[d, rows - HEADER :, :128] = facts.astype(BF16)
-    for copy in fetch([(held.at[d], ref) for d, ref in enumerate(out_refs)], sems):
+        header[d] = jnp.zeros(header.shape[1:], BF16)
+        header[d, :, :128] = facts.astype(BF16)
+    head_rows = pl.ds(rows - HEADER, HEADER)
+    headers = fetch([(header.at[d], ref.at[head_rows]) for d, ref in enumerate(out_refs)], hsem)
+
+    def drain(i, carry):
+        some = pl.ds(0, span_len)
+        for half, ref in enumerate((q_ref, g_ref)):
+            pltpu.make_async_copy(ref.at[some], out_refs[0].at[some], sems.at[i, half]).wait()
+        return carry
+
+    lax.fori_loop(0, requests, drain, 0)
+    for copy in headers:
         copy.wait()
 
 
@@ -209,15 +225,16 @@
         functools.partial(dispatch_kernel, len(waits)),
         out_shape=[jax.ShapeDtypeStruct(piece, BF16)] * groups
         + [jax.ShapeDtypeStruct((requests,), jnp.int32)] * 2,
-        in_specs=[smem()] * 3 + [vmem(), vmem()] + [anyspace()] * len(waits),
+        in_specs=[smem()] * 3 + [vmem()] * 2 + [anyspace()] * len(waits),
         out_specs=[anyspace()] * groups + [smem()] * 2,
         scratch_shapes=[
             pltpu.SMEM((groups,), jnp.int32),
-            pltpu.VMEM((groups, *piece), BF16),
             pltpu.VMEM((groups, HEADER, 128), jnp.int32),
+            pltpu.VMEM((groups, HEADER, width), BF16),
+            pltpu.SemaphoreType.DMA((requests, 2)),
             pltpu.SemaphoreType.DMA((groups,)),
         ],
-        compiler_params=params(56),
+        compiler_params=params(62),
         cost_estimate=cost(0, groups * capacity * span_len * width * 6),
         name="dispatch",
     )(me, group_ids, slot_ids, queries, grad_ctx, *waits)
@@ -370,6 +387,7 @@
     capacity = (rows - HEADER) // (2 * span_len)
     slots = groups * capacity
     pairs = heads // 2
+    unroll = min(UNROLL, capacity)
     factor = math.log2(math.e) / math.sqrt(HD)
     head_rows = pl.ds(rows - HEADER, HEADER)
     heads_in = fetch(
@@ -402,8 +420,8 @@
         arrival(qg, d, isem).wait()
 
         def step(i, carry):
-            for u in range(UNROLL):
-                k = jnp.minimum(UNROLL * i + u, counts[d] - 1)
+            for u in range(unroll):
+                k = jnp.minimum(unroll * i + u, counts[d] - 1)
                 j = d * capacity + k
                 q_diag, g_diag = diag[2 * u], diag[2 * u + 1]
                 fill_diagonal(q_diag, slot_rows(qg, d, 2 * k, span_len), heads, span_len)
@@ -421,7 +439,7 @@
                 store_heads(ctx.at[d], k, mm(turned, values, NN), span_len)
             return carry
 
-        lax.fori_loop(0, (counts[d] + UNROLL - 1) // UNROLL, step, 0)
+        lax.fori_loop(0, (counts[d] + unroll - 1) // unroll, step, 0)
         for e in range(groups):
 
             @pl.when(d == e)
@@ -461,7 +479,7 @@
             pltpu.SemaphoreType.DMA((groups + 1,)),
         ]
         + [pltpu.VMEM((lanes, 2 * HD), BF16)] * (2 * UNROLL),
-        compiler_params=params(56),
+        compiler_params=params(62),
         cost_estimate=cost(
             slots * 48 * row_len * lanes * HD,
             kv.size * 2 + slots * span_len * width * 6,
@@ -484,19 +502,21 @@
     heads = width // HD
     scale = 1.0 / math.sqrt(HD)
     pairs = heads // 2
+    unroll = min(UNROLL, capacity)
     factor = math.log2(math.e) * scale
     stats_in = fetch(
         [(ref, stats.at[pl.ds(d * slots, slots)]) for d, ref in enumerate(stat_refs)], ssem
     )
-    kv_in, kw_in, vw_in = fetch([(kv_ref, kv), (kw_ref, kw), (vw_ref, vw)], ksem)
+    (kv_in,) = fetch([(kv_ref, kv)], ksem)
     fetch([(ref, qg.at[d]) for d, ref in enumerate(qg_refs)], qsem)
+    kw_in, vw_in = fetch([(kw_ref, kw), (vw_ref, vw)], ksem.at[pl.ds(1, 2)])
     gq_out = [
         pltpu.make_async_copy(gq.at[d, pl.ds(0, capacity)], ref, osem.at[d])
         for d, ref in enumerate(gq_refs)
     ]
     for ref in diag:
         ref[...] = jnp.zeros_like(ref)
-    some = 2 if acc.shape[0] % 2 == 0 else 1
+    some = 4 if acc.shape[0] % 4 == 0 else 1
     block = some * row_len
     blocks = acc.shape[0] // some
 
@@ -515,8 +535,8 @@
         arrival(qg, d, qsem).wait()
 
         def step(i, carry):
-            for u in range(UNROLL):
-                place = UNROLL * i + u
+            for u in range(unroll):
+                place = unroll * i + u
                 live = place < counts[d]
                 k = jnp.minimum(place, counts[d] - 1)
                 j = d * capacity + k
@@ -544,7 +564,7 @@
                 acc[nbr, pairs:] += mm(on_diagonal(weights), g_diag[...], NN).reshape(shape)
             return carry
 
-        lax.fori_loop(0, (counts[d] + UNROLL - 1) // UNROLL, step, 0)
+        lax.fori_loop(0, (counts[d] + unroll - 1) // unroll, step, 0)
         for e in range(groups):
 
             @pl.when(d == e)
@@ -564,14 +584,18 @@
             pltpu.make_async_copy(dkv.at[b], dkv_ref.at[b], psem.at[i, 1]),
         )
 
-    def finish(i, carry):
+    def narrow(i, carry):
         b = rows_at(i)
         for p in range(2 * pairs):
             part_of = acc[pl.ds(i * some, some), p].reshape(block, 2 * HD)
             dkv[b, p * 2 * HD : (p + 1) * 2 * HD] = part_of.astype(BF16)
+        results(i)[1].start()
+        return carry
+
+    def finish(i, carry):
+        b = rows_at(i)
         part[b, :] = (mm(dkv[b, :width], kw[...], NT) + mm(dkv[b, width:], vw[...], NT)).astype(BF16)
-        for copy in results(i):
-            copy.start()
+        results(i)[0].start()
         return carry
 
     def drain(i, carry):
@@ -579,6 +603,7 @@
             copy.wait()
         return carry
 
+    lax.fori_loop(0, blocks, narrow, 0)
     lax.fori_loop(0, blocks, finish, 0)
     lax.fori_loop(0, blocks, drain, 0)
     for copy in gq_out:
@@ -624,7 +649,7 @@
             pltpu.SemaphoreType.DMA((kv.shape[0], 2)),
         ]
         + [pltpu.VMEM((lanes, 2 * HD), BF16)] * (2 * UNROLL),
-        compiler_params=params(56),
+        compiler_params=params(62),
         cost_estimate=cost(
             4 * rows * feat * width + slots * 72 * row_len * lanes * HD,
             rows * feat * 2 + rows * width * 8 + slots * span_len * width * 6,
@@ -654,7 +679,7 @@
         in_specs=[smem(), vmem(), vmem()] + [anyspace()] * len(waits),
         out_specs=[vmem()] * groups,
         scratch_shapes=[pltpu.VMEM((groups, feat // groups, columns), BF16)],
-        compiler_params=params(56),
+        compiler_params=params(62),
         cost_estimate=cost(WEIGHT_FLOPS, table.size * 2 + grad_kv.size * 2),
         name="grad_weights",
     )(me, table, grad_kv, *waits)

time: 172 us -> 168 us (0.977)
  starting transfers between devices: 29.1 us -> 19.6 us
  Pallas kernels: 63.2 us -> 70.6 us
  waiting for transfers between devices: 60.5 us -> 58.2 us
    ppermute x15, starting transfers between devices: 29 us -> 19.5 us  [exchange(): lax.ppermute(pieces[d], axis, [(s, s ^ d) for s in range(size)])]
    pallas_call x1, Pallas kernels: 17.9 us -> 22.9 us  [attend_grads(): pl.pallas_call(functools.partial(grads_kernel, groups, row_len, span_len)...]
    pallas_call x1, Pallas kernels: 8.76 us -> 11.8 us  [attend_local(): pl.pallas_call(functools.partial(local_kernel, groups, row_len, span_len)...]
    ppermute x15, waiting for transfers between devices: 22.7 us -> 20.8 us  [exchange(): lax.ppermute(pieces[d], axis, [(s, s ^ d) for s in range(size)])]
  transfers between devices with their start and end apart: 17 -> 17, of which waited for: 8 -> 7; matrix products, arithmetic and copies ran while one was open for 2% -> 2% of each run, Pallas kernels for 26% -> 29%
where the time goes in v5:
time: 168 us
  Pallas kernels  70.6 us (42%)
  waiting for transfers between devices  58.2 us (35%)
  starting transfers between devices  19.6 us (12%)
  between operations  14.2 us (8%)
  local copies, waits for them, and re-layouts  5.17 us (3%)
    all_gather x1, waiting for transfers between devices, body(): lax.all_gather(encoded_own, 'ret', axis=0, tiled=True).reshape(-1, feat)  36.7 us
    pallas_call x1, Pallas kernels, attend_grads(): pl.pallas_call(functools.partial(grads_kernel, groups, row_len, span_len)...  22.9 us
    ppermute x15, waiting for transfers between devices, exchange(): lax.ppermute(pieces[d], axis, [(s, s ^ d) for s in range(size)])  20.8 us
    ppermute x15, starting transfers between devices, exchange(): lax.ppermute(pieces[d], axis, [(s, s ^ d) for s in range(size)])  19.5 us
    pallas_call x1, Pallas kernels, attend_local(): pl.pallas_call(functools.partial(local_kernel, groups, row_len, span_len)...  11.8 us
    pallas_call x1, Pallas kernels, encode(): pl.pallas_call(encode_kernel, out_shape=jax.ShapeDtypeStruct(rows.shape,...  9.46 us
    pallas_call x1, Pallas kernels, grad_weights(): pl.pallas_call(functools.partial(weight_kernel, groups, len(waits)), out_...  8.77 us
    pallas_call x1, Pallas kernels, project(): pl.pallas_call(functools.partial(project_kernel, row_len), grid=(rows //...  8.22 us
  transfers between devices with their start and end apart: 17, of which 7 were waited for; matrix products, arithmetic and copies ran while one was open for 2% of the time, Pallas kernels for 29%

profile of v5, /device:TPU:0, one launch (start us, length us, event | category | flops | bytes accessed | tf_op | source)
XLA Modules:
  0.0 168.1 jit_solution(8695919867607563994)
XLA Ops:
  7.2 0.0 all-gather.2.cloned.1.call-start
  7.2 9.5 %encode.1 = bf16[256,896]{1,0:T(8,128)(2,1)} custom-call(bf16[256,896]{1,0:T(8,128)(2,1)} %bitcast.10, bf16[896,3584]{1,0:T(8,128)(2,1)} %up_ref.1, bf16[3584,896]{1,0:T(8,128)(2,1)} %down_ref.1), custom_call_target="tpu_custom_call" | custom-call | flops 3288334336 | bytes 12845056 | tf_op jit(solution)/shard_map/encode/pallas_call | solution.py:90
  16.7 0.0 all-gather.2.cloned.1.call-update
  16.7 0.0 reduce-scatter.2.cloned.1.call-start
  16.8 4.1 %dispatch.1 = (bf16[1040,512]{1,0:T(8,128)(2,1)}, bf16[1040,512]{1,0:T(8,128)(2,1)}, bf16[1040,512]{1,0:T(8,128)(2,1)}, bf16[1040,512]{1,0:T(8,128)(2,1)}, s32[24]{0:T(128)}, /*index=5*/s32[24]{0:T(128)}) custom-call(s32[1]{0:T(128)} %bitcast.me, s32[2,12]{1,0:T(2,128)} %bitcast.11, s32[2,12]{1,0:T(2,128)} %bitcast.12, bf16[768,512]{1,0:T(8,128)(2,1)} %q_ref.1, ...), custom_call_target="tpu_custom_call" | custom-call | bytes 6291456 | tf_op jit(solution)/shard_map/dispatch/pallas_call | solution.py:224
  20.9 3.0 %collective-permute-start = (bf16[1040,512]{1,0:T(8,128)(2,1)}, bf16[1040,512]{1,0:T(8,128)(2,1)S(1)}, u32[]{:S(2)}, u32[]{:S(2)}) collective-permute-start(bf16[1040,512]{1,0:T(8,128)(2,1)} %get-tuple-element.32), channel_id=1, source_target_pairs={{0,8},{8,0},{16,24},{24,16},{1,9},{9,1},{17,25},{25,17},{2,10},{10... | collective-permute-start | bytes 3194888 | tf_op jit(solution)/shard_map/ppermute | solution.py:144
  23.9 1.6 collective-permute-start.1
  25.5 36.7 %all-gather.2.cloned.1.call-done = bf16[16,128,896]{2,1,0:T(8,128)(2,1)} async-done(((bf16[2,128,896]{2,1,0:T(8,128)(2,1)}), bf16[16,128,896]{2,1,0:T(8,128)(2,1)}) %all-gather.2.cloned.1.call-update) | async-done | bytes 3670032 | tf_op jit(solution)/shard_map/all_gather | solution.py:711
  62.2 8.2 %project.1.refs_4_.refs_8_ = bf16[16,4,128,256]{3,2,1,0:T(8,128)(2,1)} custom-call(bf16[2048,896]{1,0:T(8,128)(2,1)} %bitcast.13, bf16[896,512]{1,0:T(8,128)(2,1)} %refs_9_.1, bf16[896,512]{1,0:T(8,128)(2,1)} %refs_10_.1), custom_call_target="tpu_custom_call" | custom-call | flops 7516192768 | bytes 7864320 | tf_op jit(solution)/shard_map/project/pallas_call | solution.py:125
  70.4 0.0 collective-permute-done.refs_1_
  70.4 1.6 collective-permute-done.1.refs_2_
  72.0 11.8 %attend_local.1 = (f32[32,2,256]{2,1,0:T(2,128)}, bf16[8,64,512]{2,1,0:T(8,128)(2,1)}, bf16[8,64,512]{2,1,0:T(8,128)(2,1)}, bf16[8,64,512]{2,1,0:T(8,128)(2,1)},...) custom-call(bf16[1040,512]{1,0:T(8,128)(2,1)} %get-tuple-element.31.refs_0_, ...), custom_call_target="tpu_custom_call" | custom-call | flops 6442450944 | bytes 10485760 | tf_op jit(solution)/shard_map/attend_local/pallas_call | solution.py:462
  83.8 1.9 %collective-permute-start.8 = (f32[32,2,256]{2,1,0:T(2,128)}, f32[32,2,256]{2,1,0:T(2,128)S(1)}, u32[]{:S(2)}, u32[]{:S(2)}) collective-permute-start(f32[32,2,256]{2,1,0:T(2,128)} %get-tuple-element.39.refs_4_), channel_id=1, source_target_pairs={{0,24},{8,16},{16,8},{24,0},{1,25},{9,17},{17,9},{25,1},{2,26},{10... | collective-permute-start | bytes 196616 | tf_op jit(solution)/shard_map/ppermute | solution.py:144
  85.6 1.0 collective-permute-start.7
  86.6 0.7 collective-permute-start.6
  87.3 1.3 collective-permute-start.3
  88.6 1.0 collective-permute-start.4
  89.7 0.0 collective-permute-done.8.refs_7_
  89.7 2.0 %collective-permute-start.5 = (bf16[8,64,512]{2,1,0:T(8,128)(2,1)}, bf16[8,64,512]{2,1,0:T(8,128)(2,1)S(1)}, u32[]{:S(2)}, u32[]{:S(2)}) collective-permute-start(bf16[8,64,512]{2,1,0:T(8,128)(2,1)} %get-tuple-element.38), channel_id=1, source_target_pairs={{0,24},{8,16},{16,8},{24,0},{1,25},{9,17},{17,9},{25,1},{2,26},{10... | collective-permute-start | bytes 1572872 | tf_op jit(solution)/shard_map/ppermute | solution.py:144
  91.6 0.0 collective-permute-done.7.refs_6_
  91.7 0.2 collective-permute-done.6.refs_5_
  91.9 0.4 copy-done.6
  92.3 0.2 copy-done.8
  92.5 22.9 %attend_grads.1 = (bf16[8,64,512]{2,1,0:T(8,128)(2,1)}, bf16[8,64,512]{2,1,0:T(8,128)(2,1)}, bf16[8,64,512]{2,1,0:T(8,128)(2,1)}, bf16[8,64,512]{2,1,0:T(8,128)(...) custom-call(s32[4]{0:T(128)} %get-tuple-element.40.counts, s32[32]{0:T(128)} %get-tuple-element.41.nbrs, ...), custom_call_target="tpu_custom_call" | custom-call | flops 13421772800 | bytes 18350080 | tf_op jit(solution)/shard_map/attend_grads/pallas_call | solution.py:626
  115.4 0.0 reduce-scatter.2.cloned.1.call-update
  115.4 1.2 collective-permute-start.9
  116.7 1.1 collective-permute-start.10
  117.7 0.0 collective-permute-done.3.refs_1_
  117.7 1.3 collective-permute-start.11
  119.0 0.6 slice.20.refs_0_
  119.6 0.0 collective-permute-done.4.refs_2_
  119.6 0.6 slice.21.refs_1_
  120.2 0.5 slice.22.refs_2_
  120.7 0.8 copy-done.1
  121.5 8.8 %grad_weights.1 = (bf16[224,1024]{1,0:T(8,128)(2,1)}, bf16[224,1024]{1,0:T(8,128)(2,1)}, bf16[224,1024]{1,0:T(8,128)(2,1)}, bf16[224,1024]{1,0:T(8,128)(2,1)}) custom-call(s32[1]{0:T(128)} %bitcast.me, bf16[2048,896]{1,0:T(8,128)(2,1)} %bitcast.14, bf16[2048,1024]{1,0:T(8,128)(2,1)} %get-tuple-element.48.dkv, bf16[1,1,8]{2,1,0:T(2,128)(2,1)} %slice.20.refs_0_, ...), custom_call_target="tpu_custom_call" | custom-call | flops 70000001024 | bytes 7864320 | tf_op jit(solution)/shard_map/grad_weights/pallas_call | solution.py:676
  130.3 1.4 collective-permute-start.12
  131.7 1.1 collective-permute-start.13
  132.8 0.0 copy-start.2
  132.8 1.0 copy-done.2
  133.8 2.6 %combine_context.1 = bf16[768,512]{1,0:T(8,128)(2,1)} custom-call(s32[24]{0:T(128)S(1)} %copy-done.10, s32[24]{0:T(128)S(1)} %copy-done.11, bf16[8,64,512]{2,1,0:T(8,128)(2,1)S(1)} %copy-done, bf16[8,64,512]{2,1,0:T(8,128)(2,1)S(1)} %collective-permute-done.3.refs_1_, bf16[8,64,512]{2,1,0:T(8,128)(2,1)S(1)} %collective-permute-done.4.refs_2_, ...), custom_call_target="tpu_custom_call" | custom-call | flops 1572864 | bytes 2883584 | tf_op jit(solution)/shard_map/combine_context/pallas_call | solution.py:310
  136.4 1.1 collective-permute-start.14
  137.5 4.9 %collective-permute-done.11.refs_3_ = bf16[8,64,512]{2,1,0:T(8,128)(2,1)} collective-permute-done((bf16[8,64,512]{2,1,0:T(8,128)(2,1)}, bf16[8,64,512]{2,1,0:T(8,128)(2,1)}, u32[]{:S(2)}, u32[]{:S(2)}) %collective-permute-start.11) | collective-permute-done | bytes 524320 | tf_op jit(solution)/shard_map/ppermute | solution.py:144
  142.4 2.7 %combine_grad_queries.1 = bf16[768,512]{1,0:T(8,128)(2,1)} custom-call(s32[24]{0:T(128)S(1)} %copy-done.10, bf16[8,64,512]{2,1,0:T(8,128)(2,1)S(1)} %copy-done.12, bf16[8,64,512]{2,1,0:T(8,128)(2,1)} %collective-permute-done.9.refs_1_, bf16[8,64,512]{2,1,0:T(8,128)(2,1)} %collective-permute-done.10.refs_2_, bf16[8,64,512]{2,1,0:T(8,128)(2,1)} %collective-permute-done.11.refs_3_), custom_call_target="tpu_custom_call" | custom-call | flops 32000000000 | bytes 2883584 | tf_op jit(solution)/shard_map/combine_grad_queries/pallas_call | solution.py:267
  145.1 6.5 %collective-permute-done.12 = bf16[224,1024]{1,0:T(8,128)(2,1)S(1)} collective-permute-done((bf16[224,1024]{1,0:T(8,128)(2,1)}, bf16[224,1024]{1,0:T(8,128)(2,1)S(1)}, u32[]{:S(2)}, u32[]{:S(2)}) %collective-permute-start.12) | collective-permute-done | bytes 458784 | tf_op jit(solution)/shard_map/ppermute | solution.py:144
  151.7 7.5 %collective-permute-done.13 = bf16[224,1024]{1,0:T(8,128)(2,1)S(1)} collective-permute-done((bf16[224,1024]{1,0:T(8,128)(2,1)}, bf16[224,1024]{1,0:T(8,128)(2,1)S(1)}, u32[]{:S(2)}, u32[]{:S(2)}) %collective-permute-start.13) | collective-permute-done | bytes 458784 | tf_op jit(solution)/shard_map/ppermute | solution.py:144
  159.2 0.3 convert_add_fusion
  159.5 1.0 fusion
  160.5 0.7 reduce-scatter.2.cloned.1.call-done
  (33 shorter events, 0.1 us)
Async XLA Ops:
  7.2 55.0 %all-gather.2.cloned.1.call-start = ((), (), s32[]{:S(2)}) async-start(), calls=%async_computation.1 | async-start | bytes 4128768 | tf_op jit(solution)/shard_map/all_gather | solution.py:711
  16.7 144.5 %reduce-scatter.2.cloned.1.call-start = ((), (), s32[]{:S(2)}) async-start(), calls=%async_computation.2 | async-start | bytes 4128768 | tf_op jit(solution)/shard_map/reduce_scatter | solution.py:723
  20.9 49.5 %collective-permute-start = (bf16[1040,512]{1,0:T(8,128)(2,1)}, bf16[1040,512]{1,0:T(8,128)(2,1)S(1)}, u32[]{:S(2)}, u32[]{:S(2)}) collective-permute-start(bf16[1040,512]{1,0:T(8,128)(2,1)} %get-tuple-element.32), channel_id=1, source_target_pairs={{0,8},{8,0},{16,24},{24,16},{1,9},{9,1},{17,25},{25,17},{2,10},{10... | collective-permute-start | bytes 3194888 | tf_op jit(solution)/shard_map/ppermute | solution.py:144
  23.9 48.1 %collective-permute-start.1 = (bf16[1040,512]{1,0:T(8,128)(2,1)}, bf16[1040,512]{1,0:T(8,128)(2,1)}, u32[]{:S(2)}, u32[]{:S(2)}) collective-permute-start(bf16[1040,512]{1,0:T(8,128)(2,1)} %get-tuple-element.33), channel_id=1, source_target_pairs={{0,16},{8,24},{16,0},{24,8},{1,17},{9,25},{17,1},{25,9},{2,18},{10... | collective-permute-start | bytes 3194888 | tf_op jit(solution)/shard_map/ppermute | solution.py:144
  25.5 46.5 %collective-permute-start.2 = (bf16[1040,512]{1,0:T(8,128)(2,1)}, bf16[1040,512]{1,0:T(8,128)(2,1)}, u32[]{:S(2)}, u32[]{:S(2)}) collective-permute-start(bf16[1040,512]{1,0:T(8,128)(2,1)} %get-tuple-element.34), channel_id=1, source_target_pairs={{0,24},{8,16},{16,8},{24,0},{1,25},{9,17},{17,9},{25,1},{2,26},{10... | collective-permute-start | bytes 3194888 | tf_op jit(solution)/shard_map/ppermute | solution.py:144
  70.4 1.6 copy-start.14
  83.8 5.9 %collective-permute-start.8 = (f32[32,2,256]{2,1,0:T(2,128)}, f32[32,2,256]{2,1,0:T(2,128)S(1)}, u32[]{:S(2)}, u32[]{:S(2)}) collective-permute-start(f32[32,2,256]{2,1,0:T(2,128)} %get-tuple-element.39.refs_4_), channel_id=1, source_target_pairs={{0,24},{8,16},{16,8},{24,0},{1,25},{9,17},{17,9},{25,1},{2,26},{10... | collective-permute-start | bytes 196616 | tf_op jit(solution)/shard_map/ppermute | solution.py:144
  85.6 6.0 %collective-permute-start.7 = (f32[32,2,256]{2,1,0:T(2,128)}, f32[32,2,256]{2,1,0:T(2,128)S(1)}, u32[]{:S(2)}, u32[]{:S(2)}) collective-permute-start(f32[32,2,256]{2,1,0:T(2,128)} %get-tuple-element.39.refs_4_), channel_id=1, source_target_pairs={{0,16},{8,24},{16,0},{24,8},{1,17},{9,25},{17,1},{25,9},{2,18},{10... | collective-permute-start | bytes 196616 | tf_op jit(solution)/shard_map/ppermute | solution.py:144
  86.6 5.2 %collective-permute-start.6 = (f32[32,2,256]{2,1,0:T(2,128)}, f32[32,2,256]{2,1,0:T(2,128)S(1)}, u32[]{:S(2)}, u32[]{:S(2)}) collective-permute-start(f32[32,2,256]{2,1,0:T(2,128)} %get-tuple-element.39.refs_4_), channel_id=1, source_target_pairs={{0,8},{8,0},{16,24},{24,16},{1,9},{9,1},{17,25},{25,17},{2,10},{10... | collective-permute-start | bytes 196616 | tf_op jit(solution)/shard_map/ppermute | solution.py:144
  87.3 30.4 %collective-permute-start.3 = (bf16[8,64,512]{2,1,0:T(8,128)(2,1)}, bf16[8,64,512]{2,1,0:T(8,128)(2,1)S(1)}, u32[]{:S(2)}, u32[]{:S(2)}) collective-permute-start(bf16[8,64,512]{2,1,0:T(8,128)(2,1)} %get-tuple-element.36), channel_id=1, source_target_pairs={{0,8},{8,0},{16,24},{24,16},{1,9},{9,1},{17,25},{25,17},{2,10},{10... | collective-permute-start | bytes 1572872 | tf_op jit(solution)/shard_map/ppermute | solution.py:144
  88.6 31.0 %collective-permute-start.4 = (bf16[8,64,512]{2,1,0:T(8,128)(2,1)}, bf16[8,64,512]{2,1,0:T(8,128)(2,1)S(1)}, u32[]{:S(2)}, u32[]{:S(2)}) collective-permute-start(bf16[8,64,512]{2,1,0:T(8,128)(2,1)} %get-tuple-element.37), channel_id=1, source_target_pairs={{0,16},{8,24},{16,0},{24,8},{1,17},{9,25},{17,1},{25,9},{2,18},{10... | collective-permute-start | bytes 1572872 | tf_op jit(solution)/shard_map/ppermute | solution.py:144
  89.7 2.2 %copy-start.4 = (f32[32,2,256]{2,1,0:T(2,128)}, f32[32,2,256]{2,1,0:T(2,128)S(1)}, u32[]{:S(2)}) copy-start(f32[32,2,256]{2,1,0:T(2,128)S(1)} %collective-permute-done.8.refs_7_) | copy-start | bytes 196612
  89.7 30.5 %collective-permute-start.5 = (bf16[8,64,512]{2,1,0:T(8,128)(2,1)}, bf16[8,64,512]{2,1,0:T(8,128)(2,1)S(1)}, u32[]{:S(2)}, u32[]{:S(2)}) collective-permute-start(bf16[8,64,512]{2,1,0:T(8,128)(2,1)} %get-tuple-element.38), channel_id=1, source_target_pairs={{0,24},{8,16},{16,8},{24,0},{1,25},{9,17},{17,9},{25,1},{2,26},{10... | collective-permute-start | bytes 1572872 | tf_op jit(solution)/shard_map/ppermute | solution.py:144
  91.6 0.6 copy-start.6
  91.9 0.6 copy-start.8
  115.4 21.0 %collective-permute-start.9 = (bf16[8,64,512]{2,1,0:T(8,128)(2,1)}, bf16[8,64,512]{2,1,0:T(8,128)(2,1)}, u32[]{:S(2)}, u32[]{:S(2)}) collective-permute-start(bf16[8,64,512]{2,1,0:T(8,128)(2,1)} %get-tuple-element.44), channel_id=1, source_target_pairs={{0,8},{8,0},{16,24},{24,16},{1,9},{9,1},{17,25},{25,17},{2,10},{10... | collective-permute-start | bytes 1572872 | tf_op jit(solution)/shard_map/ppermute | solution.py:144
  116.7 20.8 %collective-permute-start.10 = (bf16[8,64,512]{2,1,0:T(8,128)(2,1)}, bf16[8,64,512]{2,1,0:T(8,128)(2,1)}, u32[]{:S(2)}, u32[]{:S(2)}) collective-permute-start(bf16[8,64,512]{2,1,0:T(8,128)(2,1)} %get-tuple-element.45), channel_id=1, source_target_pairs={{0,16},{8,24},{16,0},{24,8},{1,17},{9,25},{17,1},{25,9},{2,18},{10... | collective-permute-start | bytes 1572872 | tf_op jit(solution)/shard_map/ppermute | solution.py:144
  117.7 24.7 %collective-permute-start.11 = (bf16[8,64,512]{2,1,0:T(8,128)(2,1)}, bf16[8,64,512]{2,1,0:T(8,128)(2,1)}, u32[]{:S(2)}, u32[]{:S(2)}) collective-permute-start(bf16[8,64,512]{2,1,0:T(8,128)(2,1)} %get-tuple-element.46), channel_id=1, source_target_pairs={{0,24},{8,16},{16,8},{24,0},{1,25},{9,17},{17,9},{25,1},{2,26},{10... | collective-permute-start | bytes 1572872 | tf_op jit(solution)/shard_map/ppermute | solution.py:144
  120.7 0.8 copy-start.1
  121.5 11.2 %copy-start = (bf16[8,64,512]{2,1,0:T(8,128)(2,1)S(1)}, bf16[8,64,512]{2,1,0:T(8,128)(2,1)}, u32[]{:S(2)}) copy-start(bf16[8,64,512]{2,1,0:T(8,128)(2,1)} %get-tuple-element.35.refs_0_) | copy-start | bytes 1572868
  121.5 11.2 %copy-start.3 = (f32[32,2,256]{2,1,0:T(2,128)S(1)}, f32[32,2,256]{2,1,0:T(2,128)}, u32[]{:S(2)}) copy-start(f32[32,2,256]{2,1,0:T(2,128)} %get-tuple-element.39.refs_4_) | copy-start | bytes 196612
  121.5 11.2 %copy-start.5 = (f32[32,2,256]{2,1,0:T(2,128)S(1)}, f32[32,2,256]{2,1,0:T(2,128)}, u32[]{:S(2)}) copy-start(f32[32,2,256]{2,1,0:T(2,128)} %copy-done.4) | copy-start | bytes 196612
  121.5 11.2 %copy-start.7 = (f32[32,2,256]{2,1,0:T(2,128)S(1)}, f32[32,2,256]{2,1,0:T(2,128)}, u32[]{:S(2)}) copy-start(f32[32,2,256]{2,1,0:T(2,128)} %copy-done.6) | copy-start | bytes 196612
  121.5 11.2 %copy-start.9 = (f32[32,2,256]{2,1,0:T(2,128)S(1)}, f32[32,2,256]{2,1,0:T(2,128)}, u32[]{:S(2)}) copy-start(f32[32,2,256]{2,1,0:T(2,128)} %copy-done.8) | copy-start | bytes 196612
  121.5 11.2 %copy-start.10 = (s32[24]{0:T(128)S(1)}, s32[24]{0:T(128)}, u32[]{:S(2)}) copy-start(s32[24]{0:T(128)} %get-tuple-element.29.position) | copy-start | bytes 292
  121.5 11.2 %copy-start.11 = (s32[24]{0:T(128)S(1)}, s32[24]{0:T(128)}, u32[]{:S(2)}) copy-start(s32[24]{0:T(128)} %get-tuple-element.30.place) | copy-start | bytes 292
  130.3 21.4 %collective-permute-start.12 = (bf16[224,1024]{1,0:T(8,128)(2,1)}, bf16[224,1024]{1,0:T(8,128)(2,1)S(1)}, u32[]{:S(2)}, u32[]{:S(2)}) collective-permute-start(bf16[224,1024]{1,0:T(8,128)(2,1)} %get-tuple-element.50), channel_id=1, source_target_pairs={{0,8},{8,0},{16,24},{24,16},{1,9},{9,1},{17,25},{25,17},{2,10},{10... | collective-permute-start | bytes 1376264 | tf_op jit(solution)/shard_map/ppermute | solution.py:144
  131.7 27.5 %collective-permute-start.13 = (bf16[224,1024]{1,0:T(8,128)(2,1)}, bf16[224,1024]{1,0:T(8,128)(2,1)S(1)}, u32[]{:S(2)}, u32[]{:S(2)}) collective-permute-start(bf16[224,1024]{1,0:T(8,128)(2,1)} %get-tuple-element.51), channel_id=1, source_target_pairs={{0,16},{8,24},{16,0},{24,8},{1,17},{9,25},{17,1},{25,9},{2,18},{10... | collective-permute-start | bytes 1376264 | tf_op jit(solution)/shard_map/ppermute | solution.py:144
  132.8 1.1 copy-start.2
  133.8 2.6 %copy-start.15 = (bf16[224,1024]{1,0:T(8,128)(2,1)S(1)}, bf16[224,1024]{1,0:T(8,128)(2,1)}, u32[]{:S(2)}) copy-start(bf16[224,1024]{1,0:T(8,128)(2,1)} %get-tuple-element.52) | copy-start | bytes 1376260
  133.8 8.6 %copy-start.12 = (bf16[8,64,512]{2,1,0:T(8,128)(2,1)S(1)}, bf16[8,64,512]{2,1,0:T(8,128)(2,1)}, u32[]{:S(2)}) copy-start(bf16[8,64,512]{2,1,0:T(8,128)(2,1)} %get-tuple-element.43.refs_0_) | copy-start | bytes 1572868
  136.4 22.8 %collective-permute-start.14 = (bf16[224,1024]{1,0:T(8,128)(2,1)S(1)}, bf16[224,1024]{1,0:T(8,128)(2,1)S(1)}, u32[]{:S(2)}, u32[]{:S(2)}) collective-permute-start(bf16[224,1024]{1,0:T(8,128)(2,1)S(1)} %copy-done.15), channel_id=1, source_target_pairs={{0,24},{8,16},{16,8},{24,0},{1,25},{9,17},{17,9},{25,1},{2,26},{10... | collective-permute-start | bytes 1376264 | tf_op jit(solution)/shard_map/ppermute | solution.py:144
  142.4 16.8 %copy-start.13 = (bf16[224,1024]{1,0:T(8,128)(2,1)S(1)}, bf16[224,1024]{1,0:T(8,128)(2,1)}, u32[]{:S(2)}) copy-start(bf16[224,1024]{1,0:T(8,128)(2,1)} %get-tuple-element.49) | copy-start | bytes 1376260
Sparse Core Ops, SparseCore 0:
  16.8 45.2 all-gather.1
  115.6 45.6 reduce-scatter.1

commit v6 on v5

--- a/solution.py
+++ b/solution.py
@@ -11,6 +11,7 @@
 HD = 128
 HEADER = 16
 UNROLL = 8
+KV_COPIES = 4
 TAIL_FLOPS = 32000000000
 WEIGHT_FLOPS = 70000000000
 NT = (((1,), (1,)), ((), ()))
@@ -106,7 +107,8 @@
     )(rows, up_weight, down_weight).reshape(neighbours.shape)
 
 
-def project_kernel(row_len, table_ref, kw_ref, vw_ref, kv_ref):
+def project_kernel(row_len, table_ref, kw_ref, vw_ref, *refs):
+    kv_ref = refs[-1]
     pairs = kw_ref.shape[1] // (2 * HD)
     for first, weight in ((0, kw_ref), (pairs, vw_ref)):
         product = mm(table_ref[...], weight[...], NN).astype(BF16)
@@ -117,7 +119,7 @@
                 ]
 
 
-def project(table, key_weight, value_weight, row_len):
+def project(table, key_weight, value_weight, row_len, waits):
     rows, feat = table.shape
     width = key_weight.shape[1]
     block = 512 if rows % 512 == 0 else rows
@@ -130,12 +132,13 @@
             pl.BlockSpec((block, feat), lambda i: (i, 0)),
             pl.BlockSpec((feat, width), lambda i: (0, 0)),
             pl.BlockSpec((feat, width), lambda i: (0, 0)),
-        ],
+        ]
+        + [anyspace()] * len(waits),
         out_specs=pl.BlockSpec((block // row_len, blocks, row_len, 2 * HD), lambda i: (i, 0, 0, 0)),
         compiler_params=params(59),
         cost_estimate=cost(8 * rows * feat * width, rows * (feat + 2 * width) * 2),
         name="project",
-    )(table, key_weight, value_weight)
+    )(table, key_weight, value_weight, *waits)
 
 
 def exchange(pieces, axis):
@@ -372,6 +375,11 @@
     return shrink, 1.0 / jnp.where(scaled > 0.0, scaled, 1.0)
 
 
+def quarters(src, dst):
+    size = max(1, src.shape[0] // KV_COPIES)
+    return [(src.at[pl.ds(i, size)], dst.at[pl.ds(i, size)]) for i in range(0, src.shape[0], size)]
+
+
 def arrival(held, d, sems):
     return pltpu.make_async_copy(held.at[d], held.at[d], sems.at[d])
 
@@ -393,8 +401,8 @@
     heads_in = fetch(
         [(ref.at[head_rows, pl.ds(0, 128)], heads_up.at[d]) for d, ref in enumerate(qg_refs)], hsem
     )
-    kv_in = fetch([(kv_ref, kv)], ksem)
-    fetch([(ref, qg.at[d]) for d, ref in enumerate(qg_refs)], isem)
+    kv_in = fetch(quarters(kv_ref, kv), ksem)
+    fetch([(qg_refs[0], qg.at[0])], isem)
     ctx_out = [pltpu.make_async_copy(ctx.at[d], ref, osem.at[d]) for d, ref in enumerate(ctx_refs)]
     for copy in heads_in:
         copy.wait()
@@ -414,7 +422,9 @@
     lax.fori_loop(0, slots, unpack, 0)
     for d in range(groups):
         counts[d] = plain[d, 3, 0]
-    kv_in[0].wait()
+    for copy in kv_in:
+        copy.wait()
+    fetch([(ref, qg.at[d + 1]) for d, ref in enumerate(qg_refs[1:])], isem.at[pl.ds(1, groups - 1)])
 
     def one_group(d, carry):
         arrival(qg, d, isem).wait()
@@ -473,7 +483,7 @@
             pltpu.VMEM((groups, HEADER, 128), BF16),
             pltpu.VMEM((groups, HEADER, 128), jnp.int32),
             pltpu.SMEM((groups, HEADER, 128), jnp.int32),
-            pltpu.SemaphoreType.DMA((1,)),
+            pltpu.SemaphoreType.DMA((kv.shape[0],)),
             pltpu.SemaphoreType.DMA((groups,)),
             pltpu.SemaphoreType.DMA((groups,)),
             pltpu.SemaphoreType.DMA((groups + 1,)),
@@ -498,18 +508,13 @@
     diag = refs[14:]
     width = qg_refs[0].shape[1]
     capacity = gq_refs[0].shape[0]
-    slots = groups * capacity
     heads = width // HD
     scale = 1.0 / math.sqrt(HD)
     pairs = heads // 2
     unroll = min(UNROLL, capacity)
     factor = math.log2(math.e) * scale
-    stats_in = fetch(
-        [(ref, stats.at[pl.ds(d * slots, slots)]) for d, ref in enumerate(stat_refs)], ssem
-    )
-    (kv_in,) = fetch([(kv_ref, kv)], ksem)
-    fetch([(ref, qg.at[d]) for d, ref in enumerate(qg_refs)], qsem)
-    kw_in, vw_in = fetch([(kw_ref, kw), (vw_ref, vw)], ksem.at[pl.ds(1, 2)])
+    kv_in = fetch(quarters(kv_ref, kv), ksem)
+    fetch([(qg_refs[0], qg.at[0])], qsem)
     gq_out = [
         pltpu.make_async_copy(gq.at[d, pl.ds(0, capacity)], ref, osem.at[d])
         for d, ref in enumerate(gq_refs)
@@ -528,8 +533,11 @@
         return carry
 
     lax.fori_loop(0, acc.shape[0], clear, 0)
-    for copy in [*stats_in, kv_in]:
+    gather_groups(stat_refs, stats)
+    for copy in kv_in:
         copy.wait()
+    fetch([(ref, qg.at[d + 1]) for d, ref in enumerate(qg_refs[1:])], qsem.at[pl.ds(1, groups - 1)])
+    weights_in = fetch([(kw_ref, kw), (vw_ref, vw)], ssem)
 
     def one_group(d, carry):
         arrival(qg, d, qsem).wait()
@@ -574,8 +582,8 @@
         return carry
 
     lax.fori_loop(0, groups, one_group, 0)
-    kw_in.wait()
-    vw_in.wait()
+    for copy in weights_in:
+        copy.wait()
 
     def results(i):
         b = rows_at(i)
@@ -594,7 +602,7 @@
 
     def finish(i, carry):
         b = rows_at(i)
-        part[b, :] = (mm(dkv[b, :width], kw[...], NT) + mm(dkv[b, width:], vw[...], NT)).astype(BF16)
+        part[b, :] = (mm(dkv[b, :width], kw[...], NN) + mm(dkv[b, width:], vw[...], NN)).astype(BF16)
         results(i)[0].start()
         return carry
 
@@ -622,7 +630,7 @@
     slots = groups * capacity
     lanes = span_len * (width // HD)
     rows = kv.shape[0] * row_len
-    feat = key_weight.shape[0]
+    feat = key_weight.shape[1]
     outs = pl.pallas_call(
         functools.partial(grads_kernel, groups, row_len, span_len),
         out_shape=[jax.ShapeDtypeStruct((capacity, span_len, width), BF16)] * groups
@@ -630,21 +638,21 @@
             jax.ShapeDtypeStruct((rows, 2 * width), BF16),
             jax.ShapeDtypeStruct((rows, feat), BF16),
         ],
-        in_specs=[smem()] * 3 + [anyspace()] * (2 * groups + 3),
+        in_specs=[smem()] * 3 + [anyspace()] * groups + [vmem()] * groups + [anyspace()] * 3,
         out_specs=[anyspace()] * (groups + 2),
         scratch_shapes=[
             pltpu.VMEM(kv.shape, BF16),
             pltpu.VMEM((groups, *qg[0].shape), BF16),
             pltpu.VMEM((groups * slots, 2, lanes), F32),
-            pltpu.VMEM((feat, width), BF16),
-            pltpu.VMEM((feat, width), BF16),
+            pltpu.VMEM((width, feat), BF16),
+            pltpu.VMEM((width, feat), BF16),
             pltpu.VMEM((groups, capacity + 1, span_len, width), BF16),
             pltpu.VMEM(kv.shape, F32),
             pltpu.VMEM((rows, 2 * width), BF16),
             pltpu.VMEM((rows, feat), BF16),
-            pltpu.SemaphoreType.DMA((3,)),
+            pltpu.SemaphoreType.DMA((kv.shape[0],)),
             pltpu.SemaphoreType.DMA((groups,)),
-            pltpu.SemaphoreType.DMA((groups,)),
+            pltpu.SemaphoreType.DMA((2,)),
             pltpu.SemaphoreType.DMA((groups,)),
             pltpu.SemaphoreType.DMA((kv.shape[0], 2)),
         ]
@@ -713,12 +721,13 @@
         me, group_ids.T, slot_ids.T, queries, grad_ctx, groups, capacity, span_len, [encoded_own]
     )
     arrived = exchange(outgoing, "seq")
-    kv = project(table, key_weight, value_weight, row_len)
+    turned = [key_weight.T, value_weight.T]
+    kv = project(table, key_weight, value_weight, row_len, turned)
     own_stats, local_ctx, lists = attend_local(arrived, kv, row_len, span_len)
     stats = exchange([own_stats] * groups, "seq")
     ctx_back = exchange(local_ctx, "seq")
     local_gq, grad_kv, grad_table = attend_grads(
-        lists, arrived, stats, kv, key_weight, value_weight, row_len, span_len
+        lists, arrived, stats, kv, *turned, row_len, span_len
     )
     grad_encoded = lax.psum_scatter(
         grad_table.reshape(table_len, row_len, feat), "ret", scatter_dimension=0, tiled=True

time: 168 us -> 168 us (level)
  local copies, waits for them, and re-layouts: 5.17 us -> 7.75 us
  waiting for transfers between devices: 58.2 us -> 55.7 us
    all_gather x1, waiting for transfers between devices: 36.7 us -> 34.1 us  [body(): lax.all_gather(encoded_own, 'ret', axis=0, tiled=True).reshape(-1, feat)]
    unnamed x32 -> x38, local copies, waits for them, and re-layouts: 2.49 us -> 5.06 us
  transfers between devices with their start and end apart: 17 -> 17, of which waited for: 7 -> 7; matrix products, arithmetic and copies ran while one was open for 2% -> 3% of each run, Pallas kernels for 29% -> 29%
where the time goes in v6:
time: 168 us
  Pallas kernels  70.3 us (42%)
  waiting for transfers between devices  55.7 us (33%)
  starting transfers between devices  19.4 us (12%)
  between operations  14.2 us (8%)
  local copies, waits for them, and re-layouts  7.75 us (5%)
    all_gather x1, waiting for transfers between devices, body(): lax.all_gather(encoded_own, 'ret', axis=0, tiled=True).reshape(-1, feat)  34.1 us
    pallas_call x1, Pallas kernels, attend_grads(): pl.pallas_call(functools.partial(grads_kernel, groups, row_len, span_len)...  22.3 us
    ppermute x15, waiting for transfers between devices, exchange(): lax.ppermute(pieces[d], axis, [(s, s ^ d) for s in range(size)])  20.9 us
    ppermute x15, starting transfers between devices, exchange(): lax.ppermute(pieces[d], axis, [(s, s ^ d) for s in range(size)])  19.3 us
    pallas_call x1, Pallas kernels, attend_local(): pl.pallas_call(functools.partial(local_kernel, groups, row_len, span_len)...  11.9 us
    pallas_call x1, Pallas kernels, encode(): pl.pallas_call(encode_kernel, out_shape=jax.ShapeDtypeStruct(rows.shape,...  9.46 us
    pallas_call x1, Pallas kernels, grad_weights(): pl.pallas_call(functools.partial(weight_kernel, groups, len(waits)), out_...  8.77 us
    pallas_call x1, Pallas kernels, project(): pl.pallas_call(functools.partial(project_kernel, row_len), grid=(rows //...  8.23 us
  transfers between devices with their start and end apart: 17, of which 7 were waited for; matrix products, arithmetic and copies ran while one was open for 3% of the time, Pallas kernels for 29%

profile of v6, /device:TPU:0, one launch (start us, length us, event | category | flops | bytes accessed | tf_op | source)
XLA Modules:
  0.0 167.6 jit_solution(4916315662889956277)
XLA Ops:
  7.2 0.0 all-gather.2.cloned.1.call-start
  7.2 9.5 %encode.1 = bf16[256,896]{1,0:T(8,128)(2,1)} custom-call(bf16[256,896]{1,0:T(8,128)(2,1)} %bitcast.16, bf16[896,3584]{1,0:T(8,128)(2,1)} %up_ref.1, bf16[3584,896]{1,0:T(8,128)(2,1)} %down_ref.1), custom_call_target="tpu_custom_call" | custom-call | flops 3288334336 | bytes 12845056 | tf_op jit(solution)/shard_map/encode/pallas_call | solution.py:91
  16.7 0.0 all-gather.2.cloned.1.call-update
  16.7 0.0 copy-start.13
  16.7 0.0 reduce-scatter.2.cloned.1.call-start
  16.8 4.3 %dispatch.1 = (bf16[1040,512]{1,0:T(8,128)(2,1)}, bf16[1040,512]{1,0:T(8,128)(2,1)}, bf16[1040,512]{1,0:T(8,128)(2,1)}, bf16[1040,512]{1,0:T(8,128)(2,1)}, s32[24]{0:T(128)}, /*index=5*/s32[24]{0:T(128)}) custom-call(s32[1]{0:T(128)} %bitcast.me, s32[2,12]{1,0:T(2,128)} %bitcast.17, s32[2,12]{1,0:T(2,128)} %bitcast.18, bf16[768,512]{1,0:T(8,128)(2,1)} %q_ref.1, ...), custom_call_target="tpu_custom_call" | custom-call | bytes 6291456 | tf_op jit(solution)/shard_map/dispatch/pallas_call | solution.py:227
  21.0 0.0 copy-start.14
  21.1 2.9 %collective-permute-start = (bf16[1040,512]{1,0:T(8,128)(2,1)}, bf16[1040,512]{1,0:T(8,128)(2,1)S(1)}, u32[]{:S(2)}, u32[]{:S(2)}) collective-permute-start(bf16[1040,512]{1,0:T(8,128)(2,1)} %get-tuple-element.32), channel_id=1, source_target_pairs={{0,8},{8,0},{16,24},{24,16},{1,9},{9,1},{17,25},{25,17},{2,10},{10... | collective-permute-start | bytes 3194888 | tf_op jit(solution)/shard_map/ppermute | solution.py:147
  24.0 1.5 collective-permute-start.1
  25.5 0.1 collective-permute-start.2
  25.5 1.3 copy.16
  26.8 1.3 copy.17
  28.1 34.1 %all-gather.2.cloned.1.call-done = bf16[16,128,896]{2,1,0:T(8,128)(2,1)} async-done(((bf16[2,128,896]{2,1,0:T(8,128)(2,1)}), bf16[16,128,896]{2,1,0:T(8,128)(2,1)}) %all-gather.2.cloned.1.call-update) | async-done | bytes 3670032 | tf_op jit(solution)/shard_map/all_gather | solution.py:719
  62.2 8.2 %project.1.refs_4_.refs_8_ = bf16[16,4,128,256]{3,2,1,0:T(8,128)(2,1)} custom-call(bf16[2048,896]{1,0:T(8,128)(2,1)} %bitcast.19, bf16[896,512]{1,0:T(8,128)(2,1)} %kw_ref.1, bf16[896,512]{1,0:T(8,128)(2,1)} %vw_ref.1, bf16[512,896]{1,0:T(8,128)(2,1)} %bitcast.12, bf16[512,896]{1,0:T(8,128)(2,1)} %bitcast.14), custom_call_target="tpu_custom_call" | custom-call | flops 7516192768 | bytes 7864320 | tf_op jit(solution)/shard_map/project/pallas_call | solution.py:127
  70.4 1.7 %collective-permute-done.1.refs_2_ = bf16[1040,512]{1,0:T(8,128)(2,1)} collective-permute-done((bf16[1040,512]{1,0:T(8,128)(2,1)}, bf16[1040,512]{1,0:T(8,128)(2,1)}, u32[]{:S(2)}, u32[]{:S(2)}) %collective-permute-start.1) | collective-permute-done | bytes 1064992 | tf_op jit(solution)/shard_map/ppermute | solution.py:147
  72.1 11.9 %attend_local.1 = (f32[32,2,256]{2,1,0:T(2,128)}, bf16[8,64,512]{2,1,0:T(8,128)(2,1)}, bf16[8,64,512]{2,1,0:T(8,128)(2,1)}, bf16[8,64,512]{2,1,0:T(8,128)(2,1)},...) custom-call(bf16[1040,512]{1,0:T(8,128)(2,1)} %get-tuple-element.31.refs_0_, ...), custom_call_target="tpu_custom_call" | custom-call | flops 6442450944 | bytes 10485760 | tf_op jit(solution)/shard_map/attend_local/pallas_call | solution.py:472
  84.0 1.7 %collective-permute-start.8 = (f32[32,2,256]{2,1,0:T(2,128)}, f32[32,2,256]{2,1,0:T(2,128)S(1)}, u32[]{:S(2)}, u32[]{:S(2)}) collective-permute-start(f32[32,2,256]{2,1,0:T(2,128)} %get-tuple-element.39.refs_4_), channel_id=1, source_target_pairs={{0,24},{8,16},{16,8},{24,0},{1,25},{9,17},{17,9},{25,1},{2,26},{10... | collective-permute-start | bytes 196616 | tf_op jit(solution)/shard_map/ppermute | solution.py:147
  85.7 1.0 collective-permute-start.7
  86.8 0.8 collective-permute-start.6
  87.6 1.2 collective-permute-start.3
  88.8 1.0 collective-permute-start.4
  89.8 2.0 %collective-permute-start.5 = (bf16[8,64,512]{2,1,0:T(8,128)(2,1)}, bf16[8,64,512]{2,1,0:T(8,128)(2,1)S(1)}, u32[]{:S(2)}, u32[]{:S(2)}) collective-permute-start(bf16[8,64,512]{2,1,0:T(8,128)(2,1)} %get-tuple-element.38), channel_id=1, source_target_pairs={{0,24},{8,16},{16,8},{24,0},{1,25},{9,17},{17,9},{25,1},{2,26},{10... | collective-permute-start | bytes 1572872 | tf_op jit(solution)/shard_map/ppermute | solution.py:147
  91.8 0.2 collective-permute-done.6.refs_5_
  92.0 0.4 copy-done.6
  92.4 0.2 copy-done.8
  92.6 22.3 %attend_grads.1 = (bf16[8,64,512]{2,1,0:T(8,128)(2,1)}, bf16[8,64,512]{2,1,0:T(8,128)(2,1)}, bf16[8,64,512]{2,1,0:T(8,128)(2,1)}, bf16[8,64,512]{2,1,0:T(8,128)(...) custom-call(s32[4]{0:T(128)} %get-tuple-element.40.counts, s32[32]{0:T(128)} %get-tuple-element.41.nbrs, ...), custom_call_target="tpu_custom_call" | custom-call | flops 13421772800 | bytes 18350080 | tf_op jit(solution)/shard_map/attend_grads/pallas_call | solution.py:634
  114.9 0.0 reduce-scatter.2.cloned.1.call-update
  115.0 1.2 collective-permute-start.9
  116.2 1.1 collective-permute-start.10
  117.3 1.3 collective-permute-start.11
  118.5 0.5 slice.20.refs_0_
  119.1 0.6 slice.21.refs_1_
  119.6 0.6 slice.22.refs_2_
  120.2 0.8 copy-done.1
  121.1 8.8 %grad_weights.1 = (bf16[224,1024]{1,0:T(8,128)(2,1)}, bf16[224,1024]{1,0:T(8,128)(2,1)}, bf16[224,1024]{1,0:T(8,128)(2,1)}, bf16[224,1024]{1,0:T(8,128)(2,1)}) custom-call(s32[1]{0:T(128)} %bitcast.me, bf16[2048,896]{1,0:T(8,128)(2,1)} %bitcast.20, bf16[2048,1024]{1,0:T(8,128)(2,1)} %get-tuple-element.48.dkv, bf16[1,1,8]{2,1,0:T(2,128)(2,1)} %slice.20.refs_0_, ...), custom_call_target="tpu_custom_call" | custom-call | flops 70000001024 | bytes 7864320 | tf_op jit(solution)/shard_map/grad_weights/pallas_call | solution.py:684
  129.8 1.4 collective-permute-start.12
  131.2 1.1 collective-permute-start.13
  132.3 0.0 copy-start.2
  132.3 1.0 copy-done.2
  133.4 2.6 %combine_context.1 = bf16[768,512]{1,0:T(8,128)(2,1)} custom-call(s32[24]{0:T(128)S(1)} %copy-done.10, s32[24]{0:T(128)S(1)} %copy-done.11, bf16[8,64,512]{2,1,0:T(8,128)(2,1)S(1)} %copy-done, bf16[8,64,512]{2,1,0:T(8,128)(2,1)S(1)} %collective-permute-done.3.refs_1_, bf16[8,64,512]{2,1,0:T(8,128)(2,1)S(1)} %collective-permute-done.4.refs_2_, ...), custom_call_target="tpu_custom_call" | custom-call | flops 1572864 | bytes 2883584 | tf_op jit(solution)/shard_map/combine_context/pallas_call | solution.py:313
  135.9 1.1 collective-permute-start.14
  137.0 4.9 %collective-permute-done.11.refs_3_ = bf16[8,64,512]{2,1,0:T(8,128)(2,1)} collective-permute-done((bf16[8,64,512]{2,1,0:T(8,128)(2,1)}, bf16[8,64,512]{2,1,0:T(8,128)(2,1)}, u32[]{:S(2)}, u32[]{:S(2)}) %collective-permute-start.11) | collective-permute-done | bytes 524320 | tf_op jit(solution)/shard_map/ppermute | solution.py:147
  141.9 2.7 %combine_grad_queries.1 = bf16[768,512]{1,0:T(8,128)(2,1)} custom-call(s32[24]{0:T(128)S(1)} %copy-done.10, bf16[8,64,512]{2,1,0:T(8,128)(2,1)S(1)} %copy-done.12, bf16[8,64,512]{2,1,0:T(8,128)(2,1)} %collective-permute-done.9.refs_1_, bf16[8,64,512]{2,1,0:T(8,128)(2,1)} %collective-permute-done.10.refs_2_, bf16[8,64,512]{2,1,0:T(8,128)(2,1)} %collective-permute-done.11.refs_3_), custom_call_target="tpu_custom_call" | custom-call | flops 32000000000 | bytes 2883584 | tf_op jit(solution)/shard_map/combine_grad_queries/pallas_call | solution.py:270
  144.7 6.5 %collective-permute-done.12 = bf16[224,1024]{1,0:T(8,128)(2,1)S(1)} collective-permute-done((bf16[224,1024]{1,0:T(8,128)(2,1)}, bf16[224,1024]{1,0:T(8,128)(2,1)S(1)}, u32[]{:S(2)}, u32[]{:S(2)}) %collective-permute-start.12) | collective-permute-done | bytes 458784 | tf_op jit(solution)/shard_map/ppermute | solution.py:147
  151.2 7.5 %collective-permute-done.13 = bf16[224,1024]{1,0:T(8,128)(2,1)S(1)} collective-permute-done((bf16[224,1024]{1,0:T(8,128)(2,1)}, bf16[224,1024]{1,0:T(8,128)(2,1)S(1)}, u32[]{:S(2)}, u32[]{:S(2)}) %collective-permute-start.13) | collective-permute-done | bytes 458784 | tf_op jit(solution)/shard_map/ppermute | solution.py:147
  158.7 0.3 convert_add_fusion
  159.0 1.0 fusion
  160.0 0.7 reduce-scatter.2.cloned.1.call-done
  (39 shorter events, 0.1 us)
Async XLA Ops:
  7.2 55.0 %all-gather.2.cloned.1.call-start = ((), (), s32[]{:S(2)}) async-start(), calls=%async_computation.1 | async-start | bytes 4128768 | tf_op jit(solution)/shard_map/all_gather | solution.py:719
  16.7 8.8 %copy-start.13 = (bf16[896,512]{1,0:T(8,128)(2,1)S(1)}, bf16[896,512]{1,0:T(8,128)(2,1)}, u32[]{:S(2)}) copy-start(bf16[896,512]{1,0:T(8,128)(2,1)} %kw_ref.1) | copy-start | bytes 2752516
  16.7 144.0 %reduce-scatter.2.cloned.1.call-start = ((), (), s32[]{:S(2)}) async-start(), calls=%async_computation.2 | async-start | bytes 4128768 | tf_op jit(solution)/shard_map/reduce_scatter | solution.py:732
  21.0 5.8 %copy-start.14 = (bf16[896,512]{1,0:T(8,128)(2,1)S(1)}, bf16[896,512]{1,0:T(8,128)(2,1)}, u32[]{:S(2)}) copy-start(bf16[896,512]{1,0:T(8,128)(2,1)} %vw_ref.1) | copy-start | bytes 2752516
  21.1 49.3 %collective-permute-start = (bf16[1040,512]{1,0:T(8,128)(2,1)}, bf16[1040,512]{1,0:T(8,128)(2,1)S(1)}, u32[]{:S(2)}, u32[]{:S(2)}) collective-permute-start(bf16[1040,512]{1,0:T(8,128)(2,1)} %get-tuple-element.32), channel_id=1, source_target_pairs={{0,8},{8,0},{16,24},{24,16},{1,9},{9,1},{17,25},{25,17},{2,10},{10... | collective-permute-start | bytes 3194888 | tf_op jit(solution)/shard_map/ppermute | solution.py:147
  24.0 48.1 %collective-permute-start.1 = (bf16[1040,512]{1,0:T(8,128)(2,1)}, bf16[1040,512]{1,0:T(8,128)(2,1)}, u32[]{:S(2)}, u32[]{:S(2)}) collective-permute-start(bf16[1040,512]{1,0:T(8,128)(2,1)} %get-tuple-element.33), channel_id=1, source_target_pairs={{0,16},{8,24},{16,0},{24,8},{1,17},{9,25},{17,1},{25,9},{2,18},{10... | collective-permute-start | bytes 3194888 | tf_op jit(solution)/shard_map/ppermute | solution.py:147
  25.5 46.6 %collective-permute-start.2 = (bf16[1040,512]{1,0:T(8,128)(2,1)}, bf16[1040,512]{1,0:T(8,128)(2,1)}, u32[]{:S(2)}, u32[]{:S(2)}) collective-permute-start(bf16[1040,512]{1,0:T(8,128)(2,1)} %get-tuple-element.34), channel_id=1, source_target_pairs={{0,24},{8,16},{16,8},{24,0},{1,25},{9,17},{17,9},{25,1},{2,26},{10... | collective-permute-start | bytes 3194888 | tf_op jit(solution)/shard_map/ppermute | solution.py:147
  70.4 1.7 %copy-start.16 = (bf16[1040,512]{1,0:T(8,128)(2,1)}, bf16[1040,512]{1,0:T(8,128)(2,1)S(1)}, u32[]{:S(2)}) copy-start(bf16[1040,512]{1,0:T(8,128)(2,1)S(1)} %collective-permute-done.refs_1_) | copy-start | bytes 3194884
  84.0 5.8 %collective-permute-start.8 = (f32[32,2,256]{2,1,0:T(2,128)}, f32[32,2,256]{2,1,0:T(2,128)S(1)}, u32[]{:S(2)}, u32[]{:S(2)}) collective-permute-start(f32[32,2,256]{2,1,0:T(2,128)} %get-tuple-element.39.refs_4_), channel_id=1, source_target_pairs={{0,24},{8,16},{16,8},{24,0},{1,25},{9,17},{17,9},{25,1},{2,26},{10... | collective-permute-start | bytes 196616 | tf_op jit(solution)/shard_map/ppermute | solution.py:147
  85.7 6.0 %collective-permute-start.7 = (f32[32,2,256]{2,1,0:T(2,128)}, f32[32,2,256]{2,1,0:T(2,128)S(1)}, u32[]{:S(2)}, u32[]{:S(2)}) collective-permute-start(f32[32,2,256]{2,1,0:T(2,128)} %get-tuple-element.39.refs_4_), channel_id=1, source_target_pairs={{0,16},{8,24},{16,0},{24,8},{1,17},{9,25},{17,1},{25,9},{2,18},{10... | collective-permute-start | bytes 196616 | tf_op jit(solution)/shard_map/ppermute | solution.py:147
  86.8 5.2 %collective-permute-start.6 = (f32[32,2,256]{2,1,0:T(2,128)}, f32[32,2,256]{2,1,0:T(2,128)S(1)}, u32[]{:S(2)}, u32[]{:S(2)}) collective-permute-start(f32[32,2,256]{2,1,0:T(2,128)} %get-tuple-element.39.refs_4_), channel_id=1, source_target_pairs={{0,8},{8,0},{16,24},{24,16},{1,9},{9,1},{17,25},{25,17},{2,10},{10... | collective-permute-start | bytes 196616 | tf_op jit(solution)/shard_map/ppermute | solution.py:147
  87.6 29.7 %collective-permute-start.3 = (bf16[8,64,512]{2,1,0:T(8,128)(2,1)}, bf16[8,64,512]{2,1,0:T(8,128)(2,1)S(1)}, u32[]{:S(2)}, u32[]{:S(2)}) collective-permute-start(bf16[8,64,512]{2,1,0:T(8,128)(2,1)} %get-tuple-element.36), channel_id=1, source_target_pairs={{0,8},{8,0},{16,24},{24,16},{1,9},{9,1},{17,25},{25,17},{2,10},{10... | collective-permute-start | bytes 1572872 | tf_op jit(solution)/shard_map/ppermute | solution.py:147
  88.8 30.3 %collective-permute-start.4 = (bf16[8,64,512]{2,1,0:T(8,128)(2,1)}, bf16[8,64,512]{2,1,0:T(8,128)(2,1)S(1)}, u32[]{:S(2)}, u32[]{:S(2)}) collective-permute-start(bf16[8,64,512]{2,1,0:T(8,128)(2,1)} %get-tuple-element.37), channel_id=1, source_target_pairs={{0,16},{8,24},{16,0},{24,8},{1,17},{9,25},{17,1},{25,9},{2,18},{10... | collective-permute-start | bytes 1572872 | tf_op jit(solution)/shard_map/ppermute | solution.py:147
  89.8 2.2 %copy-start.4 = (f32[32,2,256]{2,1,0:T(2,128)}, f32[32,2,256]{2,1,0:T(2,128)S(1)}, u32[]{:S(2)}) copy-start(f32[32,2,256]{2,1,0:T(2,128)S(1)} %collective-permute-done.8.refs_7_) | copy-start | bytes 196612
  89.8 29.8 %collective-permute-start.5 = (bf16[8,64,512]{2,1,0:T(8,128)(2,1)}, bf16[8,64,512]{2,1,0:T(8,128)(2,1)S(1)}, u32[]{:S(2)}, u32[]{:S(2)}) collective-permute-start(bf16[8,64,512]{2,1,0:T(8,128)(2,1)} %get-tuple-element.38), channel_id=1, source_target_pairs={{0,24},{8,16},{16,8},{24,0},{1,25},{9,17},{17,9},{25,1},{2,26},{10... | collective-permute-start | bytes 1572872 | tf_op jit(solution)/shard_map/ppermute | solution.py:147
  91.8 0.6 copy-start.6
  92.0 0.6 copy-start.8
  115.0 21.0 %collective-permute-start.9 = (bf16[8,64,512]{2,1,0:T(8,128)(2,1)}, bf16[8,64,512]{2,1,0:T(8,128)(2,1)}, u32[]{:S(2)}, u32[]{:S(2)}) collective-permute-start(bf16[8,64,512]{2,1,0:T(8,128)(2,1)} %get-tuple-element.44), channel_id=1, source_target_pairs={{0,8},{8,0},{16,24},{24,16},{1,9},{9,1},{17,25},{25,17},{2,10},{10... | collective-permute-start | bytes 1572872 | tf_op jit(solution)/shard_map/ppermute | solution.py:147
  116.2 20.8 %collective-permute-start.10 = (bf16[8,64,512]{2,1,0:T(8,128)(2,1)}, bf16[8,64,512]{2,1,0:T(8,128)(2,1)}, u32[]{:S(2)}, u32[]{:S(2)}) collective-permute-start(bf16[8,64,512]{2,1,0:T(8,128)(2,1)} %get-tuple-element.45), channel_id=1, source_target_pairs={{0,16},{8,24},{16,0},{24,8},{1,17},{9,25},{17,1},{25,9},{2,18},{10... | collective-permute-start | bytes 1572872 | tf_op jit(solution)/shard_map/ppermute | solution.py:147
  117.3 24.7 %collective-permute-start.11 = (bf16[8,64,512]{2,1,0:T(8,128)(2,1)}, bf16[8,64,512]{2,1,0:T(8,128)(2,1)}, u32[]{:S(2)}, u32[]{:S(2)}) collective-permute-start(bf16[8,64,512]{2,1,0:T(8,128)(2,1)} %get-tuple-element.46), channel_id=1, source_target_pairs={{0,24},{8,16},{16,8},{24,0},{1,25},{9,17},{17,9},{25,1},{2,26},{10... | collective-permute-start | bytes 1572872 | tf_op jit(solution)/shard_map/ppermute | solution.py:147
  120.2 0.8 copy-start.1
  121.0 11.2 %copy-start = (bf16[8,64,512]{2,1,0:T(8,128)(2,1)S(1)}, bf16[8,64,512]{2,1,0:T(8,128)(2,1)}, u32[]{:S(2)}) copy-start(bf16[8,64,512]{2,1,0:T(8,128)(2,1)} %get-tuple-element.35.refs_0_) | copy-start | bytes 1572868
  121.0 11.3 %copy-start.3 = (f32[32,2,256]{2,1,0:T(2,128)S(1)}, f32[32,2,256]{2,1,0:T(2,128)}, u32[]{:S(2)}) copy-start(f32[32,2,256]{2,1,0:T(2,128)} %get-tuple-element.39.refs_4_) | copy-start | bytes 196612
  121.0 11.3 %copy-start.5 = (f32[32,2,256]{2,1,0:T(2,128)S(1)}, f32[32,2,256]{2,1,0:T(2,128)}, u32[]{:S(2)}) copy-start(f32[32,2,256]{2,1,0:T(2,128)} %copy-done.4) | copy-start | bytes 196612
  121.0 11.3 %copy-start.7 = (f32[32,2,256]{2,1,0:T(2,128)S(1)}, f32[32,2,256]{2,1,0:T(2,128)}, u32[]{:S(2)}) copy-start(f32[32,2,256]{2,1,0:T(2,128)} %copy-done.6) | copy-start | bytes 196612
  121.0 11.3 %copy-start.9 = (f32[32,2,256]{2,1,0:T(2,128)S(1)}, f32[32,2,256]{2,1,0:T(2,128)}, u32[]{:S(2)}) copy-start(f32[32,2,256]{2,1,0:T(2,128)} %copy-done.8) | copy-start | bytes 196612
  121.0 11.3 %copy-start.10 = (s32[24]{0:T(128)S(1)}, s32[24]{0:T(128)}, u32[]{:S(2)}) copy-start(s32[24]{0:T(128)} %get-tuple-element.29.position) | copy-start | bytes 292
  121.0 11.3 %copy-start.11 = (s32[24]{0:T(128)S(1)}, s32[24]{0:T(128)}, u32[]{:S(2)}) copy-start(s32[24]{0:T(128)} %get-tuple-element.30.place) | copy-start | bytes 292
  129.8 21.4 %collective-permute-start.12 = (bf16[224,1024]{1,0:T(8,128)(2,1)}, bf16[224,1024]{1,0:T(8,128)(2,1)S(1)}, u32[]{:S(2)}, u32[]{:S(2)}) collective-permute-start(bf16[224,1024]{1,0:T(8,128)(2,1)} %get-tuple-element.50), channel_id=1, source_target_pairs={{0,8},{8,0},{16,24},{24,16},{1,9},{9,1},{17,25},{25,17},{2,10},{10... | collective-permute-start | bytes 1376264 | tf_op jit(solution)/shard_map/ppermute | solution.py:147
  131.2 27.5 %collective-permute-start.13 = (bf16[224,1024]{1,0:T(8,128)(2,1)}, bf16[224,1024]{1,0:T(8,128)(2,1)S(1)}, u32[]{:S(2)}, u32[]{:S(2)}) collective-permute-start(bf16[224,1024]{1,0:T(8,128)(2,1)} %get-tuple-element.51), channel_id=1, source_target_pairs={{0,16},{8,24},{16,0},{24,8},{1,17},{9,25},{17,1},{25,9},{2,18},{10... | collective-permute-start | bytes 1376264 | tf_op jit(solution)/shard_map/ppermute | solution.py:147
  132.3 1.1 copy-start.2
  133.4 2.6 %copy-start.17 = (bf16[224,1024]{1,0:T(8,128)(2,1)S(1)}, bf16[224,1024]{1,0:T(8,128)(2,1)}, u32[]{:S(2)}) copy-start(bf16[224,1024]{1,0:T(8,128)(2,1)} %get-tuple-element.52) | copy-start | bytes 1376260
  133.4 8.6 %copy-start.12 = (bf16[8,64,512]{2,1,0:T(8,128)(2,1)S(1)}, bf16[8,64,512]{2,1,0:T(8,128)(2,1)}, u32[]{:S(2)}) copy-start(bf16[8,64,512]{2,1,0:T(8,128)(2,1)} %get-tuple-element.43.refs_0_) | copy-start | bytes 1572868
  135.9 22.8 %collective-permute-start.14 = (bf16[224,1024]{1,0:T(8,128)(2,1)S(1)}, bf16[224,1024]{1,0:T(8,128)(2,1)S(1)}, u32[]{:S(2)}, u32[]{:S(2)}) collective-permute-start(bf16[224,1024]{1,0:T(8,128)(2,1)S(1)} %copy-done.17), channel_id=1, source_target_pairs={{0,24},{8,16},{16,8},{24,0},{1,25},{9,17},{17,9},{25,1},{2,26},{10... | collective-permute-start | bytes 1376264 | tf_op jit(solution)/shard_map/ppermute | solution.py:147
  141.9 16.8 %copy-start.15 = (bf16[224,1024]{1,0:T(8,128)(2,1)S(1)}, bf16[224,1024]{1,0:T(8,128)(2,1)}, u32[]{:S(2)}) copy-start(bf16[224,1024]{1,0:T(8,128)(2,1)} %get-tuple-element.49) | copy-start | bytes 1376260
Sparse Core Ops, SparseCore 0:
  16.8 45.2 all-gather.1
  115.1 45.6 reduce-scatter.1

commit v7 on v6

--- a/solution.py
+++ b/solution.py
@@ -69,14 +69,20 @@
     normed[...] = (x * lax.rsqrt(jnp.mean(x * x, axis=-1, keepdims=True) + 1e-06)).astype(BF16)
     acc[...] = x
 
+    middle = min(512, block)
+    parts = [(0, middle), (middle, block)] if middle < block else [(0, block)]
+
     def step(i, carry):
         up_in, down_in = copies(i)
         up_in.wait()
-        h = mm(normed[...], up[i], NN)
-        inner = math.sqrt(2.0 / math.pi) * (h + 0.044715 * (h * h * h))
-        hidden = (0.5 * h * (1.0 + jnp.tanh(inner))).astype(BF16)
+        sums = [mm(normed[...], up[i, :, first:last], NN) for first, last in parts]
         down_in.wait()
-        acc[...] += mm(hidden, down[i], NN)
+        total = acc[...]
+        for h, (first, last) in zip(sums, parts):
+            inner = math.sqrt(2.0 / math.pi) * (h + 0.044715 * (h * h * h))
+            hidden = (0.5 * h * (1.0 + jnp.tanh(inner))).astype(BF16)
+            total += mm(hidden, down[i, first:last, :], NN)
+        acc[...] = total
         return carry
 
     lax.fori_loop(0, steps, step, 0)
@@ -101,7 +107,7 @@
             pltpu.SemaphoreType.DMA((steps,)),
             pltpu.SemaphoreType.DMA((steps,)),
         ],
-        compiler_params=params(62),
+        compiler_params=params(58),
         cost_estimate=cost(4 * rows.shape[0] * feat * hidden, 4 * feat * hidden, rows.shape[0] * hidden),
         name="encode",
     )(rows, up_weight, down_weight).reshape(neighbours.shape)
@@ -237,7 +243,7 @@
             pltpu.SemaphoreType.DMA((requests, 2)),
             pltpu.SemaphoreType.DMA((groups,)),
         ],
-        compiler_params=params(62),
+        compiler_params=params(16),
         cost_estimate=cost(0, groups * capacity * span_len * width * 6),
         name="dispatch",
     )(me, group_ids, slot_ids, queries, grad_ctx, *waits)

time: 168 us -> 170 us (1.012)
  local copies, waits for them, and re-layouts: 7.75 us -> 9.81 us
    all_gather x1, waiting for transfers between devices: 34.1 us -> 31.2 us  [body(): lax.all_gather(encoded_own, 'ret', axis=0, tiled=True).reshape(-1, feat)]
    unnamed x38 -> x42, local copies, waits for them, and re-layouts: 5.06 us -> 7.21 us
    ppermute x15, waiting for transfers between devices: 20.9 us -> 22.7 us  [exchange(): lax.ppermute(pieces[d], axis, [(s, s ^ d) for s in range(size)])]
  transfers between devices with their start and end apart: 17 -> 17, of which waited for: 7 -> 9; matrix products, arithmetic and copies ran while one was open for 3% -> 4% of each run, Pallas kernels for 29% -> 29%
where the time goes in v7:
time: 170 us; the launch traced here: 169 us
  Pallas kernels  70.5 us (41%)
  waiting for transfers between devices  56.1 us (33%)
  starting transfers between devices  18.4 us (11%)
  between operations  14.2 us (8%)
  local copies, waits for them, and re-layouts  9.81 us (6%)
    all_gather x1, waiting for transfers between devices, body(): lax.all_gather(encoded_own, 'ret', axis=0, tiled=True).reshape(-1, feat)  31.2 us
    ppermute x15, waiting for transfers between devices, exchange(): lax.ppermute(pieces[d], axis, [(s, s ^ d) for s in range(size)])  22.7 us
    pallas_call x1, Pallas kernels, attend_grads(): pl.pallas_call(functools.partial(grads_kernel, groups, row_len, span_len)...  22.5 us
    ppermute x15, starting transfers between devices, exchange(): lax.ppermute(pieces[d], axis, [(s, s ^ d) for s in range(size)])  18.3 us
    pallas_call x1, Pallas kernels, attend_local(): pl.pallas_call(functools.partial(local_kernel, groups, row_len, span_len)...  12 us
    pallas_call x1, Pallas kernels, encode(): pl.pallas_call(encode_kernel, out_shape=jax.ShapeDtypeStruct(rows.shape,...  9.29 us
    pallas_call x1, Pallas kernels, grad_weights(): pl.pallas_call(functools.partial(weight_kernel, groups, len(waits)), out_...  8.81 us
    pallas_call x1, Pallas kernels, project(): pl.pallas_call(functools.partial(project_kernel, row_len), grid=(rows //...  8.22 us
  transfers between devices with their start and end apart: 17, of which 9 were waited for; matrix products, arithmetic and copies ran while one was open for 4% of the time, Pallas kernels for 29%

profile of v7, /device:TPU:0, one launch (start us, length us, event | category | flops | bytes accessed | tf_op | source)
XLA Modules:
  0.0 169.3 jit_solution(3629298914473111388)
XLA Ops:
  7.2 0.0 all-gather.2.cloned.1.call-start
  7.3 9.3 %encode.1 = bf16[256,896]{1,0:T(8,128)(2,1)} custom-call(bf16[256,896]{1,0:T(8,128)(2,1)} %bitcast.18, bf16[896,3584]{1,0:T(8,128)(2,1)} %up_ref.1, bf16[3584,896]{1,0:T(8,128)(2,1)} %down_ref.1), custom_call_target="tpu_custom_call" | custom-call | flops 3288334336 | bytes 12845056 | tf_op jit(solution)/shard_map/encode/pallas_call | solution.py:97
  16.6 0.0 all-gather.2.cloned.1.call-update
  16.6 0.0 reduce-scatter.2.cloned.1.call-start
  16.7 0.0 copy-start
  16.7 1.0 copy-done
  17.7 4.3 %dispatch.1 = (bf16[1040,512]{1,0:T(8,128)(2,1)S(1)}, bf16[1040,512]{1,0:T(8,128)(2,1)}, bf16[1040,512]{1,0:T(8,128)(2,1)}, bf16[1040,512]{1,0:T(8,128)(2,1)}, s32[24]{0:T(128)S(1)}, /*index=5*/s32[24]{0:T(128)S(1)}) custom-call(s32[1]{0:T(128)} %bitcast.me, s32[2,12]{1,0:T(2,128)S(1)} %bitcast.11, s32[2,12]{1,0:T(2,128)S(1)} %bitcast.12, ...), custom_call_target="tpu_custom_call" | custom-call | bytes 6291456 | tf_op jit(solution)/shard_map/dispatch/pallas_call | solution.py:233
  22.1 3.5 %collective-permute-start = (bf16[1040,512]{1,0:T(8,128)(2,1)}, bf16[1040,512]{1,0:T(8,128)(2,1)}, u32[]{:S(2)}, u32[]{:S(2)}) collective-permute-start(bf16[1040,512]{1,0:T(8,128)(2,1)} %get-tuple-element.32), channel_id=1, source_target_pairs={{0,8},{8,0},{16,24},{24,16},{1,9},{9,1},{17,25},{25,17},{2,10},{10... | collective-permute-start | bytes 3194888 | tf_op jit(solution)/shard_map/ppermute | solution.py:153
  25.6 1.3 collective-permute-start.1
  26.9 0.2 collective-permute-start.2
  27.1 2.4 %copy.16 = bf16[896,512]{0,1:T(8,128)(2,1)} copy(bf16[896,512]{1,0:T(8,128)(2,1)} %kw_ref.1) | data formatting | bytes 1835008 | tf_op args[5]
  29.5 1.3 copy.17
  30.8 31.2 %all-gather.2.cloned.1.call-done = bf16[16,128,896]{2,1,0:T(8,128)(2,1)} async-done(((bf16[2,128,896]{2,1,0:T(8,128)(2,1)}), bf16[16,128,896]{2,1,0:T(8,128)(2,1)}) %all-gather.2.cloned.1.call-update) | async-done | bytes 3670032 | tf_op jit(solution)/shard_map/all_gather | solution.py:725
  62.0 8.2 %project.1.refs_4_.refs_8_ = bf16[16,4,128,256]{3,2,1,0:T(8,128)(2,1)} custom-call(bf16[2048,896]{1,0:T(8,128)(2,1)} %bitcast.19, bf16[896,512]{1,0:T(8,128)(2,1)} %kw_ref.1, bf16[896,512]{1,0:T(8,128)(2,1)} %vw_ref.1, bf16[512,896]{1,0:T(8,128)(2,1)} %bitcast.14, bf16[512,896]{1,0:T(8,128)(2,1)} %bitcast.16), custom_call_target="tpu_custom_call" | custom-call | flops 7516192768 | bytes 7864320 | tf_op jit(solution)/shard_map/project/pallas_call | solution.py:133
  70.3 3.4 %collective-permute-done.1.refs_2_ = bf16[1040,512]{1,0:T(8,128)(2,1)} collective-permute-done((bf16[1040,512]{1,0:T(8,128)(2,1)}, bf16[1040,512]{1,0:T(8,128)(2,1)}, u32[]{:S(2)}, u32[]{:S(2)}) %collective-permute-start.1) | collective-permute-done | bytes 1064992 | tf_op jit(solution)/shard_map/ppermute | solution.py:153
  73.7 12.0 %attend_local.1 = (f32[32,2,256]{2,1,0:T(2,128)}, bf16[8,64,512]{2,1,0:T(8,128)(2,1)}, bf16[8,64,512]{2,1,0:T(8,128)(2,1)}, bf16[8,64,512]{2,1,0:T(8,128)(2,1)},...) custom-call(bf16[1040,512]{1,0:T(8,128)(2,1)} %copy-done.15, ...), custom_call_target="tpu_custom_call" | custom-call | flops 6442450944 | bytes 10485760 | tf_op jit(solution)/shard_map/attend_local/pallas_call | solution.py:478
  85.7 1.2 collective-permute-start.8
  86.9 1.3 collective-permute-start.7
  88.3 1.0 collective-permute-start.6
  89.3 1.0 collective-permute-start.3
  90.3 0.7 collective-permute-start.4
  91.0 0.8 collective-permute-done.8.refs_7_
  91.8 0.9 collective-permute-start.5
  92.8 0.8 collective-permute-done.6.refs_5_
  93.5 0.6 copy-done.11
  94.1 22.5 %attend_grads.1 = (bf16[8,64,512]{2,1,0:T(8,128)(2,1)}, bf16[8,64,512]{2,1,0:T(8,128)(2,1)}, bf16[8,64,512]{2,1,0:T(8,128)(2,1)}, bf16[8,64,512]{2,1,0:T(8,128)(...) custom-call(s32[4]{0:T(128)} %get-tuple-element.40.counts, s32[32]{0:T(128)} %get-tuple-element.41.nbrs, ...), custom_call_target="tpu_custom_call" | custom-call | flops 13421772800 | bytes 18350080 | tf_op jit(solution)/shard_map/attend_grads/pallas_call | solution.py:640
  116.7 0.0 reduce-scatter.2.cloned.1.call-update
  116.7 1.2 collective-permute-start.9
  117.9 1.2 collective-permute-start.10
  119.1 1.2 collective-permute-start.11
  120.2 0.6 slice.20.refs_0_
  120.8 0.5 slice.21.refs_1_
  121.3 0.5 slice.22.refs_2_
  121.9 0.8 copy-done.4
  122.7 8.8 %grad_weights.1 = (bf16[224,1024]{1,0:T(8,128)(2,1)}, bf16[224,1024]{1,0:T(8,128)(2,1)}, bf16[224,1024]{1,0:T(8,128)(2,1)}, bf16[224,1024]{1,0:T(8,128)(2,1)}) custom-call(s32[1]{0:T(128)} %bitcast.me, bf16[2048,896]{1,0:T(8,128)(2,1)} %bitcast.20, bf16[2048,1024]{1,0:T(8,128)(2,1)} %get-tuple-element.48.dkv, bf16[1,1,8]{2,1,0:T(2,128)(2,1)} %slice.20.refs_0_, ...), custom_call_target="tpu_custom_call" | custom-call | flops 70000001024 | bytes 7864320 | tf_op jit(solution)/shard_map/grad_weights/pallas_call | solution.py:690
  131.5 1.3 collective-permute-start.12
  132.8 1.2 collective-permute-start.13
  134.0 1.0 copy-done.5
  135.1 2.6 %combine_context.1 = bf16[768,512]{1,0:T(8,128)(2,1)} custom-call(s32[24]{0:T(128)S(1)} %get-tuple-element.29.position, s32[24]{0:T(128)S(1)} %get-tuple-element.30.place, bf16[8,64,512]{2,1,0:T(8,128)(2,1)S(1)} %copy-done.3, bf16[8,64,512]{2,1,0:T(8,128)(2,1)S(1)} %collective-permute-done.3.refs_1_, bf16[8,64,512]{2,1,0:T(8,128)(2,1)S(1)} %collective-permute-done.4.refs_2_, ...), custom_call_target="tpu_custom_call" | custom-call | flops 1572864 | bytes 2883584 | tf_op jit(solution)/shard_map/combine_context/pallas_call | solution.py:319
  137.6 1.0 collective-permute-start.14
  138.6 4.9 %collective-permute-done.11.refs_3_ = bf16[8,64,512]{2,1,0:T(8,128)(2,1)} collective-permute-done((bf16[8,64,512]{2,1,0:T(8,128)(2,1)}, bf16[8,64,512]{2,1,0:T(8,128)(2,1)}, u32[]{:S(2)}, u32[]{:S(2)}) %collective-permute-start.11) | collective-permute-done | bytes 524320 | tf_op jit(solution)/shard_map/ppermute | solution.py:153
  143.5 2.7 %combine_grad_queries.1 = bf16[768,512]{1,0:T(8,128)(2,1)} custom-call(s32[24]{0:T(128)S(1)} %get-tuple-element.29.position, bf16[8,64,512]{2,1,0:T(8,128)(2,1)S(1)} %copy-done.16, bf16[8,64,512]{2,1,0:T(8,128)(2,1)} %collective-permute-done.9.refs_1_, bf16[8,64,512]{2,1,0:T(8,128)(2,1)} %collective-permute-done.10.refs_2_, ...), custom_call_target="tpu_custom_call" | custom-call | flops 32000000000 | bytes 2883584 | tf_op jit(solution)/shard_map/combine_grad_queries/pallas_call | solution.py:276
  146.3 6.7 %collective-permute-done.12 = bf16[224,1024]{1,0:T(8,128)(2,1)S(1)} collective-permute-done((bf16[224,1024]{1,0:T(8,128)(2,1)}, bf16[224,1024]{1,0:T(8,128)(2,1)S(1)}, u32[]{:S(2)}, u32[]{:S(2)}) %collective-permute-start.12) | collective-permute-done | bytes 458784 | tf_op jit(solution)/shard_map/ppermute | solution.py:153
  152.9 0.3 collective-permute-done.13
  153.3 5.7 %collective-permute-done.14 = bf16[224,1024]{1,0:T(8,128)(2,1)S(1)} collective-permute-done((bf16[224,1024]{1,0:T(8,128)(2,1)S(1)}, bf16[224,1024]{1,0:T(8,128)(2,1)S(1)}, u32[]{:S(2)}, u32[]{:S(2)}) %collective-permute-start.14) | collective-permute-done | bytes 458784 | tf_op jit(solution)/shard_map/ppermute | solution.py:153
  159.0 0.3 convert_add_fusion
  159.3 1.0 fusion
  160.3 2.2 %reduce-scatter.2.cloned.1.call-done = bf16[2,128,896]{2,1,0:T(8,128)(2,1)} async-done(((bf16[16,128,896]{2,1,0:T(8,128)(2,1)}), bf16[2,128,896]{2,1,0:T(8,128)(2,1)}) %reduce-scatter.2.cloned.1.call-update) | async-done | bytes 458768 | tf_op jit(solution)/shard_map/reduce_scatter | solution.py:738
  (43 shorter events, 0.1 us)
Async XLA Ops:
  7.2 54.9 %all-gather.2.cloned.1.call-start = ((), (), s32[]{:S(2)}) async-start(), calls=%async_computation.1 | async-start | bytes 4128768 | tf_op jit(solution)/shard_map/all_gather | solution.py:725
  7.2 9.4 %copy-start.1 = (bf16[768,512]{1,0:T(8,128)(2,1)S(1)}, bf16[768,512]{1,0:T(8,128)(2,1)}, u32[]{:S(2)}) copy-start(bf16[768,512]{1,0:T(8,128)(2,1)} %q_ref.1) | copy-start | bytes 2359300
  7.2 9.4 %copy-start.2 = (bf16[768,512]{1,0:T(8,128)(2,1)S(1)}, bf16[768,512]{1,0:T(8,128)(2,1)}, u32[]{:S(2)}) copy-start(bf16[768,512]{1,0:T(8,128)(2,1)} %g_ref.1) | copy-start | bytes 2359300
  7.2 9.4 %copy-start.13 = (s32[12,2]{0,1:T(2,128)S(1)}, s32[12,2]{0,1:T(2,128)}, u32[]{:S(2)}) copy-start(s32[12,2]{0,1:T(2,128)} %param.16) | copy-start | bytes 292
  7.2 9.4 %copy-start.14 = (s32[12,2]{0,1:T(2,128)S(1)}, s32[12,2]{0,1:T(2,128)}, u32[]{:S(2)}) copy-start(s32[12,2]{0,1:T(2,128)} %param.17) | copy-start | bytes 292
  16.6 145.9 %reduce-scatter.2.cloned.1.call-start = ((), (), s32[]{:S(2)}) async-start(), calls=%async_computation.2 | async-start | bytes 4128768 | tf_op jit(solution)/shard_map/reduce_scatter | solution.py:738
  16.7 1.0 copy-start
  22.0 8.8 %copy-start.15 = (bf16[1040,512]{1,0:T(8,128)(2,1)}, bf16[1040,512]{1,0:T(8,128)(2,1)S(1)}, u32[]{:S(2)}) copy-start(bf16[1040,512]{1,0:T(8,128)(2,1)S(1)} %get-tuple-element.31.refs_0_) | copy-start | bytes 3194884
  22.1 7.5 %copy-start.17 = (bf16[896,512]{1,0:T(8,128)(2,1)S(1)}, bf16[896,512]{1,0:T(8,128)(2,1)}, u32[]{:S(2)}) copy-start(bf16[896,512]{1,0:T(8,128)(2,1)} %vw_ref.1) | copy-start | bytes 2752516
  22.1 48.2 %collective-permute-start = (bf16[1040,512]{1,0:T(8,128)(2,1)}, bf16[1040,512]{1,0:T(8,128)(2,1)}, u32[]{:S(2)}, u32[]{:S(2)}) collective-permute-start(bf16[1040,512]{1,0:T(8,128)(2,1)} %get-tuple-element.32), channel_id=1, source_target_pairs={{0,8},{8,0},{16,24},{24,16},{1,9},{9,1},{17,25},{25,17},{2,10},{10... | collective-permute-start | bytes 3194888 | tf_op jit(solution)/shard_map/ppermute | solution.py:153
  25.6 48.1 %collective-permute-start.1 = (bf16[1040,512]{1,0:T(8,128)(2,1)}, bf16[1040,512]{1,0:T(8,128)(2,1)}, u32[]{:S(2)}, u32[]{:S(2)}) collective-permute-start(bf16[1040,512]{1,0:T(8,128)(2,1)} %get-tuple-element.33), channel_id=1, source_target_pairs={{0,16},{8,24},{16,0},{24,8},{1,17},{9,25},{17,1},{25,9},{2,18},{10... | collective-permute-start | bytes 3194888 | tf_op jit(solution)/shard_map/ppermute | solution.py:153
  26.9 46.8 %collective-permute-start.2 = (bf16[1040,512]{1,0:T(8,128)(2,1)}, bf16[1040,512]{1,0:T(8,128)(2,1)}, u32[]{:S(2)}, u32[]{:S(2)}) collective-permute-start(bf16[1040,512]{1,0:T(8,128)(2,1)} %get-tuple-element.34), channel_id=1, source_target_pairs={{0,24},{8,16},{16,8},{24,0},{1,25},{9,17},{17,9},{25,1},{2,26},{10... | collective-permute-start | bytes 3194888 | tf_op jit(solution)/shard_map/ppermute | solution.py:153
  85.7 6.1 %collective-permute-start.8 = (f32[32,2,256]{2,1,0:T(2,128)}, f32[32,2,256]{2,1,0:T(2,128)S(1)}, u32[]{:S(2)}, u32[]{:S(2)}) collective-permute-start(f32[32,2,256]{2,1,0:T(2,128)} %get-tuple-element.39.refs_4_), channel_id=1, source_target_pairs={{0,24},{8,16},{16,8},{24,0},{1,25},{9,17},{17,9},{25,1},{2,26},{10... | collective-permute-start | bytes 196616 | tf_op jit(solution)/shard_map/ppermute | solution.py:153
  86.9 5.8 %collective-permute-start.7 = (f32[32,2,256]{2,1,0:T(2,128)}, f32[32,2,256]{2,1,0:T(2,128)S(1)}, u32[]{:S(2)}, u32[]{:S(2)}) collective-permute-start(f32[32,2,256]{2,1,0:T(2,128)} %get-tuple-element.39.refs_4_), channel_id=1, source_target_pairs={{0,16},{8,24},{16,0},{24,8},{1,17},{9,25},{17,1},{25,9},{2,18},{10... | collective-permute-start | bytes 196616 | tf_op jit(solution)/shard_map/ppermute | solution.py:153
  88.3 5.2 %collective-permute-start.6 = (f32[32,2,256]{2,1,0:T(2,128)}, f32[32,2,256]{2,1,0:T(2,128)S(1)}, u32[]{:S(2)}, u32[]{:S(2)}) collective-permute-start(f32[32,2,256]{2,1,0:T(2,128)} %get-tuple-element.39.refs_4_), channel_id=1, source_target_pairs={{0,8},{8,0},{16,24},{24,16},{1,9},{9,1},{17,25},{25,17},{2,10},{10... | collective-permute-start | bytes 196616 | tf_op jit(solution)/shard_map/ppermute | solution.py:153
  89.3 29.8 %collective-permute-start.3 = (bf16[8,64,512]{2,1,0:T(8,128)(2,1)}, bf16[8,64,512]{2,1,0:T(8,128)(2,1)S(1)}, u32[]{:S(2)}, u32[]{:S(2)}) collective-permute-start(bf16[8,64,512]{2,1,0:T(8,128)(2,1)} %get-tuple-element.36), channel_id=1, source_target_pairs={{0,8},{8,0},{16,24},{24,16},{1,9},{9,1},{17,25},{25,17},{2,10},{10... | collective-permute-start | bytes 1572872 | tf_op jit(solution)/shard_map/ppermute | solution.py:153
  90.3 30.5 %collective-permute-start.4 = (bf16[8,64,512]{2,1,0:T(8,128)(2,1)}, bf16[8,64,512]{2,1,0:T(8,128)(2,1)S(1)}, u32[]{:S(2)}, u32[]{:S(2)}) collective-permute-start(bf16[8,64,512]{2,1,0:T(8,128)(2,1)} %get-tuple-element.37), channel_id=1, source_target_pairs={{0,16},{8,24},{16,0},{24,8},{1,17},{9,25},{17,1},{25,9},{2,18},{10... | collective-permute-start | bytes 1572872 | tf_op jit(solution)/shard_map/ppermute | solution.py:153
  91.8 1.7 %copy-start.7 = (f32[32,2,256]{2,1,0:T(2,128)}, f32[32,2,256]{2,1,0:T(2,128)S(1)}, u32[]{:S(2)}) copy-start(f32[32,2,256]{2,1,0:T(2,128)S(1)} %collective-permute-done.8.refs_7_) | copy-start | bytes 196612
  91.8 29.5 %collective-permute-start.5 = (bf16[8,64,512]{2,1,0:T(8,128)(2,1)}, bf16[8,64,512]{2,1,0:T(8,128)(2,1)S(1)}, u32[]{:S(2)}, u32[]{:S(2)}) collective-permute-start(bf16[8,64,512]{2,1,0:T(8,128)(2,1)} %get-tuple-element.38), channel_id=1, source_target_pairs={{0,24},{8,16},{16,8},{24,0},{1,25},{9,17},{17,9},{25,1},{2,26},{10... | collective-permute-start | bytes 1572872 | tf_op jit(solution)/shard_map/ppermute | solution.py:153
  92.8 0.8 copy-start.9
  93.5 0.6 copy-start.11
  116.7 21.0 %collective-permute-start.9 = (bf16[8,64,512]{2,1,0:T(8,128)(2,1)}, bf16[8,64,512]{2,1,0:T(8,128)(2,1)}, u32[]{:S(2)}, u32[]{:S(2)}) collective-permute-start(bf16[8,64,512]{2,1,0:T(8,128)(2,1)} %get-tuple-element.44), channel_id=1, source_target_pairs={{0,8},{8,0},{16,24},{24,16},{1,9},{9,1},{17,25},{25,17},{2,10},{10... | collective-permute-start | bytes 1572872 | tf_op jit(solution)/shard_map/ppermute | solution.py:153
  117.9 20.8 %collective-permute-start.10 = (bf16[8,64,512]{2,1,0:T(8,128)(2,1)}, bf16[8,64,512]{2,1,0:T(8,128)(2,1)}, u32[]{:S(2)}, u32[]{:S(2)}) collective-permute-start(bf16[8,64,512]{2,1,0:T(8,128)(2,1)} %get-tuple-element.45), channel_id=1, source_target_pairs={{0,16},{8,24},{16,0},{24,8},{1,17},{9,25},{17,1},{25,9},{2,18},{10... | collective-permute-start | bytes 1572872 | tf_op jit(solution)/shard_map/ppermute | solution.py:153
  119.1 24.5 %collective-permute-start.11 = (bf16[8,64,512]{2,1,0:T(8,128)(2,1)}, bf16[8,64,512]{2,1,0:T(8,128)(2,1)}, u32[]{:S(2)}, u32[]{:S(2)}) collective-permute-start(bf16[8,64,512]{2,1,0:T(8,128)(2,1)} %get-tuple-element.46), channel_id=1, source_target_pairs={{0,24},{8,16},{16,8},{24,0},{1,25},{9,17},{17,9},{25,1},{2,26},{10... | collective-permute-start | bytes 1572872 | tf_op jit(solution)/shard_map/ppermute | solution.py:153
  121.9 0.8 copy-start.4
  122.6 11.3 %copy-start.3 = (bf16[8,64,512]{2,1,0:T(8,128)(2,1)S(1)}, bf16[8,64,512]{2,1,0:T(8,128)(2,1)}, u32[]{:S(2)}) copy-start(bf16[8,64,512]{2,1,0:T(8,128)(2,1)} %get-tuple-element.35.refs_0_) | copy-start | bytes 1572868
  122.6 11.3 %copy-start.6 = (f32[32,2,256]{2,1,0:T(2,128)S(1)}, f32[32,2,256]{2,1,0:T(2,128)}, u32[]{:S(2)}) copy-start(f32[32,2,256]{2,1,0:T(2,128)} %get-tuple-element.39.refs_4_) | copy-start | bytes 196612
  122.6 11.3 %copy-start.8 = (f32[32,2,256]{2,1,0:T(2,128)S(1)}, f32[32,2,256]{2,1,0:T(2,128)}, u32[]{:S(2)}) copy-start(f32[32,2,256]{2,1,0:T(2,128)} %copy-done.7) | copy-start | bytes 196612
  122.7 11.3 %copy-start.10 = (f32[32,2,256]{2,1,0:T(2,128)S(1)}, f32[32,2,256]{2,1,0:T(2,128)}, u32[]{:S(2)}) copy-start(f32[32,2,256]{2,1,0:T(2,128)} %copy-done.9) | copy-start | bytes 196612
  122.7 11.3 %copy-start.12 = (f32[32,2,256]{2,1,0:T(2,128)S(1)}, f32[32,2,256]{2,1,0:T(2,128)}, u32[]{:S(2)}) copy-start(f32[32,2,256]{2,1,0:T(2,128)} %copy-done.11) | copy-start | bytes 196612
  131.5 21.4 %collective-permute-start.12 = (bf16[224,1024]{1,0:T(8,128)(2,1)}, bf16[224,1024]{1,0:T(8,128)(2,1)S(1)}, u32[]{:S(2)}, u32[]{:S(2)}) collective-permute-start(bf16[224,1024]{1,0:T(8,128)(2,1)} %get-tuple-element.50), channel_id=1, source_target_pairs={{0,8},{8,0},{16,24},{24,16},{1,9},{9,1},{17,25},{25,17},{2,10},{10... | collective-permute-start | bytes 1376264 | tf_op jit(solution)/shard_map/ppermute | solution.py:153
  132.8 20.5 %collective-permute-start.13 = (bf16[224,1024]{1,0:T(8,128)(2,1)}, bf16[224,1024]{1,0:T(8,128)(2,1)S(1)}, u32[]{:S(2)}, u32[]{:S(2)}) collective-permute-start(bf16[224,1024]{1,0:T(8,128)(2,1)} %get-tuple-element.51), channel_id=1, source_target_pairs={{0,16},{8,24},{16,0},{24,8},{1,17},{9,25},{17,1},{25,9},{2,18},{10... | collective-permute-start | bytes 1376264 | tf_op jit(solution)/shard_map/ppermute | solution.py:153
  134.0 1.1 copy-start.5
  135.1 2.6 %copy-start.19 = (bf16[224,1024]{1,0:T(8,128)(2,1)S(1)}, bf16[224,1024]{1,0:T(8,128)(2,1)}, u32[]{:S(2)}) copy-start(bf16[224,1024]{1,0:T(8,128)(2,1)} %get-tuple-element.52) | copy-start | bytes 1376260
  135.1 8.5 %copy-start.16 = (bf16[8,64,512]{2,1,0:T(8,128)(2,1)S(1)}, bf16[8,64,512]{2,1,0:T(8,128)(2,1)}, u32[]{:S(2)}) copy-start(bf16[8,64,512]{2,1,0:T(8,128)(2,1)} %get-tuple-element.43.refs_0_) | copy-start | bytes 1572868
  137.6 21.3 %collective-permute-start.14 = (bf16[224,1024]{1,0:T(8,128)(2,1)S(1)}, bf16[224,1024]{1,0:T(8,128)(2,1)S(1)}, u32[]{:S(2)}, u32[]{:S(2)}) collective-permute-start(bf16[224,1024]{1,0:T(8,128)(2,1)S(1)} %copy-done.19), channel_id=1, source_target_pairs={{0,24},{8,16},{16,8},{24,0},{1,25},{9,17},{17,9},{25,1},{2,26},{10... | collective-permute-start | bytes 1376264 | tf_op jit(solution)/shard_map/ppermute | solution.py:153
  143.5 15.5 %copy-start.18 = (bf16[224,1024]{1,0:T(8,128)(2,1)S(1)}, bf16[224,1024]{1,0:T(8,128)(2,1)}, u32[]{:S(2)}) copy-start(bf16[224,1024]{1,0:T(8,128)(2,1)} %get-tuple-element.49) | copy-start | bytes 1376260
Sparse Core Ops, SparseCore 0:
  16.7 45.2 all-gather.1
  116.8 45.6 reduce-scatter.1
